TPU v7x, 32 devices: a whole 2x2x4 slice. The times are simulated.
32 devices in a mesh: blk: 4 (over z), leaf: 4 (over y, x), samp: 2 (over core).
Axes of the slice: x: 2, y: 2, z: 4, core: 2. Of those that a mesh axis runs over, the one named last changes fastest.
Arguments:
- points: float32 [3, 4096], P(None, ('blk', 'leaf')), may hold values from 0 to 8, as said below
- neighbors: int32 [16, 8], P(('blk', 'leaf')), may hold values from -1 to 15, as said below
- omega: float32 [512, 4096], P(None, ('blk', 'leaf')), may hold values from -6 to 6
- observed: float32 [4096], P(('blk', 'leaf')), may hold values from -6 to 6
- prior_draws: float32 [64, 4096], P('samp', ('blk', 'leaf')), may hold values from -6 to 6
Outputs:
- weights: float32 [64, 4096], P('samp', ('blk', 'leaf'))
- residual: float32 [64, 4096], P('samp', ('blk', 'leaf'))
Inputs may be any that keep to these rules, and one draw needn't show every extreme that they name: Block g's points lie in the unit cell with integer corner (cx, cy, cz), where cx // 2 = g // 4 and 0 <= cy, cz < 3. `neighbors`: row g lists in ascending order every block h whose unit cell touches g's (cells at most one apart in every coordinate, the first taken periodic of period 2 * 4), which includes every block with a point within distance 1 of a point of g, followed by -1 in the unused slots; the relation is symmetric, and every listed block has a slab index h // 4 equal to or cyclically next to g // 4.
All inputs are finite; a program needn't handle non-finite values.
Results may differ from a plain program's by a relative error of at most 0.0003.
Values sent between devices are 32-bit elements; how exact they have to be, the bound alone decides.
No kernel may reach another device: no remote copies, remote signals or barrier semaphores. Data moves between devices by JAX's collectives and lax.ppermute only.
A program may use at most 64 MiB of HBM per device.

v0:
```python
import functools

import jax
import jax.numpy as jnp
from jax import lax
from jax.experimental import pallas as pl
from jax.experimental.pallas import tpu as pltpu
from jax.sharding import PartitionSpec as P

support_radius = 0.8
noise_variance = 1.0
sketch_shift = 1.0
HIGHEST = lax.Precision.HIGHEST
POINT_AXES = ("blk", "leaf")
TILE = 128
PIVOT, BASE, AHEAD, REFINES = 8, 128, False, 1


def mm(left, right):
    return jnp.dot(left, right, precision=HIGHEST, preferred_element_type=jnp.float32)


def rough_mm(left, right):
    return jnp.dot(left, right, preferred_element_type=jnp.float32)


def mm_t(left, right):
    return lax.dot_general(
        left, right, (((1,), (1,)), ((), ())), precision=HIGHEST, preferred_element_type=jnp.float32
    )


def tree_sum(terms):
    terms = list(terms)
    while len(terms) > 1:
        terms = [
            terms[i] + terms[i + 1] if i + 1 < len(terms) else terms[i] for i in range(0, len(terms), 2)
        ]
    return terms[0]


def reciprocal(value):
    guess = pl.reciprocal(value, approx=True)
    for _ in range(REFINES):
        guess = guess * (2.0 - value * guess)
    return guess


def small_inverse(entries, size):
    def at(table, a, b):
        return table[(min(a, b), max(a, b))]

    if size == 1:
        return {(0, 0): reciprocal(entries[(0, 0)])}
    if size == 2:
        det = entries[(0, 0)] * entries[(1, 1)] - entries[(0, 1)] * entries[(0, 1)]
        inv = reciprocal(det)
        return {(0, 0): entries[(1, 1)] * inv, (1, 1): entries[(0, 0)] * inv, (0, 1): -entries[(0, 1)] * inv}
    half = size // 2
    idx = range(half)
    upper = [(a, b) for a in idx for b in range(a, half)]
    first = small_inverse({(a, b): entries[(a, b)] for a, b in upper}, half)
    cross = [[entries[(a, half + b)] for b in idx] for a in idx]
    lift = [[tree_sum(at(first, a, c) * cross[c][b] for c in idx) for b in idx] for a in idx]
    schur = {
        (a, b): entries[(half + a, half + b)] - tree_sum(cross[c][a] * lift[c][b] for c in idx)
        for a, b in upper
    }
    last = small_inverse(schur, half)
    mixed = [[tree_sum(lift[a][c] * at(last, c, b) for c in idx) for b in idx] for a in idx]
    result = {}
    for a, b in upper:
        result[(half + a, half + b)] = last[(a, b)]
        result[(a, b)] = first[(a, b)] + tree_sum(mixed[a][c] * lift[b][c] for c in idx)
    for a in idx:
        for b in idx:
            result[(a, half + b)] = -mixed[a][b]
    return result


def pivot_inverse(matrix):
    size = matrix.shape[0]
    lane = lax.broadcasted_iota(jnp.int32, (8, size), 1)
    sub = lax.broadcasted_iota(jnp.int32, (8, size), 0)
    parts = [matrix[8 * i : 8 * i + 8, :] for i in range(size // 8)]
    idx = range(PIVOT)
    upper = [(a, b) for a in idx for b in range(a, PIVOT)]

    def row(r):
        return jnp.broadcast_to(parts[r // 8][r % 8 : r % 8 + 1, :], (8, size))

    def entry(values, c):
        return jnp.broadcast_to(values[:, c : c + 1], (8, size))

    entries = None
    for k in range(0, size, PIVOT):
        home, first = k // 8, k % 8
        rows = [row(k + a) for a in idx]
        if entries is None:
            entries = {(a, b): entry(rows[a], k + b) for a, b in upper}
        ahead = AHEAD and k + PIVOT < size
        if ahead:
            later = k + PIVOT
            side = [[entry(rows[a], later + b) for b in idx] for a in idx]
            later_rows = [row(later + a) for a in idx]
            later_entries = {(a, b): entry(later_rows[a], later + b) for a, b in upper}
        inverse = small_inverse(entries, PIVOT)
        full = [[inverse[(min(a, b), max(a, b))] for b in idx] for a in idx]
        entries = None
        if ahead:
            lift = [[tree_sum(full[a][c] * side[c][b] for c in idx) for b in idx] for a in idx]
            entries = {
                (a, b): later_entries[(a, b)] - tree_sum(side[c][a] * lift[c][b] for c in idx)
                for a, b in upper
            }
        here = (lane >= k) & (lane < k + PIVOT)
        rows = [jnp.where(here, jnp.where(lane == k + a, 1.0, 0.0), rows[a]) for a in idx]
        scaled = [tree_sum(full[a][b] * rows[b] for b in idx) for a in idx]
        updated = []
        for i, part in enumerate(parts):
            columns = [entry(part, k + a) for a in idx]
            base = jnp.where(here, 0.0, part)
            if i == home:
                inside = (sub >= first) & (sub < first + PIVOT)
                base = jnp.where(inside, 0.0, base)
                columns = [
                    jnp.where(inside, jnp.where(sub == first + a, -1.0, 0.0), column)
                    for a, column in enumerate(columns)
                ]
            updated.append(base - tree_sum(columns[a] * scaled[a] for a in idx))
        parts = updated
    return jnp.concatenate(parts, axis=0)


def block_inverse(matrix):
    size = matrix.shape[0]
    if size <= BASE:
        return pivot_inverse(matrix)
    half = size // 2
    corner, side = matrix[:half, :half], matrix[:half, half:]
    first = block_inverse(corner)
    lift = mm(first, side)
    last = block_inverse(matrix[half:, half:] - mm(side.T, lift))
    mixed = mm(lift, last)
    top = jnp.concatenate([first + mm(mixed, lift.T), -mixed], axis=1)
    return jnp.concatenate([top, jnp.concatenate([-mixed.T, last], axis=1)], axis=0)


def assemble(core_ref, own_ref, other_ref, system_ref):
    half = system_ref.shape[0] // 2
    count = half // TILE

    def put(row, column, block):
        system_ref[row : row + TILE, column : column + TILE] = block

    flag = jnp.zeros((TILE, TILE), jnp.int32) + core_ref[0] == 0

    def tile(at, share):
        own, other = own_ref[at : at + TILE, :], other_ref[at : at + TILE, :]
        return jnp.where(flag, own, other) if share == 0 else jnp.where(flag, other, own)

    for share, corner in ((0, 0), (1, half)):
        at = 0
        for i in range(count):
            for j in range(i, count):
                block = tile(at, share)
                at += TILE
                if i == j:
                    put(corner + i * TILE, corner + i * TILE, 0.5 * (block + block.T))
                else:
                    put(corner + i * TILE, corner + j * TILE, block)
                    put(corner + j * TILE, corner + i * TILE, block.T)
    share_columns = count // 2
    for share in (0, 1):
        at = count * (count + 1) // 2 * TILE
        for j in range(share * share_columns, (share + 1) * share_columns):
            for i in range(count):
                block = tile(at, share)
                at += TILE
                put(i * TILE, half + j * TILE, block)
                put(half + j * TILE, i * TILE, block.T)


def eliminate(inverse_ref, begin, end):
    size = inverse_ref.shape[0]
    count = size // TILE
    row_id = lax.broadcasted_iota(jnp.int32, (TILE, TILE), 0)
    column_id = lax.broadcasted_iota(jnp.int32, (TILE, TILE), 1)

    def span(index):
        return pl.ds(pl.multiple_of(index * TILE, TILE), TILE)

    def step(k, carry):
        own = span(k)
        block = block_inverse(inverse_ref[own, own])
        inverse_ref[own, own] = jnp.where(row_id == column_id, 1.0, 0.0)
        scaled = mm(block, inverse_ref[own, :])
        inverse_ref[own, :] = scaled
        for ahead in range(1, count):
            other = span(lax.rem(k + ahead, count))
            column = inverse_ref[other, own]
            inverse_ref[other, own] = jnp.zeros((TILE, TILE), jnp.float32)
            inverse_ref[other, :] = inverse_ref[other, :] - mm(column, scaled)
        return carry

    lax.fori_loop(begin, end, step, 0)


def inverse_kernel(core_ref, own_ref, other_ref, system_ref, inverse_ref, solved_ref):
    assemble(core_ref, own_ref, other_ref, system_ref)
    inverse_ref[...] = system_ref[...]
    count = system_ref.shape[0] // TILE
    eliminate(inverse_ref, 0, count)
    samples = solved_ref.shape[0]
    begin = own_ref.shape[0] - count * samples
    rhs = jnp.concatenate(
        [own_ref[begin + i * samples : begin + (i + 1) * samples, :] for i in range(count)], axis=1
    )
    guess = mm(rhs, inverse_ref[...])
    solved_ref[...] = guess + rough_mm(rhs - mm(guess, system_ref[...]), inverse_ref[...])


def image_kernel(
    core_ref, solved_ref, sketch_ref, own_ref, other_ref, rhs_ref, image_rhs_ref,
    sketches_ref, direction_ref, image_ref, moved_ref, dots_ref,
):
    half, width = own_ref.shape
    core = core_ref[0]
    sketches_ref[:, :width] = sketch_ref[...]
    sketches_ref[pl.ds(pl.multiple_of(core * half, half), half), width:] = own_ref[...]
    sketches_ref[pl.ds(pl.multiple_of((1 - core) * half, half), half), width:] = other_ref[...]
    taken = mm(solved_ref[...], sketches_ref[...])
    rhs = rhs_ref[...]
    direction = (rhs - taken[:, :width]) / noise_variance
    image = (image_rhs_ref[...] - taken[:, width:]) / noise_variance
    direction_ref[...] = direction
    image_ref[...] = image
    moved = mm_t(image, sketch_ref[...])
    samples = rhs.shape[0]
    for i in range(moved.shape[1] // TILE):
        moved_ref[i * samples : (i + 1) * samples, :] = moved[:, i * TILE : (i + 1) * TILE]
    ones = jnp.ones((8, width), jnp.float32)
    dots_ref[...] = jnp.zeros(dots_ref.shape, jnp.float32)
    dots_ref[0:1, :samples] = mm_t(ones, rhs * direction)[0:1, :]
    dots_ref[1:2, :samples] = mm_t(ones, direction * image)[0:1, :]


def prepare_kernel(
    core_ref, points_ref, neighbors_ref, omega_ref, observed_ref, prior_ref, block_ref, meta_ref,
    points_vmem, neighbors_vmem, observed_vmem, prior_vmem, sems,
):
    samples = prior_vmem.shape[0]
    half = block_ref.shape[0] - samples - 8
    begin = pl.multiple_of(core_ref[0] * half, half)
    copies = [
        pltpu.make_async_copy(source, target, sems.at[i])
        for i, (source, target) in enumerate(
            (
                (omega_ref.at[pl.ds(begin, half), :], block_ref.at[0:half, :]),
                (points_ref, points_vmem),
                (neighbors_ref, neighbors_vmem),
                (observed_ref, observed_vmem),
                (prior_ref, prior_vmem),
            )
        )
    ]
    for copy in copies:
        copy.start()
    meta_ref[...] = jnp.full(meta_ref.shape, -1.0, jnp.float32)
    for copy in copies:
        copy.wait()
    block_ref[half : half + samples, :] = observed_vmem[...] - prior_vmem[...]
    meta_ref[0:3, :] = points_vmem[...]
    meta_ref[3:4, : neighbors_vmem.shape[1]] = neighbors_vmem[...].astype(jnp.float32)
    block_ref[half + samples :, :] = meta_ref[...]


def prepare(core, points, neighbors, omega, observed, prior, half):
    width = omega.shape[1]
    samples = prior.shape[0]
    vmem = pl.BlockSpec(memory_space=pltpu.VMEM)
    hbm = pl.BlockSpec(memory_space=pl.ANY)
    shapes = [(half + samples + 8, width), (8, width)]
    return pl.pallas_call(
        prepare_kernel,
        out_shape=tuple(jax.ShapeDtypeStruct(shape, jnp.float32) for shape in shapes),
        in_specs=[pl.BlockSpec(memory_space=pltpu.SMEM)] + [hbm] * 5,
        out_specs=(vmem, vmem),
        scratch_shapes=[
            pltpu.VMEM(points.shape, jnp.float32),
            pltpu.VMEM(neighbors.shape, jnp.int32),
            pltpu.VMEM(observed.shape, jnp.float32),
            pltpu.VMEM(prior.shape, jnp.float32),
            pltpu.SemaphoreType.DMA((5,)),
        ],
        name="prepare",
        cost_estimate=pl.CostEstimate(flops=10**9, bytes_accessed=2**19, transcendentals=0),
    )(core, points, neighbors, omega, observed, prior)


def payload_kernel(core_ref, omega_ref, own_ref, other_ref, rhs_ref, sketch_ref, payload_ref):
    half, width = own_ref.shape
    split = half // 2
    core = core_ref[0]
    begin = pl.multiple_of(core * half, half)
    sketch_ref[pl.ds(begin, half), :] = own_ref[...]
    sketch_ref[pl.ds(pl.multiple_of((1 - core) * half, half), half), :] = other_ref[...]
    own, other = own_ref[...], other_ref[...]
    lifted = noise_variance * omega_ref[...] + own
    count = half // TILE
    at = 0
    for i in range(count):
        product = mm_t(lifted[i * TILE : (i + 1) * TILE], own[i * TILE :])
        for j in range(count - i):
            payload_ref[at : at + TILE, :] = product[:, j * TILE : (j + 1) * TILE]
            at += TILE
    on_first = jnp.zeros((half, width), jnp.int32) + core == 0
    left = jnp.where(on_first, lifted, other)
    right = jnp.where(on_first[:split], other[:split], lifted[split:])
    product = mm_t(left, right)
    for j in range(split // TILE):
        payload_ref[at : at + half, :] = product[:, j * TILE : (j + 1) * TILE]
        at += half
    product = mm_t(rhs_ref[...], sketch_ref[...])
    samples = rhs_ref.shape[0]
    for j in range(2 * count):
        payload_ref[at : at + samples, :] = product[:, j * TILE : (j + 1) * TILE]
        at += samples


def kernel_call(kernel, name, outputs, *operands, blocks=(), flops=10**8):
    vmem = pl.BlockSpec(memory_space=pltpu.VMEM)
    smem = pl.BlockSpec(memory_space=pltpu.SMEM)
    scratch = []
    if blocks:
        scratch = [pltpu.VMEM((len(blocks),) + blocks[0].shape, jnp.float32), pltpu.SemaphoreType.DMA((len(blocks),))]
    return pl.pallas_call(
        kernel,
        out_shape=tuple(jax.ShapeDtypeStruct(shape, jnp.float32) for shape in outputs),
        in_specs=[smem if o.ndim == 1 else vmem for o in operands] + [pl.BlockSpec(memory_space=pltpu.HBM)] * len(blocks),
        out_specs=(vmem,) * len(outputs),
        scratch_shapes=scratch,
        name=name,
        compiler_params=pltpu.CompilerParams(vmem_limit_bytes=32 * 2**20),
        cost_estimate=pl.CostEstimate(flops=flops, bytes_accessed=2**20, transcendentals=0),
    )(*operands, *blocks)


def shifted(values, axis, distance):
    size = lax.axis_size(axis)
    return lax.ppermute(values, axis, [(i, (i + distance) % size) for i in range(size)])


def swapped(values, axis, mask):
    size = lax.axis_size(axis)
    return lax.ppermute(values, axis, [(i, i ^ mask) for i in range(size)])


def slab(values):
    return [values] + [swapped(values, "leaf", m) for m in range(1, lax.axis_size("leaf"))]


def group_size():
    return lax.axis_size(POINT_AXES)


def exchange(values):
    return lax.all_to_all(values, POINT_AXES, 0, 0, tiled=True)


def share_sum(values):
    count = group_size()
    return exchange(values).reshape(count, values.shape[0] // count, values.shape[1]).sum(axis=0)


def spread(values):
    count = group_size()
    sent = jnp.broadcast_to(values[None], (count,) + values.shape).reshape(-1, values.shape[1])
    return exchange(sent).reshape((count,) + values.shape)


def to_tiles(values):
    return jnp.concatenate([values[:, c : c + TILE] for c in range(0, values.shape[1], TILE)], axis=0)


def from_tiles(tiles, rows):
    return jnp.concatenate([tiles[r : r + rows] for r in range(0, tiles.shape[0], rows)], axis=1)


def dot_rows(left, right):
    return jnp.sum(left * right, axis=1)


def local(points, neighbors, omega, observed, prior_draws):
    cycle = lax.axis_size("blk")
    leaves = lax.axis_size("leaf")
    cores = lax.axis_size("samp")
    own_slab, own_leaf, own_core = (lax.axis_index(a) for a in ("blk", "leaf", "samp"))
    sketch_size, width = omega.shape
    half = sketch_size // cores
    samples = prior_draws.shape[0]
    period = 2.0 * cycle

    core = own_core.astype(jnp.int32).reshape(1)
    block, meta = prepare(core, points, neighbors, omega, observed[None, :], prior_draws, half)

    def other_core(values):
        return swapped(values, "samp", 1)

    def sent(upward, downward):
        return shifted(upward, "blk", 1), shifted(downward, "blk", -1)

    blocks = slab(block)
    above, below = shifted(meta, "blk", -1), shifted(meta, "blk", 1)
    sources = jnp.concatenate([b[half + samples : half + samples + 3] for b in blocks], axis=1)
    targets = [above, meta, below]
    source_ids = own_slab * leaves + jnp.stack([own_leaf ^ m for m in range(leaves)])
    target_lists = jnp.stack([t[3, : neighbors.shape[1]] for t in targets])
    usable = (target_lists[None] == source_ids[:, None, None].astype(jnp.float32)).astype(jnp.float32).sum(axis=2)

    def kernel_columns(index):
        offset = sources[:, :, None] - targets[index][:3, None, :]
        along = offset[0]
        along = jnp.where(along >= 0.5 * period, along - period, along)
        along = jnp.where(along < -0.5 * period, along + period, along)
        squared = along * along + offset[1] * offset[1] + offset[2] * offset[2]
        radius = jnp.sqrt(squared) / support_radius
        remain = jnp.maximum(1.0 - radius, 0.0)
        squared_remain = remain * remain
        values = squared_remain * squared_remain * (4.0 * radius + 1.0)
        weight = jnp.repeat(usable[:, index], width)
        return values * weight[:, None]

    columns = [kernel_columns(i) for i in range(3)]

    def sums(values):
        gathered = jnp.concatenate(values, axis=1)
        return mm(gathered, columns[0]), mm(gathered, columns[2]), gathered

    upward, downward, gathered = sums([b[: half + samples] for b in blocks])
    from_below, from_above = sent(upward, downward)
    applied = mm(gathered, columns[1]) + from_below + from_above
    omega_half, rhs = block[:half], block[half : half + samples]
    sketch_half = applied[:half] + sketch_shift * omega_half
    image_rhs = applied[half:] + noise_variance * rhs

    count = half // TILE
    matrix_rows = (count * (count + 1) // 2 + count * count // 2) * TILE
    sketch, payload = kernel_call(
        payload_kernel,
        "payload",
        [(sketch_size, width), (matrix_rows + samples * (sketch_size // TILE), TILE)],
        core,
        omega_half,
        sketch_half,
        other_core(sketch_half),
        rhs,
        flops=10**9,
    )
    payload, late_sketch = lax.optimization_barrier((payload, sketch_half))
    upward, downward, gathered = sums(slab(late_sketch))
    here = mm(gathered, columns[1]) + noise_variance * late_sketch
    reduced = spread(share_sum(payload)).reshape(payload.shape)
    other_reduced = other_core(reduced)
    reduced, upward, downward, here = lax.optimization_barrier((reduced, upward, downward, here))
    from_below, from_above = sent(upward, downward)
    system, inverse, solved = kernel_call(
        inverse_kernel,
        "inverse_and_solve",
        [(sketch_size, sketch_size)] * 2 + [(samples, sketch_size)],
        core,
        reduced,
        other_reduced,
        flops=30 * 10**9,
    )
    from_below, from_above, solved = lax.optimization_barrier((from_below, from_above, solved))
    own_image = here + from_below + from_above

    sketches, direction, image, moved, dots = kernel_call(
        image_kernel,
        "image",
        [(sketch_size, 2 * width)] + [(samples, width)] * 2 + [(samples * (sketch_size // TILE), TILE), (8, TILE)],
        core,
        solved,
        sketch,
        own_image,
        other_core(own_image),
        rhs,
        image_rhs,
    )
    moved, late_image = lax.optimization_barrier((moved, image))
    upward, downward, gathered = sums(slab(late_image))
    from_below, from_above = sent(upward, downward)
    image_twice = mm(gathered, columns[1]) + from_below + from_above + noise_variance * late_image
    moved_share = share_sum(moved)
    inverse, moved_share = lax.optimization_barrier((inverse, moved_share))
    solves = mm(inverse, sketches)
    solves = solves + rough_mm(inverse, sketches - mm(system, solves))

    arrived = spread(jnp.concatenate([moved_share, dots], axis=0))
    rows = moved_share.shape[0]
    moved = from_tiles(arrived[:, :rows].reshape(-1, TILE), samples)
    dots = arrived[:, rows:].sum(axis=0)
    inner_first, curvature = dots[0, :samples, None], dots[1, :samples, None]
    step = inner_first / curvature

    taken = mm(moved, solves)
    precond = direction - step * ((image - taken[:, :width]) / noise_variance)
    image_precond = image - step * ((image_twice - taken[:, width:]) / noise_variance)
    residual = rhs - step * image
    dots = jnp.stack([dot_rows(residual, precond), dot_rows(precond, image_precond), dot_rows(precond, image)])
    dots = spread(jnp.pad(dots, ((0, 5), (0, TILE - samples)))).sum(axis=0)
    inner_second, curvature_precond, mixed = (dots[i, :samples, None] for i in range(3))
    beta = inner_second / inner_first
    step_second = inner_second / (curvature_precond + beta * (2.0 * mixed + beta * curvature))
    weights = step * direction + step_second * (precond + beta * direction)
    residual = residual - step_second * (image_precond + beta * image)
    return (weights, residual)


def solution(mesh):
    in_specs = (
        P(None, ("blk", "leaf")),
        P(("blk", "leaf"), None),
        P(None, ("blk", "leaf")),
        P(("blk", "leaf")),
        P("samp", ("blk", "leaf")),
    )
    out_specs = (P("samp", ("blk", "leaf")), P("samp", ("blk", "leaf")))
    return jax.shard_map(local, mesh=mesh, in_specs=in_specs, out_specs=out_specs, check_vma=False)
```

profile of v0, /device:TPU:0, one launch (start us, length us, event | category | flops | bytes accessed | tf_op | source)
XLA Modules:
  0.0 164.3 jit_solution(12814277769315353283)
XLA Ops:
  0.6 1.7 %prepare.1 = (f32[296,256]{1,0:T(8,128)}, f32[8,256]{1,0:T(8,128)}) custom-call(s32[1]{0:T(128)} %bitcast.core_ref, f32[3,256]{1,0:T(4,128)} %points_ref.1, s32[1,8]{1,0:T(1,128)} %neighbors_ref.1, f32[512,256]{1,0:T(8,128)} %omega_ref.1, f32[1,256]{1,0:T(1,128)} %bitcast.142, f32[32,256]{1,0:T(8,128)} %prior_ref.1), custom_call_target="tpu_custom_call" | custom-call | flops 1000000000 | bytes 524288 | tf_op jit(solution)/shard_map/prepare/pallas_call | solution.py:284
  2.4 5.1 %collective-permute-start.3 = (f32[8,256]{1,0:T(8,128)}, f32[8,256]{1,0:T(8,128)S(1)}, u32[]{:S(2)}, u32[]{:S(2)}) collective-permute-start(f32[8,256]{1,0:T(8,128)} %get-tuple-element.28), channel_id=1, source_target_pairs={{0,24},{8,0},{16,8},{24,16},{1,25},{9,1},{17,9},{25,17},{2,26},{10... | collective-permute-start | bytes 24584 | tf_op jit(solution)/shard_map/ppermute | solution.py:351
  7.5 1.5 collective-permute-start
  9.0 1.5 collective-permute-start.1
  14.5 3.3 %collective-permute-done = f32[296,256]{1,0:T(8,128)S(1)} collective-permute-done((f32[296,256]{1,0:T(8,128)}, f32[296,256]{1,0:T(8,128)S(1)}, u32[]{:S(2)}, u32[]{:S(2)}) %collective-permute-start) | collective-permute-done | bytes 303136 | tf_op jit(solution)/shard_map/ppermute | solution.py:356
  17.8 6.2 %collective-permute-done.1 = f32[296,256]{1,0:T(8,128)S(1)} collective-permute-done((f32[296,256]{1,0:T(8,128)}, f32[296,256]{1,0:T(8,128)S(1)}, u32[]{:S(2)}, u32[]{:S(2)}) %collective-permute-start.1) | collective-permute-done | bytes 303136 | tf_op jit(solution)/shard_map/ppermute | solution.py:356
  29.0 3.9 %collective-permute-start.6 = (f32[288,256]{1,0:T(8,128)S(1)}, f32[288,256]{1,0:T(8,128)S(1)}, u32[]{:S(2)}, u32[]{:S(2)}) collective-permute-start(f32[288,256]{1,0:T(8,128)S(1)} %fusion.24), channel_id=1, source_target_pairs={{0,24},{8,0},{16,8},{24,16},{1,25},{9,1},{17,9},{25,17},{2,26},{10... | collective-permute-start | bytes 884744 | tf_op jit(solution)/shard_map/ppermute | solution.py:351
  33.8 4.9 %collective-permute-done.5 = f32[288,256]{1,0:T(8,128)S(1)} collective-permute-done((f32[288,256]{1,0:T(8,128)S(1)}, f32[288,256]{1,0:T(8,128)S(1)}, u32[]{:S(2)}, u32[]{:S(2)}) %collective-permute-start.5) | collective-permute-done | bytes 294944 | tf_op jit(solution)/shard_map/ppermute | solution.py:351
  38.7 3.7 %collective-permute-done.6 = f32[288,256]{1,0:T(8,128)S(1)} collective-permute-done((f32[288,256]{1,0:T(8,128)S(1)}, f32[288,256]{1,0:T(8,128)S(1)}, u32[]{:S(2)}, u32[]{:S(2)}) %collective-permute-start.6) | collective-permute-done | bytes 294944 | tf_op jit(solution)/shard_map/ppermute | solution.py:351
  43.7 1.5 collective-permute-done.7.other_ref
  45.2 1.8 %payload.1 = (f32[512,256]{1,0:T(8,128)S(1)}, f32[768,128]{1,0:T(8,128)}) custom-call(s32[1]{0:T(128)} %bitcast.core_ref, f32[256,256]{1,0:T(8,128)S(1)} %get-tuple-element.61.omega_ref, f32[256,256]{1,0:T(8,128)S(1)} %get-tuple-element.31.own_ref, f32[256,256]{1,0:T(8,128)S(1)} %collective-permute-done.7.other_ref, f32[32,256]{1,0:T(8,128)S(1)} %get-tuple-element.59.rhs_ref), custom_call_target="tpu_custom_call" | custom-call | flops 1000000000 | bytes 1048576 | tf_op jit(solution)/shard_map/payload/pallas_call | solution.py:337
  47.9 3.7 %all-to-all-start = ((f32[16,48,128]{2,1,0:T(8,128)}), f32[16,48,128]{2,1,0:T(8,128)S(1)}, u32[]{:S(2)}, u32[]{:S(2)}) async-start(f32[16,48,128]{2,1,0:T(8,128)} %bitcast.18), calls=%async_computation | async-start | bytes 786432 | tf_op jit(solution)/shard_map/all_to_all | solution.py:368
  51.6 1.9 %collective-permute-start.8 = (f32[256,256]{1,0:T(8,128)S(1)}, f32[256,256]{1,0:T(8,128)S(1)}, u32[]{:S(2)}, u32[]{:S(2)}) collective-permute-start(f32[256,256]{1,0:T(8,128)S(1)} %get-tuple-element.31.own_ref), channel_id=1, source_target_pairs={{0,2},{2,0},{4,6},{6,4},{1,3},{3,1},{5,7},{7,5},{8,10},{10,8},{12,... | collective-permute-start | bytes 786440 | tf_op jit(solution)/shard_map/ppermute | solution.py:356
  55.1 9.5 %all-to-all-done = f32[16,48,128]{2,1,0:T(8,128)S(1)} async-done(((f32[16,48,128]{2,1,0:T(8,128)}), f32[16,48,128]{2,1,0:T(8,128)S(1)}, u32[]{:S(2)}, u32[]{:S(2)}) %all-to-all-start) | async-done | bytes 393248 | tf_op jit(solution)/shard_map/all_to_all | solution.py:368
  65.5 3.8 %all-to-all-start.1 = ((f32[16,48,128]{2,1,0:T(8,128)}), f32[16,48,128]{2,1,0:T(8,128)S(1)}, u32[]{:S(2)}, u32[]{:S(2)}) async-start(f32[16,48,128]{2,1,0:T(8,128)} %broadcast_in_dim.18), calls=%async_computation.1 | async-start | bytes 786432 | tf_op jit(solution)/shard_map/all_to_all | solution.py:368
  72.5 8.4 %all-to-all-done.1 = f32[16,48,128]{2,1,0:T(8,128)S(1)} async-done(((f32[16,48,128]{2,1,0:T(8,128)}), f32[16,48,128]{2,1,0:T(8,128)S(1)}, u32[]{:S(2)}, u32[]{:S(2)}) %all-to-all-start.1) | async-done | bytes 393248 | tf_op jit(solution)/shard_map/all_to_all | solution.py:368
  80.9 2.6 %fusion.45 = f32[256,256]{1,0:T(8,128)S(1)} fusion(f32[256,1024]{1,0:T(8,128)} %copy-done.8, f32[1024,256]{1,0:T(8,128)} %copy-done.4), kind=kOutput, calls=%fused_computation.113 | convolution fusion | flops 805306368 | bytes 2359296 | tf_op jit(solution)/shard_map/dot_general | solution.py:20
  85.8 2.7 %collective-permute-start.13 = (f32[256,256]{1,0:T(8,128)S(1)}, f32[256,256]{1,0:T(8,128)S(1)}, u32[]{:S(2)}, u32[]{:S(2)}) collective-permute-start(f32[256,256]{1,0:T(8,128)S(1)} %fusion.46), channel_id=1, source_target_pairs={{0,24},{8,0},{16,8},{24,16},{1,25},{9,1},{17,9},{25,17},{2,26},{10... | collective-permute-start | bytes 786440 | tf_op jit(solution)/shard_map/ppermute | solution.py:351
  88.5 29.2 %inverse_and_solve.1 = (f32[512,512]{1,0:T(8,128)S(1)}, f32[512,512]{1,0:T(8,128)S(1)}, f32[32,512]{1,0:T(8,128)S(1)}) custom-call(s32[1]{0:T(128)} %bitcast.core_ref, f32[768,128]{1,0:T(8,128)S(1)} %bitcast.135, f32[768,128]{1,0:T(8,128)S(1)} %collective-permute-done.11.other_ref), custom_call_target="tpu_custom_call" | custom-call | flops 30000001024 | bytes 1048576 | tf_op jit(solution)/shard_map/inverse_and_solve/pallas_call | solution.py:337
  117.8 1.5 collective-permute-done.14.other_ref
  119.4 1.9 %image.1 = (f32[512,512]{1,0:T(8,128)S(1)}, f32[32,256]{1,0:T(8,128)S(1)}, f32[32,256]{1,0:T(8,128)S(1)}, f32[128,128]{1,0:T(8,128)}, f32[8,128]{1,0:T(8,128)S(1)}) custom-call(s32[1]{0:T(128)} %bitcast.core_ref, f32[32,512]{1,0:T(8,128)S(1)} %get-tuple-element.37.solved_ref, f32[512,256]{1,0:T(8,128)S(1)} %copy-done.1, f32[256,256]{1,0:T(8,128)S(1)} %add_add_fusion.own_ref, ...), custom_call_target="tpu_custom_call" | custom-call | flops 100000000 | bytes 1048576 | tf_op jit(solution)/shard_map/image/pallas_call | solution.py:337
  122.7 2.1 %collective-permute-start.17 = (f32[32,256]{1,0:T(8,128)S(1)}, f32[32,256]{1,0:T(8,128)S(1)}, u32[]{:S(2)}, u32[]{:S(2)}) collective-permute-start(f32[32,256]{1,0:T(8,128)S(1)} %get-tuple-element.51), channel_id=1, source_target_pairs={{0,6},{2,4},{4,2},{6,0},{1,7},{3,5},{5,3},{7,1},{8,14},{10,12},{12... | collective-permute-start | bytes 98312 | tf_op jit(solution)/shard_map/ppermute | solution.py:356
  124.8 3.7 %all-to-all-start.2 = ((f32[16,8,128]{2,1,0:T(8,128)}), f32[16,8,128]{2,1,0:T(8,128)S(1)}, u32[]{:S(2)}, u32[]{:S(2)}) async-start(f32[16,8,128]{2,1,0:T(8,128)} %bitcast.20), calls=%async_computation.2 | async-start | bytes 131072 | tf_op jit(solution)/shard_map/all_to_all | solution.py:368
  128.6 2.5 %fusion.48 = f32[32,256]{1,0:T(8,128)} fusion(f32[32,1024]{1,0:T(8,128)S(1)} %constant_dynamic-update-slice_fusion.4, f32[1024,256]{1,0:T(8,128)} %copy-done.4), kind=kOutput, calls=%fused_computation.116 | convolution fusion | flops 100663296 | bytes 1212416 | tf_op jit(solution)/shard_map/dot_general | solution.py:20
  132.3 1.6 collective-permute-start.18
  133.9 2.2 %collective-permute-start.19 = (f32[32,256]{1,0:T(8,128)}, f32[32,256]{1,0:T(8,128)}, u32[]{:S(2)}, u32[]{:S(2)}) collective-permute-start(f32[32,256]{1,0:T(8,128)} %fusion.49), channel_id=1, source_target_pairs={{0,24},{8,0},{16,8},{24,16},{1,25},{9,1},{17,9},{25,17},{2,26},{10... | collective-permute-start | bytes 98312 | tf_op jit(solution)/shard_map/ppermute | solution.py:351
  136.8 4.9 %all-to-all-start.3 = ((f32[16,16,128]{2,1,0:T(8,128)}), f32[16,16,128]{2,1,0:T(8,128)S(1)}, u32[]{:S(2)}, u32[]{:S(2)}) async-start(f32[16,16,128]{2,1,0:T(8,128)} %broadcast_in_dim.19), calls=%async_computation.3 | async-start | bytes 262144 | tf_op jit(solution)/shard_map/all_to_all | solution.py:368
  141.6 1.9 %fusion.47 = f32[512,512]{1,0:T(8,128)S(1)} fusion(f32[512,512]{1,0:T(8,128)S(1)} %get-tuple-element.48, f32[512,512]{1,0:T(8,128)S(1)} %get-tuple-element.49), kind=kOutput, calls=%fused_computation.115 | convolution fusion | flops 1610612736 | bytes 3145728 | tf_op jit(solution)/shard_map/dot_general | solution.py:20
  143.5 1.9 %convolution_subtract_fusion = bf16[512,512]{1,0:T(8,128)(2,1)S(1)} fusion(f32[512,512]{1,0:T(8,128)S(1)} %get-tuple-element.49, f32[512,512]{1,0:T(8,128)S(1)} %get-tuple-element.50, f32[512,512]{1,0:T(8,128)S(1)} %fusion.47), kind=kOutput, calls=%fused_computation.10 | convolution fusion | flops 1611137024 | bytes 3670016 | tf_op jit(solution)/shard_map/dot_general | solution.py:20
  145.8 3.6 %all-to-all-done.3 = f32[16,16,128]{2,1,0:T(8,128)S(1)} async-done(((f32[16,16,128]{2,1,0:T(8,128)}), f32[16,16,128]{2,1,0:T(8,128)S(1)}, u32[]{:S(2)}, u32[]{:S(2)}) %all-to-all-start.3) | async-done | bytes 131104 | tf_op jit(solution)/shard_map/all_to_all | solution.py:368
  150.2 1.5 multiply_reduce_fusion.2
  151.8 11.0 %all_to_all.39 = f32[16,8,128]{2,1,0:T(8,128)S(1)} all-to-all(f32[16,8,128]{2,1,0:T(8,128)S(1)} %broadcast_in_dim.20), channel_id=1, replica_groups=mesh['blk'=4,'leaf'=4,'samp'=2] {'blk','leaf'}, dimensions={0} | all-to-all | bytes 131072 | tf_op jit(solution)/shard_map/all_to_all | solution.py:368
  (108 shorter events, 25.9 us)
Async XLA Ops:
  2.4 11.7 %collective-permute-start.3 = (f32[8,256]{1,0:T(8,128)}, f32[8,256]{1,0:T(8,128)S(1)}, u32[]{:S(2)}, u32[]{:S(2)}) collective-permute-start(f32[8,256]{1,0:T(8,128)} %get-tuple-element.28), channel_id=1, source_target_pairs={{0,24},{8,0},{16,8},{24,16},{1,25},{9,1},{17,9},{25,17},{2,26},{10... | collective-permute-start | bytes 24584 | tf_op jit(solution)/shard_map/ppermute | solution.py:351
  7.5 6.7 %collective-permute-start.4 = (f32[8,256]{1,0:T(8,128)}, f32[8,256]{1,0:T(8,128)S(1)}, u32[]{:S(2)}, u32[]{:S(2)}) collective-permute-start(f32[8,256]{1,0:T(8,128)} %get-tuple-element.28), channel_id=1, source_target_pairs={{0,8},{8,16},{16,24},{24,0},{1,9},{9,17},{17,25},{25,1},{2,10},{10... | collective-permute-start | bytes 24584 | tf_op jit(solution)/shard_map/ppermute | solution.py:351
  7.5 10.3 %collective-permute-start = (f32[296,256]{1,0:T(8,128)}, f32[296,256]{1,0:T(8,128)S(1)}, u32[]{:S(2)}, u32[]{:S(2)}) collective-permute-start(f32[296,256]{1,0:T(8,128)} %get-tuple-element.27), channel_id=1, source_target_pairs={{0,2},{2,0},{4,6},{6,4},{1,3},{3,1},{5,7},{7,5},{8,10},{10,8},{12,... | collective-permute-start | bytes 909320 | tf_op jit(solution)/shard_map/ppermute | solution.py:356
  9.0 15.1 %collective-permute-start.1 = (f32[296,256]{1,0:T(8,128)}, f32[296,256]{1,0:T(8,128)S(1)}, u32[]{:S(2)}, u32[]{:S(2)}) collective-permute-start(f32[296,256]{1,0:T(8,128)} %get-tuple-element.27), channel_id=1, source_target_pairs={{0,4},{2,6},{4,0},{6,2},{1,5},{3,7},{5,1},{7,3},{8,12},{10,14},{12... | collective-permute-start | bytes 909320 | tf_op jit(solution)/shard_map/ppermute | solution.py:356
  10.5 13.6 %collective-permute-start.2 = (f32[296,256]{1,0:T(8,128)}, f32[296,256]{1,0:T(8,128)S(1)}, u32[]{:S(2)}, u32[]{:S(2)}) collective-permute-start(f32[296,256]{1,0:T(8,128)} %get-tuple-element.27), channel_id=1, source_target_pairs={{0,6},{2,4},{4,2},{6,0},{1,7},{3,5},{5,3},{7,1},{8,14},{10,12},{12... | collective-permute-start | bytes 909320 | tf_op jit(solution)/shard_map/ppermute | solution.py:356
  25.7 1.2 copy-start.4
  26.9 11.8 %collective-permute-start.5 = (f32[288,256]{1,0:T(8,128)S(1)}, f32[288,256]{1,0:T(8,128)S(1)}, u32[]{:S(2)}, u32[]{:S(2)}) collective-permute-start(f32[288,256]{1,0:T(8,128)S(1)} %fusion.25), channel_id=1, source_target_pairs={{0,8},{8,16},{16,24},{24,0},{1,9},{9,17},{17,25},{25,1},{2,10},{10... | collective-permute-start | bytes 884744 | tf_op jit(solution)/shard_map/ppermute | solution.py:351
  29.0 13.4 %collective-permute-start.6 = (f32[288,256]{1,0:T(8,128)S(1)}, f32[288,256]{1,0:T(8,128)S(1)}, u32[]{:S(2)}, u32[]{:S(2)}) collective-permute-start(f32[288,256]{1,0:T(8,128)S(1)} %fusion.24), channel_id=1, source_target_pairs={{0,24},{8,0},{16,8},{24,16},{1,25},{9,1},{17,9},{25,17},{2,26},{10... | collective-permute-start | bytes 884744 | tf_op jit(solution)/shard_map/ppermute | solution.py:351
  33.8 49.7 %copy-start.2 = (f32[1024,256]{1,0:T(8,128)}, f32[1024,256]{1,0:T(8,128)S(1)}, u32[]{:S(2)}) copy-start(f32[1024,256]{1,0:T(8,128)S(1)} %multiply_multiply_fusion.2) | copy-start | bytes 3145732
  33.8 9.7 %copy-start.10 = (f32[296,256]{1,0:T(8,128)S(1)}, f32[296,256]{1,0:T(8,128)}, u32[]{:S(2)}) copy-start(f32[296,256]{1,0:T(8,128)} %get-tuple-element.27) | copy-start | bytes 909316
  43.6 1.6 collective-permute-start.7
  47.9 16.8 %all-to-all-start = ((f32[16,48,128]{2,1,0:T(8,128)}), f32[16,48,128]{2,1,0:T(8,128)S(1)}, u32[]{:S(2)}, u32[]{:S(2)}) async-start(f32[16,48,128]{2,1,0:T(8,128)} %bitcast.18), calls=%async_computation | async-start | bytes 786432 | tf_op jit(solution)/shard_map/all_to_all | solution.py:368
  51.6 17.7 %collective-permute-start.8 = (f32[256,256]{1,0:T(8,128)S(1)}, f32[256,256]{1,0:T(8,128)S(1)}, u32[]{:S(2)}, u32[]{:S(2)}) collective-permute-start(f32[256,256]{1,0:T(8,128)S(1)} %get-tuple-element.31.own_ref), channel_id=1, source_target_pairs={{0,2},{2,0},{4,6},{6,4},{1,3},{3,1},{5,7},{7,5},{8,10},{10,8},{12,... | collective-permute-start | bytes 786440 | tf_op jit(solution)/shard_map/ppermute | solution.py:356
  53.5 15.8 %collective-permute-start.9 = (f32[256,256]{1,0:T(8,128)S(1)}, f32[256,256]{1,0:T(8,128)S(1)}, u32[]{:S(2)}, u32[]{:S(2)}) collective-permute-start(f32[256,256]{1,0:T(8,128)S(1)} %get-tuple-element.31.own_ref), channel_id=1, source_target_pairs={{0,4},{2,6},{4,0},{6,2},{1,5},{3,7},{5,1},{7,3},{8,12},{10,14},{12... | collective-permute-start | bytes 786440 | tf_op jit(solution)/shard_map/ppermute | solution.py:356
  55.0 15.5 %collective-permute-start.10 = (f32[256,256]{1,0:T(8,128)S(1)}, f32[256,256]{1,0:T(8,128)S(1)}, u32[]{:S(2)}, u32[]{:S(2)}) collective-permute-start(f32[256,256]{1,0:T(8,128)S(1)} %get-tuple-element.31.own_ref), channel_id=1, source_target_pairs={{0,6},{2,4},{4,2},{6,0},{1,7},{3,5},{5,3},{7,1},{8,14},{10,12},{12... | collective-permute-start | bytes 786440 | tf_op jit(solution)/shard_map/ppermute | solution.py:356
  65.5 15.4 %all-to-all-start.1 = ((f32[16,48,128]{2,1,0:T(8,128)}), f32[16,48,128]{2,1,0:T(8,128)S(1)}, u32[]{:S(2)}, u32[]{:S(2)}) async-start(f32[16,48,128]{2,1,0:T(8,128)} %broadcast_in_dim.18), calls=%async_computation.1 | async-start | bytes 786432 | tf_op jit(solution)/shard_map/all_to_all | solution.py:368
  69.2 2.3 %copy-start.6 = (f32[1024,256]{1,0:T(8,128)S(1)}, f32[1024,256]{1,0:T(8,128)}, u32[]{:S(2)}) copy-start(f32[1024,256]{1,0:T(8,128)} %copy-done.5) | copy-start | bytes 3145732
  80.9 2.7 %copy-start.9 = (f32[256,1024]{1,0:T(8,128)S(1)}, f32[256,1024]{1,0:T(8,128)}, u32[]{:S(2)}) copy-start(f32[256,1024]{1,0:T(8,128)} %copy-done.8) | copy-start | bytes 3145732
  80.9 7.6 %collective-permute-start.11 = (f32[768,128]{1,0:T(8,128)S(1)}, f32[768,128]{1,0:T(8,128)S(1)}, u32[]{:S(2)}, u32[]{:S(2)}) collective-permute-start(f32[768,128]{1,0:T(8,128)S(1)} %bitcast.134), channel_id=1, source_target_pairs={{0,1},{1,0},{2,3},{3,2},{4,5},{5,4},{6,7},{7,6},{8,9},{9,8},{10,11... | collective-permute-start | bytes 1179656 | tf_op jit(solution)/shard_map/ppermute | solution.py:356
  84.6 33.1 %collective-permute-start.12 = (f32[256,256]{1,0:T(8,128)S(1)}, f32[256,256]{1,0:T(8,128)S(1)}, u32[]{:S(2)}, u32[]{:S(2)}) collective-permute-start(f32[256,256]{1,0:T(8,128)S(1)} %fusion.45), channel_id=1, source_target_pairs={{0,8},{8,16},{16,24},{24,0},{1,9},{9,17},{17,25},{25,1},{2,10},{10... | collective-permute-start | bytes 786440 | tf_op jit(solution)/shard_map/ppermute | solution.py:351
  85.8 31.9 %collective-permute-start.13 = (f32[256,256]{1,0:T(8,128)S(1)}, f32[256,256]{1,0:T(8,128)S(1)}, u32[]{:S(2)}, u32[]{:S(2)}) collective-permute-start(f32[256,256]{1,0:T(8,128)S(1)} %fusion.46), channel_id=1, source_target_pairs={{0,24},{8,0},{16,8},{24,16},{1,25},{9,1},{17,9},{25,17},{2,26},{10... | collective-permute-start | bytes 786440 | tf_op jit(solution)/shard_map/ppermute | solution.py:351
  117.7 1.7 %copy-start.1 = (f32[512,256]{1,0:T(8,128)S(1)}, f32[512,256]{1,0:T(8,128)}, u32[]{:S(2)}) copy-start(f32[512,256]{1,0:T(8,128)} %copy-done) | copy-start | bytes 1572868
  117.8 1.6 collective-permute-start.14
  121.3 7.2 %collective-permute-start.15 = (f32[32,256]{1,0:T(8,128)S(1)}, f32[32,256]{1,0:T(8,128)S(1)}, u32[]{:S(2)}, u32[]{:S(2)}) collective-permute-start(f32[32,256]{1,0:T(8,128)S(1)} %get-tuple-element.51), channel_id=1, source_target_pairs={{0,2},{2,0},{4,6},{6,4},{1,3},{3,1},{5,7},{7,5},{8,10},{10,8},{12,... | collective-permute-start | bytes 98312 | tf_op jit(solution)/shard_map/ppermute | solution.py:356
  121.8 6.7 %collective-permute-start.16 = (f32[32,256]{1,0:T(8,128)S(1)}, f32[32,256]{1,0:T(8,128)S(1)}, u32[]{:S(2)}, u32[]{:S(2)}) collective-permute-start(f32[32,256]{1,0:T(8,128)S(1)} %get-tuple-element.51), channel_id=1, source_target_pairs={{0,4},{2,6},{4,0},{6,2},{1,5},{3,7},{5,1},{7,3},{8,12},{10,14},{12... | collective-permute-start | bytes 98312 | tf_op jit(solution)/shard_map/ppermute | solution.py:356
  122.7 5.8 %collective-permute-start.17 = (f32[32,256]{1,0:T(8,128)S(1)}, f32[32,256]{1,0:T(8,128)S(1)}, u32[]{:S(2)}, u32[]{:S(2)}) collective-permute-start(f32[32,256]{1,0:T(8,128)S(1)} %get-tuple-element.51), channel_id=1, source_target_pairs={{0,6},{2,4},{4,2},{6,0},{1,7},{3,5},{5,3},{7,1},{8,14},{10,12},{12... | collective-permute-start | bytes 98312 | tf_op jit(solution)/shard_map/ppermute | solution.py:356
  124.8 11.3 %all-to-all-start.2 = ((f32[16,8,128]{2,1,0:T(8,128)}), f32[16,8,128]{2,1,0:T(8,128)S(1)}, u32[]{:S(2)}, u32[]{:S(2)}) async-start(f32[16,8,128]{2,1,0:T(8,128)} %bitcast.20), calls=%async_computation.2 | async-start | bytes 131072 | tf_op jit(solution)/shard_map/all_to_all | solution.py:368
  128.5 2.6 %copy-start.7 = (f32[1024,256]{1,0:T(8,128)S(1)}, f32[1024,256]{1,0:T(8,128)}, u32[]{:S(2)}) copy-start(f32[1024,256]{1,0:T(8,128)} %copy-done.5) | copy-start | bytes 3145732
  132.3 17.9 %collective-permute-start.18 = (f32[32,256]{1,0:T(8,128)}, f32[32,256]{1,0:T(8,128)}, u32[]{:S(2)}, u32[]{:S(2)}) collective-permute-start(f32[32,256]{1,0:T(8,128)} %fusion.48), channel_id=1, source_target_pairs={{0,8},{8,16},{16,24},{24,0},{1,9},{9,17},{17,25},{25,1},{2,10},{10... | collective-permute-start | bytes 98312 | tf_op jit(solution)/shard_map/ppermute | solution.py:351
  133.9 16.3 %collective-permute-start.19 = (f32[32,256]{1,0:T(8,128)}, f32[32,256]{1,0:T(8,128)}, u32[]{:S(2)}, u32[]{:S(2)}) collective-permute-start(f32[32,256]{1,0:T(8,128)} %fusion.49), channel_id=1, source_target_pairs={{0,24},{8,0},{16,8},{24,16},{1,25},{9,1},{17,9},{25,17},{2,26},{10... | collective-permute-start | bytes 98312 | tf_op jit(solution)/shard_map/ppermute | solution.py:351
  136.8 12.7 %all-to-all-start.3 = ((f32[16,16,128]{2,1,0:T(8,128)}), f32[16,16,128]{2,1,0:T(8,128)S(1)}, u32[]{:S(2)}, u32[]{:S(2)}) async-start(f32[16,16,128]{2,1,0:T(8,128)} %broadcast_in_dim.19), calls=%async_computation.3 | async-start | bytes 262144 | tf_op jit(solution)/shard_map/all_to_all | solution.py:368
  145.8 4.4 %copy-start.3 = (f32[1024,256]{1,0:T(8,128)S(1)}, f32[1024,256]{1,0:T(8,128)}, u32[]{:S(2)}) copy-start(f32[1024,256]{1,0:T(8,128)} %copy-done.2) | copy-start | bytes 3145732
  (3 other events, 2.9 us)
where the time goes:
time: 165 us; the launch traced here: 164 us
  waiting for transfers between devices  43.8 us (27%)
  starting transfers between devices  43.4 us (26%)
  Pallas kernels  34.6 us (21%)
  matrix products  18.1 us (11%)
  blocking collectives  11 us (7%)
  local copies, waits for them, and re-layouts  6.68 us (4%)
  other arithmetic  5.39 us (3%)
    pallas_call x3, Pallas kernels, kernel_call(): pl.pallas_call(kernel, out_shape=tuple((jax.ShapeDtypeStruct(shape, jnp.f...  32.9 us
    all_to_all x4, waiting for transfers between devices, exchange(): return lax.all_to_all(values, POINT_AXES, 0, 0, tiled=True)  21.5 us
    dot_general x12, matrix products, mm(): jnp.dot(left, right, precision=HIGHEST, preferred_element_type=jnp.float32)  17.7 us
    ppermute x8, starting transfers between devices, shifted(): lax.ppermute(values, axis, [(i, (i + distance) % size) for i in range(siz...  16.7 us
    all_to_all x4, starting transfers between devices, exchange(): return lax.all_to_all(values, POINT_AXES, 0, 0, tiled=True)  16 us
    ppermute x12, waiting for transfers between devices, swapped(): return lax.ppermute(values, axis, [(i, i ^ mask) for i in range(size)])  13.7 us
    all_to_all x1, blocking collectives, exchange(): return lax.all_to_all(values, POINT_AXES, 0, 0, tiled=True)  11 us
    ppermute x12, starting transfers between devices, swapped(): return lax.ppermute(values, axis, [(i, i ^ mask) for i in range(size)])  10.7 us
  transfers between devices with their start and end apart: 24, of which 10 were waited for; matrix products, arithmetic and copies ran while one was open for 13% of the time, Pallas kernels for 18%

commit v1 on v0

--- a/solution.py
+++ b/solution.py
@@ -206,8 +206,15 @@
     lax.fori_loop(begin, end, step, 0)
 
 
-def inverse_kernel(core_ref, own_ref, other_ref, system_ref, inverse_ref, solved_ref):
-    assemble(core_ref, own_ref, other_ref, system_ref)
+def inverse_kernel(place_ref, *refs):
+    shares, (system_ref, inverse_ref, solved_ref, own_ref, other_ref) = refs[:-5], refs[-5:]
+    leaves = len(shares) // 2
+    rows = shares[0].shape[0]
+    for m in range(leaves):
+        at = pl.ds(pl.multiple_of((place_ref[1] ^ m) * rows, rows), rows)
+        own_ref[at, :] = shares[m][...]
+        other_ref[at, :] = shares[leaves + m][...]
+    assemble(place_ref, own_ref, other_ref, system_ref)
     inverse_ref[...] = system_ref[...]
     count = system_ref.shape[0] // TILE
     eliminate(inverse_ref, 0, count)
@@ -222,7 +229,7 @@
 
 def image_kernel(
     core_ref, solved_ref, sketch_ref, own_ref, other_ref, rhs_ref, image_rhs_ref,
-    sketches_ref, direction_ref, image_ref, moved_ref, dots_ref,
+    sketches_ref, direction_ref, image_ref, sums_ref,
 ):
     half, width = own_ref.shape
     core = core_ref[0]
@@ -237,26 +244,29 @@
     image_ref[...] = image
     moved = mm_t(image, sketch_ref[...])
     samples = rhs.shape[0]
-    for i in range(moved.shape[1] // TILE):
-        moved_ref[i * samples : (i + 1) * samples, :] = moved[:, i * TILE : (i + 1) * TILE]
+    count = moved.shape[1] // TILE
+    for i in range(count):
+        sums_ref[i * samples : (i + 1) * samples, :] = moved[:, i * TILE : (i + 1) * TILE]
+    at = count * samples
     ones = jnp.ones((8, width), jnp.float32)
-    dots_ref[...] = jnp.zeros(dots_ref.shape, jnp.float32)
-    dots_ref[0:1, :samples] = mm_t(ones, rhs * direction)[0:1, :]
-    dots_ref[1:2, :samples] = mm_t(ones, direction * image)[0:1, :]
+    sums_ref[at:, :] = jnp.zeros((8, TILE), jnp.float32)
+    sums_ref[at : at + 1, :samples] = mm_t(ones, rhs * direction)[0:1, :]
+    sums_ref[at + 1 : at + 2, :samples] = mm_t(ones, direction * image)[0:1, :]
 
 
 def prepare_kernel(
-    core_ref, points_ref, neighbors_ref, omega_ref, observed_ref, prior_ref, block_ref, meta_ref,
+    core_ref, points_ref, neighbors_ref, omega_ref, observed_ref, prior_ref, first_ref, second_ref, meta_ref,
     points_vmem, neighbors_vmem, observed_vmem, prior_vmem, sems,
 ):
+    split = second_ref.shape[0]
     samples = prior_vmem.shape[0]
-    half = block_ref.shape[0] - samples - 8
-    begin = pl.multiple_of(core_ref[0] * half, half)
+    begin = pl.multiple_of(core_ref[0] * (2 * split), 2 * split)
     copies = [
         pltpu.make_async_copy(source, target, sems.at[i])
         for i, (source, target) in enumerate(
             (
-                (omega_ref.at[pl.ds(begin, half), :], block_ref.at[0:half, :]),
+                (omega_ref.at[pl.ds(begin, split), :], first_ref.at[0:split, :]),
+                (omega_ref.at[pl.ds(begin + split, split), :], second_ref),
                 (points_ref, points_vmem),
                 (neighbors_ref, neighbors_vmem),
                 (observed_ref, observed_vmem),
@@ -269,39 +279,40 @@
     meta_ref[...] = jnp.full(meta_ref.shape, -1.0, jnp.float32)
     for copy in copies:
         copy.wait()
-    block_ref[half : half + samples, :] = observed_vmem[...] - prior_vmem[...]
+    first_ref[split : split + samples, :] = observed_vmem[...] - prior_vmem[...]
     meta_ref[0:3, :] = points_vmem[...]
     meta_ref[3:4, : neighbors_vmem.shape[1]] = neighbors_vmem[...].astype(jnp.float32)
-    block_ref[half + samples :, :] = meta_ref[...]
-
-
-def prepare(core, points, neighbors, omega, observed, prior, half):
+    first_ref[split + samples :, :] = meta_ref[...]
+
+
+def prepare(core, points, neighbors, omega, observed, prior, split):
     width = omega.shape[1]
     samples = prior.shape[0]
     vmem = pl.BlockSpec(memory_space=pltpu.VMEM)
     hbm = pl.BlockSpec(memory_space=pl.ANY)
-    shapes = [(half + samples + 8, width), (8, width)]
+    shapes = [(split + samples + 8, width), (split, width), (8, width)]
     return pl.pallas_call(
         prepare_kernel,
         out_shape=tuple(jax.ShapeDtypeStruct(shape, jnp.float32) for shape in shapes),
         in_specs=[pl.BlockSpec(memory_space=pltpu.SMEM)] + [hbm] * 5,
-        out_specs=(vmem, vmem),
+        out_specs=(vmem,) * 3,
         scratch_shapes=[
             pltpu.VMEM(points.shape, jnp.float32),
             pltpu.VMEM(neighbors.shape, jnp.int32),
             pltpu.VMEM(observed.shape, jnp.float32),
             pltpu.VMEM(prior.shape, jnp.float32),
-            pltpu.SemaphoreType.DMA((5,)),
+            pltpu.SemaphoreType.DMA((6,)),
         ],
         name="prepare",
-        cost_estimate=pl.CostEstimate(flops=10**9, bytes_accessed=2**19, transcendentals=0),
+        cost_estimate=pl.CostEstimate(flops=10**6, bytes_accessed=2**19, transcendentals=0),
     )(core, points, neighbors, omega, observed, prior)
 
 
-def payload_kernel(core_ref, omega_ref, own_ref, other_ref, rhs_ref, sketch_ref, payload_ref):
+def payload_kernel(place_ref, omega_ref, own_ref, other_ref, rhs_ref, sketch_ref, *refs):
     half, width = own_ref.shape
     split = half // 2
-    core = core_ref[0]
+    core, leaf = place_ref[0], place_ref[1]
+    shares, payload_ref = refs[:-1], refs[-1]
     begin = pl.multiple_of(core * half, half)
     sketch_ref[pl.ds(begin, half), :] = own_ref[...]
     sketch_ref[pl.ds(pl.multiple_of((1 - core) * half, half), half), :] = other_ref[...]
@@ -326,24 +337,24 @@
     for j in range(2 * count):
         payload_ref[at : at + samples, :] = product[:, j * TILE : (j + 1) * TILE]
         at += samples
-
-
-def kernel_call(kernel, name, outputs, *operands, blocks=(), flops=10**8):
+    rows = shares[0].shape[0]
+    for m, share in enumerate(shares):
+        share[...] = payload_ref[pl.ds(pl.multiple_of((leaf ^ m) * rows, rows), rows), :]
+
+
+def kernel_call(kernel, name, outputs, *operands, scratch=(), flops=10**8):
     vmem = pl.BlockSpec(memory_space=pltpu.VMEM)
     smem = pl.BlockSpec(memory_space=pltpu.SMEM)
-    scratch = []
-    if blocks:
-        scratch = [pltpu.VMEM((len(blocks),) + blocks[0].shape, jnp.float32), pltpu.SemaphoreType.DMA((len(blocks),))]
     return pl.pallas_call(
         kernel,
         out_shape=tuple(jax.ShapeDtypeStruct(shape, jnp.float32) for shape in outputs),
-        in_specs=[smem if o.ndim == 1 else vmem for o in operands] + [pl.BlockSpec(memory_space=pltpu.HBM)] * len(blocks),
+        in_specs=[smem if o.ndim == 1 else vmem for o in operands],
         out_specs=(vmem,) * len(outputs),
-        scratch_shapes=scratch,
+        scratch_shapes=[pltpu.VMEM(shape, jnp.float32) for shape in scratch],
         name=name,
-        compiler_params=pltpu.CompilerParams(vmem_limit_bytes=32 * 2**20),
+        compiler_params=pltpu.CompilerParams(vmem_limit_bytes=12 * 2**20),
         cost_estimate=pl.CostEstimate(flops=flops, bytes_accessed=2**20, transcendentals=0),
-    )(*operands, *blocks)
+    )(*operands)
 
 
 def shifted(values, axis, distance):
@@ -368,9 +379,11 @@
     return lax.all_to_all(values, POINT_AXES, 0, 0, tiled=True)
 
 
-def share_sum(values):
-    count = group_size()
-    return exchange(values).reshape(count, values.shape[0] // count, values.shape[1]).sum(axis=0)
+def axis_sum(values, axis):
+    if lax.axis_size(axis) != 4:
+        return lax.psum(values, axis)
+    one, two, three = (swapped(values, axis, m) for m in (1, 2, 3))
+    return (values + one) + (two + three)
 
 
 def spread(values):
@@ -402,7 +415,11 @@
     period = 2.0 * cycle
 
     core = own_core.astype(jnp.int32).reshape(1)
-    block, meta = prepare(core, points, neighbors, omega, observed[None, :], prior_draws, half)
+    place = jnp.stack([own_core, own_leaf]).astype(jnp.int32)
+    split = half // 2
+    first_block, second_block, meta = prepare(
+        core, points, neighbors, omega, observed[None, :], prior_draws, split
+    )
 
     def other_core(values):
         return swapped(values, "samp", 1)
@@ -410,9 +427,10 @@
     def sent(upward, downward):
         return shifted(upward, "blk", 1), shifted(downward, "blk", -1)
 
-    blocks = slab(block)
+    first_blocks, second_blocks = slab(first_block), slab(second_block)
     above, below = shifted(meta, "blk", -1), shifted(meta, "blk", 1)
-    sources = jnp.concatenate([b[half + samples : half + samples + 3] for b in blocks], axis=1)
+    begin = split + samples
+    sources = jnp.concatenate([b[begin : begin + 3] for b in first_blocks], axis=1)
     targets = [above, meta, below]
     source_ids = own_slab * leaves + jnp.stack([own_leaf ^ m for m in range(leaves)])
     target_lists = jnp.stack([t[3, : neighbors.shape[1]] for t in targets])
@@ -437,49 +455,61 @@
         gathered = jnp.concatenate(values, axis=1)
         return mm(gathered, columns[0]), mm(gathered, columns[2]), gathered
 
-    upward, downward, gathered = sums([b[: half + samples] for b in blocks])
+    upward, downward, gathered = sums([b[:begin] for b in first_blocks])
+    _, _, *second_blocks = lax.optimization_barrier((upward, downward, *second_blocks))
     from_below, from_above = sent(upward, downward)
     applied = mm(gathered, columns[1]) + from_below + from_above
-    omega_half, rhs = block[:half], block[half : half + samples]
-    sketch_half = applied[:half] + sketch_shift * omega_half
-    image_rhs = applied[half:] + noise_variance * rhs
+    upward, downward, gathered = sums(second_blocks)
+    from_below, from_above = sent(upward, downward)
+    applied_second = mm(gathered, columns[1]) + from_below + from_above
+    rhs = first_block[split:begin]
+    omega_half = jnp.concatenate([first_block[:split], second_block], axis=0)
+    sketch_half = jnp.concatenate([applied[:split], applied_second], axis=0) + sketch_shift * omega_half
+    image_rhs = applied[split:] + noise_variance * rhs
 
     count = half // TILE
     matrix_rows = (count * (count + 1) // 2 + count * count // 2) * TILE
-    sketch, payload = kernel_call(
+    payload_rows = matrix_rows + samples * (sketch_size // TILE)
+    sketch, *shares = kernel_call(
         payload_kernel,
         "payload",
-        [(sketch_size, width), (matrix_rows + samples * (sketch_size // TILE), TILE)],
-        core,
+        [(sketch_size, width)] + [(payload_rows // leaves, TILE)] * leaves,
+        place,
         omega_half,
         sketch_half,
         other_core(sketch_half),
         rhs,
+        scratch=[(payload_rows, TILE)],
         flops=10**9,
     )
-    payload, late_sketch = lax.optimization_barrier((payload, sketch_half))
+
+    share = shares[0]
+    for m in range(1, leaves):
+        share = share + swapped(shares[m], "leaf", m)
+    share, late_sketch = lax.optimization_barrier((share, sketch_half))
     upward, downward, gathered = sums(slab(late_sketch))
     here = mm(gathered, columns[1]) + noise_variance * late_sketch
-    reduced = spread(share_sum(payload)).reshape(payload.shape)
-    other_reduced = other_core(reduced)
-    reduced, upward, downward, here = lax.optimization_barrier((reduced, upward, downward, here))
+    shares = slab(axis_sum(share, "blk"))
+    *shares, upward, downward, here = lax.optimization_barrier((*shares, upward, downward, here))
+    other_shares = [other_core(s) for s in shares]
     from_below, from_above = sent(upward, downward)
     system, inverse, solved = kernel_call(
         inverse_kernel,
         "inverse_and_solve",
         [(sketch_size, sketch_size)] * 2 + [(samples, sketch_size)],
-        core,
-        reduced,
-        other_reduced,
+        place,
+        *shares,
+        *other_shares,
+        scratch=[(payload_rows, TILE)] * 2,
         flops=30 * 10**9,
     )
     from_below, from_above, solved = lax.optimization_barrier((from_below, from_above, solved))
     own_image = here + from_below + from_above
 
-    sketches, direction, image, moved, dots = kernel_call(
+    sketches, direction, image, partial = kernel_call(
         image_kernel,
         "image",
-        [(sketch_size, 2 * width)] + [(samples, width)] * 2 + [(samples * (sketch_size // TILE), TILE), (8, TILE)],
+        [(sketch_size, 2 * width)] + [(samples, width)] * 2 + [(samples * (sketch_size // TILE) + 8, TILE)],
         core,
         solved,
         sketch,
@@ -488,19 +518,17 @@
         rhs,
         image_rhs,
     )
-    moved, late_image = lax.optimization_barrier((moved, image))
+    partial, late_image = lax.optimization_barrier((partial, image))
     upward, downward, gathered = sums(slab(late_image))
     from_below, from_above = sent(upward, downward)
     image_twice = mm(gathered, columns[1]) + from_below + from_above + noise_variance * late_image
-    moved_share = share_sum(moved)
-    inverse, moved_share = lax.optimization_barrier((inverse, moved_share))
+    slab_sum = axis_sum(partial, "leaf")
+    inverse, _ = lax.optimization_barrier((inverse, slab_sum))
     solves = mm(inverse, sketches)
     solves = solves + rough_mm(inverse, sketches - mm(system, solves))
-
-    arrived = spread(jnp.concatenate([moved_share, dots], axis=0))
-    rows = moved_share.shape[0]
-    moved = from_tiles(arrived[:, :rows].reshape(-1, TILE), samples)
-    dots = arrived[:, rows:].sum(axis=0)
+    total = axis_sum(slab_sum, "blk")
+    moved = from_tiles(total[:-8], samples)
+    dots = total[-8:]
     inner_first, curvature = dots[0, :samples, None], dots[1, :samples, None]
     step = inner_first / curvature
 

time: 165 us -> 148 us (0.90)
  waiting for transfers between devices: 43.8 us -> 21.8 us
  starting transfers between devices: 43.4 us -> 55.3 us
  matrix products: 18.1 us -> 14 us
  local copies, waits for them, and re-layouts: 6.68 us -> 4.32 us
    ppermute x12 -> x33, starting transfers between devices: 10.7 us -> 34.7 us  [swapped(): return lax.ppermute(values, axis, [(i, i ^ mask) for i in range(size)])]
    all_to_all x4 -> x0, waiting for transfers between devices: 21.5 us -> none  [exchange(): return lax.all_to_all(values, POINT_AXES, 0, 0, tiled=True)]
    all_to_all x4 -> x0, starting transfers between devices: 16 us -> none  [exchange(): return lax.all_to_all(values, POINT_AXES, 0, 0, tiled=True)]
    ppermute x8 -> x10, waiting for transfers between devices: 8.59 us -> 4.4 us  [shifted(): lax.ppermute(values, axis, [(i, (i + distance) % size) for i in range(siz...]
    dot_general x12 -> x15, matrix products: 17.7 us -> 13.6 us  [mm(): jnp.dot(left, right, precision=HIGHEST, preferred_element_type=jnp.float32)]
    ppermute x8 -> x10, starting transfers between devices: 16.7 us -> 20.5 us  [shifted(): lax.ppermute(values, axis, [(i, (i + distance) % size) for i in range(siz...]
    ppermute x12 -> x33, waiting for transfers between devices: 13.7 us -> 17.4 us  [swapped(): return lax.ppermute(values, axis, [(i, i ^ mask) for i in range(size)])]
    unnamed x33 -> x18, local copies, waits for them, and re-layouts: 2.06 us -> 0.27 us
  transfers between devices with their start and end apart: 24 -> 43, of which waited for: 10 -> 11; matrix products, arithmetic and copies ran while one was open for 13% -> 14% of each run, Pallas kernels for 18% -> 20%
where the time goes in v1:
time: 148 us; the launch traced here: 147 us
  starting transfers between devices  55.3 us (37%)
  Pallas kernels  34.6 us (23%)
  waiting for transfers between devices  21.8 us (15%)
  matrix products  14 us (9%)
  blocking collectives  11.3 us (8%)
  other arithmetic  4.73 us (3%)
  local copies, waits for them, and re-layouts  4.32 us (3%)
    ppermute x33, starting transfers between devices, swapped(): return lax.ppermute(values, axis, [(i, i ^ mask) for i in range(size)])  34.7 us
    pallas_call x3, Pallas kernels, kernel_call(): pl.pallas_call(kernel, out_shape=tuple((jax.ShapeDtypeStruct(shape, jnp.f...  32.8 us
    ppermute x10, starting transfers between devices, shifted(): lax.ppermute(values, axis, [(i, (i + distance) % size) for i in range(siz...  20.5 us
    ppermute x33, waiting for transfers between devices, swapped(): return lax.ppermute(values, axis, [(i, i ^ mask) for i in range(size)])  17.4 us
    dot_general x15, matrix products, mm(): jnp.dot(left, right, precision=HIGHEST, preferred_element_type=jnp.float32)  13.6 us
    all_to_all x1, blocking collectives, exchange(): return lax.all_to_all(values, POINT_AXES, 0, 0, tiled=True)  11.3 us
    ppermute x10, waiting for transfers between devices, shifted(): lax.ppermute(values, axis, [(i, (i + distance) % size) for i in range(siz...  4.4 us
  transfers between devices with their start and end apart: 43, of which 11 were waited for; matrix products, arithmetic and copies ran while one was open for 14% of the time, Pallas kernels for 20%

profile of v1, /device:TPU:0, one launch (start us, length us, event | category | flops | bytes accessed | tf_op | source)
XLA Modules:
  0.0 147.3 jit_solution(16672899834549006887)
XLA Ops:
  0.6 1.7 %prepare.1 = (f32[168,256]{1,0:T(8,128)}, f32[128,256]{1,0:T(8,128)}, f32[8,256]{1,0:T(8,128)}) custom-call(s32[1]{0:T(128)} %bitcast.core_ref, f32[3,256]{1,0:T(4,128)} %points_ref.1, s32[1,8]{1,0:T(1,128)} %neighbors_ref.1, f32[512,256]{1,0:T(8,128)} %omega_ref.1, f32[1,256]{1,0:T(1,128)} %bitcast.139, f32[32,256]{1,0:T(8,128)} %prior_ref.1), custom_call_target="tpu_custom_call" | custom-call | flops 1000000 | bytes 524288 | tf_op jit(solution)/shard_map/prepare/pallas_call | solution.py:294
  2.4 5.1 %collective-permute-start.3 = (f32[8,256]{1,0:T(8,128)}, f32[8,256]{1,0:T(8,128)S(1)}, u32[]{:S(2)}, u32[]{:S(2)}) collective-permute-start(f32[8,256]{1,0:T(8,128)} %get-tuple-element.38), channel_id=1, source_target_pairs={{0,24},{8,0},{16,8},{24,16},{1,25},{9,1},{17,9},{25,17},{2,26},{10... | collective-permute-start | bytes 24584 | tf_op jit(solution)/shard_map/ppermute | solution.py:362
  7.5 1.5 %collective-permute-start = (f32[168,256]{1,0:T(8,128)}, f32[168,256]{1,0:T(8,128)S(1)}, u32[]{:S(2)}, u32[]{:S(2)}) collective-permute-start(f32[168,256]{1,0:T(8,128)} %get-tuple-element.36), channel_id=1, source_target_pairs={{0,2},{2,0},{4,6},{6,4},{1,3},{3,1},{5,7},{7,5},{8,10},{10,8},{12,... | collective-permute-start | bytes 516104 | tf_op jit(solution)/shard_map/ppermute | solution.py:367
  9.0 1.5 %collective-permute-start.1 = (f32[168,256]{1,0:T(8,128)}, f32[168,256]{1,0:T(8,128)S(1)}, u32[]{:S(2)}, u32[]{:S(2)}) collective-permute-start(f32[168,256]{1,0:T(8,128)} %get-tuple-element.36), channel_id=1, source_target_pairs={{0,4},{2,6},{4,0},{6,2},{1,5},{3,7},{5,1},{7,3},{8,12},{10,14},{12... | collective-permute-start | bytes 516104 | tf_op jit(solution)/shard_map/ppermute | solution.py:367
  15.0 1.6 %collective-permute-start.7 = (f32[128,256]{1,0:T(8,128)}, f32[128,256]{1,0:T(8,128)S(1)}, u32[]{:S(2)}, u32[]{:S(2)}) collective-permute-start(f32[128,256]{1,0:T(8,128)} %get-tuple-element.39), channel_id=1, source_target_pairs={{0,2},{2,0},{4,6},{6,4},{1,3},{3,1},{5,7},{7,5},{8,10},{10,8},{12,... | collective-permute-start | bytes 393224 | tf_op jit(solution)/shard_map/ppermute | solution.py:367
  16.6 1.5 %collective-permute-start.8 = (f32[128,256]{1,0:T(8,128)}, f32[128,256]{1,0:T(8,128)S(1)}, u32[]{:S(2)}, u32[]{:S(2)}) collective-permute-start(f32[128,256]{1,0:T(8,128)} %get-tuple-element.39), channel_id=1, source_target_pairs={{0,4},{2,6},{4,0},{6,2},{1,5},{3,7},{5,1},{7,3},{8,12},{10,14},{12... | collective-permute-start | bytes 393224 | tf_op jit(solution)/shard_map/ppermute | solution.py:367
  21.5 3.9 %collective-permute-start.6 = (f32[160,256]{1,0:T(8,128)S(1)}, f32[160,256]{1,0:T(8,128)S(1)}, u32[]{:S(2)}, u32[]{:S(2)}) collective-permute-start(f32[160,256]{1,0:T(8,128)S(1)} %fusion.25), channel_id=1, source_target_pairs={{0,24},{8,0},{16,8},{24,16},{1,25},{9,1},{17,9},{25,17},{2,26},{10... | collective-permute-start | bytes 491528 | tf_op jit(solution)/shard_map/ppermute | solution.py:362
  28.6 4.0 %collective-permute-start.11 = (f32[128,256]{1,0:T(8,128)S(1)}, f32[128,256]{1,0:T(8,128)S(1)}, u32[]{:S(2)}, u32[]{:S(2)}) collective-permute-start(f32[128,256]{1,0:T(8,128)S(1)} %fusion.49), channel_id=1, source_target_pairs={{0,24},{8,0},{16,8},{24,16},{1,25},{9,1},{17,9},{25,17},{2,26},{10... | collective-permute-start | bytes 393224 | tf_op jit(solution)/shard_map/ppermute | solution.py:362
  33.5 3.2 %collective-permute-done.10 = f32[128,256]{1,0:T(8,128)S(1)} collective-permute-done((f32[128,256]{1,0:T(8,128)S(1)}, f32[128,256]{1,0:T(8,128)S(1)}, u32[]{:S(2)}, u32[]{:S(2)}) %collective-permute-start.10) | collective-permute-done | bytes 131104 | tf_op jit(solution)/shard_map/ppermute | solution.py:362
  39.6 1.4 collective-permute-done.12.other_ref
  41.0 1.7 %payload.1 = (f32[512,256]{1,0:T(8,128)S(1)}, f32[192,128]{1,0:T(8,128)S(1)}, f32[192,128]{1,0:T(8,128)S(1)}, f32[192,128]{1,0:T(8,128)S(1)}, f32[192,128]{1,0:T(8,128)S(1)}) custom-call(s32[2]{0:T(128)S(1)} %pad_add_fusion.place_ref, f32[256,256]{1,0:T(8,128)S(1)} %get-tuple-element.77.omega_ref, f32[256,256]{1,0:T(8,128)S(1)} %get-tuple-element.48.own_ref, ...), custom_call_target="tpu_custom_call" | custom-call | flops 1000000000 | bytes 1048576 | tf_op jit(solution)/shard_map/payload/pallas_call | solution.py:348
  42.7 1.5 %collective-permute-start.13 = (f32[192,128]{1,0:T(8,128)S(1)}, f32[192,128]{1,0:T(8,128)S(1)}, u32[]{:S(2)}, u32[]{:S(2)}) collective-permute-start(f32[192,128]{1,0:T(8,128)S(1)} %get-tuple-element.44), channel_id=1, source_target_pairs={{0,2},{2,0},{4,6},{6,4},{1,3},{3,1},{5,7},{7,5},{8,10},{10,8},{12,... | collective-permute-start | bytes 294920 | tf_op jit(solution)/shard_map/ppermute | solution.py:367
  44.2 1.5 %collective-permute-start.14 = (f32[192,128]{1,0:T(8,128)S(1)}, f32[192,128]{1,0:T(8,128)S(1)}, u32[]{:S(2)}, u32[]{:S(2)}) collective-permute-start(f32[192,128]{1,0:T(8,128)S(1)} %get-tuple-element.45), channel_id=1, source_target_pairs={{0,4},{2,6},{4,0},{6,2},{1,5},{3,7},{5,1},{7,3},{8,12},{10,14},{12... | collective-permute-start | bytes 294920 | tf_op jit(solution)/shard_map/ppermute | solution.py:367
  46.2 1.3 collective-permute-done.13
  47.6 2.4 %collective-permute-done.14 = f32[192,128]{1,0:T(8,128)S(1)} collective-permute-done((f32[192,128]{1,0:T(8,128)S(1)}, f32[192,128]{1,0:T(8,128)S(1)}, u32[]{:S(2)}, u32[]{:S(2)}) %collective-permute-start.14) | collective-permute-done | bytes 98336 | tf_op jit(solution)/shard_map/ppermute | solution.py:367
  52.0 2.1 %collective-permute-start.17 = (f32[192,128]{1,0:T(8,128)S(1)}, f32[192,128]{1,0:T(8,128)S(1)}, u32[]{:S(2)}, u32[]{:S(2)}) collective-permute-start(f32[192,128]{1,0:T(8,128)S(1)} %add_add_fusion.2), channel_id=1, source_target_pairs={{0,16},{8,24},{16,0},{24,8},{1,17},{9,25},{17,1},{25,9},{2,18},{10... | collective-permute-start | bytes 294920 | tf_op jit(solution)/shard_map/ppermute | solution.py:367
  54.0 1.6 %collective-permute-start.18 = (f32[192,128]{1,0:T(8,128)S(1)}, f32[192,128]{1,0:T(8,128)S(1)}, u32[]{:S(2)}, u32[]{:S(2)}) collective-permute-start(f32[192,128]{1,0:T(8,128)S(1)} %add_add_fusion.2), channel_id=1, source_target_pairs={{0,24},{8,16},{16,8},{24,0},{1,25},{9,17},{17,9},{25,1},{2,26},{10... | collective-permute-start | bytes 294920 | tf_op jit(solution)/shard_map/ppermute | solution.py:367
  57.5 1.7 %collective-permute-start.24 = (f32[256,256]{1,0:T(8,128)S(1)}, f32[256,256]{1,0:T(8,128)S(1)}, u32[]{:S(2)}, u32[]{:S(2)}) collective-permute-start(f32[256,256]{1,0:T(8,128)S(1)} %get-tuple-element.48.own_ref), channel_id=1, source_target_pairs={{0,6},{2,4},{4,2},{6,0},{1,7},{3,5},{5,3},{7,1},{8,14},{10,12},{12... | collective-permute-start | bytes 786440 | tf_op jit(solution)/shard_map/ppermute | solution.py:367
  59.3 1.7 %collective-permute-done.17 = f32[192,128]{1,0:T(8,128)S(1)} collective-permute-done((f32[192,128]{1,0:T(8,128)S(1)}, f32[192,128]{1,0:T(8,128)S(1)}, u32[]{:S(2)}, u32[]{:S(2)}) %collective-permute-start.17) | collective-permute-done | bytes 98336 | tf_op jit(solution)/shard_map/ppermute | solution.py:367
  61.0 1.9 %collective-permute-start.19 = (f32[192,128]{1,0:T(8,128)S(1)}, f32[192,128]{1,0:T(8,128)S(1)}, u32[]{:S(2)}, u32[]{:S(2)}) collective-permute-start(f32[192,128]{1,0:T(8,128)S(1)} %add_add_fusion.1.refs_0_), channel_id=1, source_target_pairs={{0,2},{2,0},{4,6},{6,4},{1,3},{3,1},{5,7},{7,5},{8,10},{10,8},{12,... | collective-permute-start | bytes 294920 | tf_op jit(solution)/shard_map/ppermute | solution.py:367
  63.3 1.6 %collective-permute-done.22 = f32[256,256]{1,0:T(8,128)S(1)} collective-permute-done((f32[256,256]{1,0:T(8,128)S(1)}, f32[256,256]{1,0:T(8,128)S(1)}, u32[]{:S(2)}, u32[]{:S(2)}) %collective-permute-start.22) | collective-permute-done | bytes 262176 | tf_op jit(solution)/shard_map/ppermute | solution.py:367
  66.1 5.8 %collective-permute-done.23 = f32[256,256]{1,0:T(8,128)S(1)} collective-permute-done((f32[256,256]{1,0:T(8,128)S(1)}, f32[256,256]{1,0:T(8,128)S(1)}, u32[]{:S(2)}, u32[]{:S(2)}) %collective-permute-start.23) | collective-permute-done | bytes 262176 | tf_op jit(solution)/shard_map/ppermute | solution.py:367
  76.5 3.5 %collective-permute-start.26 = (f32[256,256]{1,0:T(8,128)S(1)}, f32[256,256]{1,0:T(8,128)S(1)}, u32[]{:S(2)}, u32[]{:S(2)}) collective-permute-start(f32[256,256]{1,0:T(8,128)S(1)} %fusion.51), channel_id=1, source_target_pairs={{0,24},{8,0},{16,8},{24,16},{1,25},{9,1},{17,9},{25,17},{2,26},{10... | collective-permute-start | bytes 786440 | tf_op jit(solution)/shard_map/ppermute | solution.py:362
  80.0 29.8 %inverse_and_solve.1 = (f32[512,512]{1,0:T(8,128)S(1)}, f32[512,512]{1,0:T(8,128)S(1)}, f32[32,512]{1,0:T(8,128)S(1)}) custom-call(s32[2]{0:T(128)S(1)} %pad_add_fusion.place_ref, f32[192,128]{1,0:T(8,128)S(1)} %add_add_fusion.1.refs_0_, f32[192,128]{1,0:T(8,128)S(1)} %collective-permute-done.19.refs_1_, f32[192,128]{1,0:T(8,128)S(1)} %collective-permute-done.20.refs_2_, ...), custom_call_target="tpu_custom_call" | custom-call | flops 30000001024 | bytes 1048576 | tf_op jit(solution)/shard_map/inverse_and_solve/pallas_call | solution.py:348
  110.0 1.5 %collective-permute-done.31.other_ref = f32[256,256]{1,0:T(8,128)S(1)} collective-permute-done((f32[256,256]{1,0:T(8,128)S(1)}, f32[256,256]{1,0:T(8,128)S(1)}, u32[]{:S(2)}, u32[]{:S(2)}) %collective-permute-start.31) | collective-permute-done | bytes 262176 | tf_op jit(solution)/shard_map/ppermute | solution.py:367
  114.0 2.4 %collective-permute-start.40 = (f32[32,256]{1,0:T(8,128)S(1)}, f32[32,256]{1,0:T(8,128)S(1)}, u32[]{:S(2)}, u32[]{:S(2)}) collective-permute-start(f32[32,256]{1,0:T(8,128)S(1)} %get-tuple-element.69), channel_id=1, source_target_pairs={{0,6},{2,4},{4,2},{6,0},{1,7},{3,5},{5,3},{7,1},{8,14},{10,12},{12... | collective-permute-start | bytes 98312 | tf_op jit(solution)/shard_map/ppermute | solution.py:367
  117.5 2.4 %collective-permute-start.34 = (f32[136,128]{1,0:T(8,128)S(1)}, f32[136,128]{1,0:T(8,128)S(1)}, u32[]{:S(2)}, u32[]{:S(2)}) collective-permute-start(f32[136,128]{1,0:T(8,128)S(1)} %get-tuple-element.63), channel_id=1, source_target_pairs={{0,6},{2,4},{4,2},{6,0},{1,7},{3,5},{5,3},{7,1},{8,14},{10,12},{12... | collective-permute-start | bytes 208904 | tf_op jit(solution)/shard_map/ppermute | solution.py:367
  121.2 3.8 %collective-permute-start.42 = (f32[32,256]{1,0:T(8,128)S(1)}, f32[32,256]{1,0:T(8,128)S(1)}, u32[]{:S(2)}, u32[]{:S(2)}) collective-permute-start(f32[32,256]{1,0:T(8,128)S(1)} %fusion.54), channel_id=1, source_target_pairs={{0,24},{8,0},{16,8},{24,16},{1,25},{9,1},{17,9},{25,17},{2,26},{10... | collective-permute-start | bytes 98312 | tf_op jit(solution)/shard_map/ppermute | solution.py:362
  125.7 3.8 %collective-permute-start.37 = (f32[136,128]{1,0:T(8,128)S(1)}, f32[136,128]{1,0:T(8,128)S(1)}, u32[]{:S(2)}, u32[]{:S(2)}) collective-permute-start(f32[136,128]{1,0:T(8,128)S(1)} %add_add_fusion.4), channel_id=1, source_target_pairs={{0,24},{8,16},{16,8},{24,0},{1,25},{9,17},{17,9},{25,1},{2,26},{10... | collective-permute-start | bytes 208904 | tf_op jit(solution)/shard_map/ppermute | solution.py:367
  129.5 1.8 %fusion.52 = f32[512,512]{1,0:T(8,128)S(1)} fusion(f32[512,512]{1,0:T(8,128)S(1)} %get-tuple-element.66, f32[512,512]{1,0:T(8,128)S(1)} %get-tuple-element.67), kind=kOutput, calls=%fused_computation.125 | convolution fusion | flops 1610612736 | bytes 3145728 | tf_op jit(solution)/shard_map/dot_general | solution.py:20
  131.4 1.9 %convolution_subtract_fusion = bf16[512,512]{1,0:T(8,128)(2,1)S(1)} fusion(f32[512,512]{1,0:T(8,128)S(1)} %get-tuple-element.67, f32[512,512]{1,0:T(8,128)S(1)} %get-tuple-element.68, f32[512,512]{1,0:T(8,128)S(1)} %fusion.52), kind=kOutput, calls=%fused_computation.10 | convolution fusion | flops 1611137024 | bytes 3670016 | tf_op jit(solution)/shard_map/dot_general | solution.py:20
  135.2 11.3 %all_to_all.6 = f32[16,8,128]{2,1,0:T(8,128)S(1)} all-to-all(f32[16,8,128]{2,1,0:T(8,128)S(1)} %broadcast_in_dim.14), channel_id=1, replica_groups=mesh['blk'=4,'leaf'=4,'samp'=2] {'blk','leaf'}, dimensions={0} | all-to-all | bytes 131072 | tf_op jit(solution)/shard_map/all_to_all | solution.py:379
  (136 shorter events, 33.4 us)
Async XLA Ops:
  2.4 12.6 %collective-permute-start.3 = (f32[8,256]{1,0:T(8,128)}, f32[8,256]{1,0:T(8,128)S(1)}, u32[]{:S(2)}, u32[]{:S(2)}) collective-permute-start(f32[8,256]{1,0:T(8,128)} %get-tuple-element.38), channel_id=1, source_target_pairs={{0,24},{8,0},{16,8},{24,16},{1,25},{9,1},{17,9},{25,17},{2,26},{10... | collective-permute-start | bytes 24584 | tf_op jit(solution)/shard_map/ppermute | solution.py:362
  7.5 9.1 %collective-permute-start.4 = (f32[8,256]{1,0:T(8,128)}, f32[8,256]{1,0:T(8,128)S(1)}, u32[]{:S(2)}, u32[]{:S(2)}) collective-permute-start(f32[8,256]{1,0:T(8,128)} %get-tuple-element.38), channel_id=1, source_target_pairs={{0,8},{8,16},{16,24},{24,0},{1,9},{9,17},{17,25},{25,1},{2,10},{10... | collective-permute-start | bytes 24584 | tf_op jit(solution)/shard_map/ppermute | solution.py:362
  7.5 10.9 %collective-permute-start = (f32[168,256]{1,0:T(8,128)}, f32[168,256]{1,0:T(8,128)S(1)}, u32[]{:S(2)}, u32[]{:S(2)}) collective-permute-start(f32[168,256]{1,0:T(8,128)} %get-tuple-element.36), channel_id=1, source_target_pairs={{0,2},{2,0},{4,6},{6,4},{1,3},{3,1},{5,7},{7,5},{8,10},{10,8},{12,... | collective-permute-start | bytes 516104 | tf_op jit(solution)/shard_map/ppermute | solution.py:367
  9.0 10.0 %collective-permute-start.1 = (f32[168,256]{1,0:T(8,128)}, f32[168,256]{1,0:T(8,128)S(1)}, u32[]{:S(2)}, u32[]{:S(2)}) collective-permute-start(f32[168,256]{1,0:T(8,128)} %get-tuple-element.36), channel_id=1, source_target_pairs={{0,4},{2,6},{4,0},{6,2},{1,5},{3,7},{5,1},{7,3},{8,12},{10,14},{12... | collective-permute-start | bytes 516104 | tf_op jit(solution)/shard_map/ppermute | solution.py:367
  10.5 8.5 %collective-permute-start.2 = (f32[168,256]{1,0:T(8,128)}, f32[168,256]{1,0:T(8,128)S(1)}, u32[]{:S(2)}, u32[]{:S(2)}) collective-permute-start(f32[168,256]{1,0:T(8,128)} %get-tuple-element.36), channel_id=1, source_target_pairs={{0,6},{2,4},{4,2},{6,0},{1,7},{3,5},{5,3},{7,1},{8,14},{10,12},{12... | collective-permute-start | bytes 516104 | tf_op jit(solution)/shard_map/ppermute | solution.py:367
  15.0 12.1 %collective-permute-start.7 = (f32[128,256]{1,0:T(8,128)}, f32[128,256]{1,0:T(8,128)S(1)}, u32[]{:S(2)}, u32[]{:S(2)}) collective-permute-start(f32[128,256]{1,0:T(8,128)} %get-tuple-element.39), channel_id=1, source_target_pairs={{0,2},{2,0},{4,6},{6,4},{1,3},{3,1},{5,7},{7,5},{8,10},{10,8},{12,... | collective-permute-start | bytes 393224 | tf_op jit(solution)/shard_map/ppermute | solution.py:367
  16.6 10.5 %collective-permute-start.8 = (f32[128,256]{1,0:T(8,128)}, f32[128,256]{1,0:T(8,128)S(1)}, u32[]{:S(2)}, u32[]{:S(2)}) collective-permute-start(f32[128,256]{1,0:T(8,128)} %get-tuple-element.39), channel_id=1, source_target_pairs={{0,4},{2,6},{4,0},{6,2},{1,5},{3,7},{5,1},{7,3},{8,12},{10,14},{12... | collective-permute-start | bytes 393224 | tf_op jit(solution)/shard_map/ppermute | solution.py:367
  18.4 8.7 %collective-permute-start.9 = (f32[128,256]{1,0:T(8,128)}, f32[128,256]{1,0:T(8,128)S(1)}, u32[]{:S(2)}, u32[]{:S(2)}) collective-permute-start(f32[128,256]{1,0:T(8,128)} %get-tuple-element.39), channel_id=1, source_target_pairs={{0,6},{2,4},{4,2},{6,0},{1,7},{3,5},{5,3},{7,1},{8,14},{10,12},{12... | collective-permute-start | bytes 393224 | tf_op jit(solution)/shard_map/ppermute | solution.py:367
  21.5 17.1 %collective-permute-start.6 = (f32[160,256]{1,0:T(8,128)S(1)}, f32[160,256]{1,0:T(8,128)S(1)}, u32[]{:S(2)}, u32[]{:S(2)}) collective-permute-start(f32[160,256]{1,0:T(8,128)S(1)} %fusion.25), channel_id=1, source_target_pairs={{0,24},{8,0},{16,8},{24,16},{1,25},{9,1},{17,9},{25,17},{2,26},{10... | collective-permute-start | bytes 491528 | tf_op jit(solution)/shard_map/ppermute | solution.py:362
  27.0 11.5 %collective-permute-start.5 = (f32[160,256]{1,0:T(8,128)S(1)}, f32[160,256]{1,0:T(8,128)S(1)}, u32[]{:S(2)}, u32[]{:S(2)}) collective-permute-start(f32[160,256]{1,0:T(8,128)S(1)} %fusion.26), channel_id=1, source_target_pairs={{0,8},{8,16},{16,24},{24,0},{1,9},{9,17},{17,25},{25,1},{2,10},{10... | collective-permute-start | bytes 491528 | tf_op jit(solution)/shard_map/ppermute | solution.py:362
  28.5 8.2 %collective-permute-start.10 = (f32[128,256]{1,0:T(8,128)S(1)}, f32[128,256]{1,0:T(8,128)S(1)}, u32[]{:S(2)}, u32[]{:S(2)}) collective-permute-start(f32[128,256]{1,0:T(8,128)S(1)} %fusion.48), channel_id=1, source_target_pairs={{0,8},{8,16},{16,24},{24,0},{1,9},{9,17},{17,25},{25,1},{2,10},{10... | collective-permute-start | bytes 393224 | tf_op jit(solution)/shard_map/ppermute | solution.py:362
  28.6 9.3 %collective-permute-start.11 = (f32[128,256]{1,0:T(8,128)S(1)}, f32[128,256]{1,0:T(8,128)S(1)}, u32[]{:S(2)}, u32[]{:S(2)}) collective-permute-start(f32[128,256]{1,0:T(8,128)S(1)} %fusion.49), channel_id=1, source_target_pairs={{0,24},{8,0},{16,8},{24,16},{1,25},{9,1},{17,9},{25,17},{2,26},{10... | collective-permute-start | bytes 393224 | tf_op jit(solution)/shard_map/ppermute | solution.py:362
  51.2 6.3 %collective-permute-start.16 = (f32[192,128]{1,0:T(8,128)S(1)}, f32[192,128]{1,0:T(8,128)S(1)}, u32[]{:S(2)}, u32[]{:S(2)}) collective-permute-start(f32[192,128]{1,0:T(8,128)S(1)} %add_add_fusion.2), channel_id=1, source_target_pairs={{0,8},{8,0},{16,24},{24,16},{1,9},{9,1},{17,25},{25,17},{2,10},{10... | collective-permute-start | bytes 294920 | tf_op jit(solution)/shard_map/ppermute | solution.py:367
  52.0 9.0 %collective-permute-start.17 = (f32[192,128]{1,0:T(8,128)S(1)}, f32[192,128]{1,0:T(8,128)S(1)}, u32[]{:S(2)}, u32[]{:S(2)}) collective-permute-start(f32[192,128]{1,0:T(8,128)S(1)} %add_add_fusion.2), channel_id=1, source_target_pairs={{0,16},{8,24},{16,0},{24,8},{1,17},{9,25},{17,1},{25,9},{2,18},{10... | collective-permute-start | bytes 294920 | tf_op jit(solution)/shard_map/ppermute | solution.py:367
  54.0 7.0 %collective-permute-start.18 = (f32[192,128]{1,0:T(8,128)S(1)}, f32[192,128]{1,0:T(8,128)S(1)}, u32[]{:S(2)}, u32[]{:S(2)}) collective-permute-start(f32[192,128]{1,0:T(8,128)S(1)} %add_add_fusion.2), channel_id=1, source_target_pairs={{0,24},{8,16},{16,8},{24,0},{1,25},{9,17},{17,9},{25,1},{2,26},{10... | collective-permute-start | bytes 294920 | tf_op jit(solution)/shard_map/ppermute | solution.py:367
  55.7 9.2 %collective-permute-start.22 = (f32[256,256]{1,0:T(8,128)S(1)}, f32[256,256]{1,0:T(8,128)S(1)}, u32[]{:S(2)}, u32[]{:S(2)}) collective-permute-start(f32[256,256]{1,0:T(8,128)S(1)} %get-tuple-element.48.own_ref), channel_id=1, source_target_pairs={{0,2},{2,0},{4,6},{6,4},{1,3},{3,1},{5,7},{7,5},{8,10},{10,8},{12,... | collective-permute-start | bytes 786440 | tf_op jit(solution)/shard_map/ppermute | solution.py:367
  56.6 15.3 %collective-permute-start.23 = (f32[256,256]{1,0:T(8,128)S(1)}, f32[256,256]{1,0:T(8,128)S(1)}, u32[]{:S(2)}, u32[]{:S(2)}) collective-permute-start(f32[256,256]{1,0:T(8,128)S(1)} %get-tuple-element.48.own_ref), channel_id=1, source_target_pairs={{0,4},{2,6},{4,0},{6,2},{1,5},{3,7},{5,1},{7,3},{8,12},{10,14},{12... | collective-permute-start | bytes 786440 | tf_op jit(solution)/shard_map/ppermute | solution.py:367
  57.5 14.4 %collective-permute-start.24 = (f32[256,256]{1,0:T(8,128)S(1)}, f32[256,256]{1,0:T(8,128)S(1)}, u32[]{:S(2)}, u32[]{:S(2)}) collective-permute-start(f32[256,256]{1,0:T(8,128)S(1)} %get-tuple-element.48.own_ref), channel_id=1, source_target_pairs={{0,6},{2,4},{4,2},{6,0},{1,7},{3,5},{5,3},{7,1},{8,14},{10,12},{12... | collective-permute-start | bytes 786440 | tf_op jit(solution)/shard_map/ppermute | solution.py:367
  61.0 14.0 %collective-permute-start.19 = (f32[192,128]{1,0:T(8,128)S(1)}, f32[192,128]{1,0:T(8,128)S(1)}, u32[]{:S(2)}, u32[]{:S(2)}) collective-permute-start(f32[192,128]{1,0:T(8,128)S(1)} %add_add_fusion.1.refs_0_), channel_id=1, source_target_pairs={{0,2},{2,0},{4,6},{6,4},{1,3},{3,1},{5,7},{7,5},{8,10},{10,8},{12,... | collective-permute-start | bytes 294920 | tf_op jit(solution)/shard_map/ppermute | solution.py:367
  62.9 12.2 %collective-permute-start.20 = (f32[192,128]{1,0:T(8,128)S(1)}, f32[192,128]{1,0:T(8,128)S(1)}, u32[]{:S(2)}, u32[]{:S(2)}) collective-permute-start(f32[192,128]{1,0:T(8,128)S(1)} %add_add_fusion.1.refs_0_), channel_id=1, source_target_pairs={{0,4},{2,6},{4,0},{6,2},{1,5},{3,7},{5,1},{7,3},{8,12},{10,14},{12... | collective-permute-start | bytes 294920 | tf_op jit(solution)/shard_map/ppermute | solution.py:367
  64.9 10.2 %collective-permute-start.21 = (f32[192,128]{1,0:T(8,128)S(1)}, f32[192,128]{1,0:T(8,128)S(1)}, u32[]{:S(2)}, u32[]{:S(2)}) collective-permute-start(f32[192,128]{1,0:T(8,128)S(1)} %add_add_fusion.1.refs_0_), channel_id=1, source_target_pairs={{0,6},{2,4},{4,2},{6,0},{1,7},{3,5},{5,3},{7,1},{8,14},{10,12},{12... | collective-permute-start | bytes 294920 | tf_op jit(solution)/shard_map/ppermute | solution.py:367
  76.2 33.7 %collective-permute-start.25 = (f32[256,256]{1,0:T(8,128)S(1)}, f32[256,256]{1,0:T(8,128)S(1)}, u32[]{:S(2)}, u32[]{:S(2)}) collective-permute-start(f32[256,256]{1,0:T(8,128)S(1)} %fusion.50), channel_id=1, source_target_pairs={{0,8},{8,16},{16,24},{24,0},{1,9},{9,17},{17,25},{25,1},{2,10},{10... | collective-permute-start | bytes 786440 | tf_op jit(solution)/shard_map/ppermute | solution.py:362
  76.5 33.4 %collective-permute-start.26 = (f32[256,256]{1,0:T(8,128)S(1)}, f32[256,256]{1,0:T(8,128)S(1)}, u32[]{:S(2)}, u32[]{:S(2)}) collective-permute-start(f32[256,256]{1,0:T(8,128)S(1)} %fusion.51), channel_id=1, source_target_pairs={{0,24},{8,0},{16,8},{24,16},{1,25},{9,1},{17,9},{25,17},{2,26},{10... | collective-permute-start | bytes 786440 | tf_op jit(solution)/shard_map/ppermute | solution.py:362
  112.9 7.0 %collective-permute-start.39 = (f32[32,256]{1,0:T(8,128)S(1)}, f32[32,256]{1,0:T(8,128)S(1)}, u32[]{:S(2)}, u32[]{:S(2)}) collective-permute-start(f32[32,256]{1,0:T(8,128)S(1)} %get-tuple-element.69), channel_id=1, source_target_pairs={{0,4},{2,6},{4,0},{6,2},{1,5},{3,7},{5,1},{7,3},{8,12},{10,14},{12... | collective-permute-start | bytes 98312 | tf_op jit(solution)/shard_map/ppermute | solution.py:367
  116.4 8.6 %collective-permute-start.32 = (f32[136,128]{1,0:T(8,128)S(1)}, f32[136,128]{1,0:T(8,128)S(1)}, u32[]{:S(2)}, u32[]{:S(2)}) collective-permute-start(f32[136,128]{1,0:T(8,128)S(1)} %get-tuple-element.63), channel_id=1, source_target_pairs={{0,2},{2,0},{4,6},{6,4},{1,3},{3,1},{5,7},{7,5},{8,10},{10,8},{12,... | collective-permute-start | bytes 208904 | tf_op jit(solution)/shard_map/ppermute | solution.py:367
  116.5 8.5 %collective-permute-start.33 = (f32[136,128]{1,0:T(8,128)S(1)}, f32[136,128]{1,0:T(8,128)S(1)}, u32[]{:S(2)}, u32[]{:S(2)}) collective-permute-start(f32[136,128]{1,0:T(8,128)S(1)} %get-tuple-element.63), channel_id=1, source_target_pairs={{0,4},{2,6},{4,0},{6,2},{1,5},{3,7},{5,1},{7,3},{8,12},{10,14},{12... | collective-permute-start | bytes 208904 | tf_op jit(solution)/shard_map/ppermute | solution.py:367
  117.5 7.5 %collective-permute-start.34 = (f32[136,128]{1,0:T(8,128)S(1)}, f32[136,128]{1,0:T(8,128)S(1)}, u32[]{:S(2)}, u32[]{:S(2)}) collective-permute-start(f32[136,128]{1,0:T(8,128)S(1)} %get-tuple-element.63), channel_id=1, source_target_pairs={{0,6},{2,4},{4,2},{6,0},{1,7},{3,5},{5,3},{7,1},{8,14},{10,12},{12... | collective-permute-start | bytes 208904 | tf_op jit(solution)/shard_map/ppermute | solution.py:367
  121.1 13.4 %collective-permute-start.41 = (f32[32,256]{1,0:T(8,128)S(1)}, f32[32,256]{1,0:T(8,128)S(1)}, u32[]{:S(2)}, u32[]{:S(2)}) collective-permute-start(f32[32,256]{1,0:T(8,128)S(1)} %fusion.53), channel_id=1, source_target_pairs={{0,8},{8,16},{16,24},{24,0},{1,9},{9,17},{17,25},{25,1},{2,10},{10... | collective-permute-start | bytes 98312 | tf_op jit(solution)/shard_map/ppermute | solution.py:362
  121.2 13.3 %collective-permute-start.42 = (f32[32,256]{1,0:T(8,128)S(1)}, f32[32,256]{1,0:T(8,128)S(1)}, u32[]{:S(2)}, u32[]{:S(2)}) collective-permute-start(f32[32,256]{1,0:T(8,128)S(1)} %fusion.54), channel_id=1, source_target_pairs={{0,24},{8,0},{16,8},{24,16},{1,25},{9,1},{17,9},{25,17},{2,26},{10... | collective-permute-start | bytes 98312 | tf_op jit(solution)/shard_map/ppermute | solution.py:362
  125.0 8.7 %collective-permute-start.35 = (f32[136,128]{1,0:T(8,128)S(1)}, f32[136,128]{1,0:T(8,128)S(1)}, u32[]{:S(2)}, u32[]{:S(2)}) collective-permute-start(f32[136,128]{1,0:T(8,128)S(1)} %add_add_fusion.4), channel_id=1, source_target_pairs={{0,8},{8,0},{16,24},{24,16},{1,9},{9,1},{17,25},{25,17},{2,10},{10... | collective-permute-start | bytes 208904 | tf_op jit(solution)/shard_map/ppermute | solution.py:367
  125.1 8.6 %collective-permute-start.36 = (f32[136,128]{1,0:T(8,128)S(1)}, f32[136,128]{1,0:T(8,128)S(1)}, u32[]{:S(2)}, u32[]{:S(2)}) collective-permute-start(f32[136,128]{1,0:T(8,128)S(1)} %add_add_fusion.4), channel_id=1, source_target_pairs={{0,16},{8,24},{16,0},{24,8},{1,17},{9,25},{17,1},{25,9},{2,18},{10... | collective-permute-start | bytes 208904 | tf_op jit(solution)/shard_map/ppermute | solution.py:367
  125.7 8.0 %collective-permute-start.37 = (f32[136,128]{1,0:T(8,128)S(1)}, f32[136,128]{1,0:T(8,128)S(1)}, u32[]{:S(2)}, u32[]{:S(2)}) collective-permute-start(f32[136,128]{1,0:T(8,128)S(1)} %add_add_fusion.4), channel_id=1, source_target_pairs={{0,24},{8,16},{16,8},{24,0},{1,25},{9,17},{17,9},{25,1},{2,26},{10... | collective-permute-start | bytes 208904 | tf_op jit(solution)/shard_map/ppermute | solution.py:367
  (13 other events, 56.4 us)

commit v2 on v1

--- a/solution.py
+++ b/solution.py
@@ -229,7 +229,7 @@
 
 def image_kernel(
     core_ref, solved_ref, sketch_ref, own_ref, other_ref, rhs_ref, image_rhs_ref,
-    sketches_ref, direction_ref, image_ref, sums_ref,
+    sketches_ref, direction_ref, image_ref, packet_ref,
 ):
     half, width = own_ref.shape
     core = core_ref[0]
@@ -246,12 +246,16 @@
     samples = rhs.shape[0]
     count = moved.shape[1] // TILE
     for i in range(count):
-        sums_ref[i * samples : (i + 1) * samples, :] = moved[:, i * TILE : (i + 1) * TILE]
+        packet_ref[i * samples : (i + 1) * samples, :] = moved[:, i * TILE : (i + 1) * TILE]
     at = count * samples
     ones = jnp.ones((8, width), jnp.float32)
-    sums_ref[at:, :] = jnp.zeros((8, TILE), jnp.float32)
-    sums_ref[at : at + 1, :samples] = mm_t(ones, rhs * direction)[0:1, :]
-    sums_ref[at + 1 : at + 2, :samples] = mm_t(ones, direction * image)[0:1, :]
+    packet_ref[at : at + 8, :] = jnp.zeros((8, TILE), jnp.float32)
+    packet_ref[at : at + 1, :samples] = mm_t(ones, rhs * direction)[0:1, :]
+    packet_ref[at + 1 : at + 2, :samples] = mm_t(ones, direction * image)[0:1, :]
+    at += 8
+    for i in range(width // TILE):
+        packet_ref[at : at + samples, :] = image[:, i * TILE : (i + 1) * TILE]
+        at += samples
 
 
 def prepare_kernel(
@@ -483,10 +487,10 @@
         flops=10**9,
     )
 
+    *shares, late_sketch = lax.optimization_barrier((*shares, sketch_half))
     share = shares[0]
     for m in range(1, leaves):
         share = share + swapped(shares[m], "leaf", m)
-    share, late_sketch = lax.optimization_barrier((share, sketch_half))
     upward, downward, gathered = sums(slab(late_sketch))
     here = mm(gathered, columns[1]) + noise_variance * late_sketch
     shares = slab(axis_sum(share, "blk"))
@@ -506,10 +510,11 @@
     from_below, from_above, solved = lax.optimization_barrier((from_below, from_above, solved))
     own_image = here + from_below + from_above
 
-    sketches, direction, image, partial = kernel_call(
+    sum_rows = samples * (sketch_size // TILE) + 8
+    sketches, direction, image, packet = kernel_call(
         image_kernel,
         "image",
-        [(sketch_size, 2 * width)] + [(samples, width)] * 2 + [(samples * (sketch_size // TILE) + 8, TILE)],
+        [(sketch_size, 2 * width)] + [(samples, width)] * 2 + [(sum_rows + samples * (width // TILE), TILE)],
         core,
         solved,
         sketch,
@@ -518,15 +523,25 @@
         rhs,
         image_rhs,
     )
-    partial, late_image = lax.optimization_barrier((partial, image))
-    upward, downward, gathered = sums(slab(late_image))
-    from_below, from_above = sent(upward, downward)
-    image_twice = mm(gathered, columns[1]) + from_below + from_above + noise_variance * late_image
-    slab_sum = axis_sum(partial, "leaf")
-    inverse, _ = lax.optimization_barrier((inverse, slab_sum))
+    packets = slab(packet)
+    slab_sum = (packets[0][:sum_rows] + packets[1][:sum_rows]) + (packets[2][:sum_rows] + packets[3][:sum_rows])
+    upward, downward, gathered = sums([from_tiles(p[sum_rows:], samples) for p in packets])
+    here = mm(gathered, columns[1]) + noise_variance * image
+    if cycle == 4:
+        even = own_slab % 2 == 0
+        one, three = (
+            swapped(jnp.concatenate([slab_sum, to_tiles(jnp.where(even, first, second))], axis=0), "blk", m)
+            for m, first, second in ((1, upward, downward), (3, downward, upward))
+        )
+        two = swapped(slab_sum, "blk", 2)
+        total = (slab_sum + one[:sum_rows]) + (two + three[:sum_rows])
+        from_below, from_above = from_tiles(one[sum_rows:], samples), from_tiles(three[sum_rows:], samples)
+    else:
+        total = lax.psum(slab_sum, "blk")
+        from_below, from_above = sent(upward, downward)
+    image_twice = here + from_below + from_above
     solves = mm(inverse, sketches)
     solves = solves + rough_mm(inverse, sketches - mm(system, solves))
-    total = axis_sum(slab_sum, "blk")
     moved = from_tiles(total[:-8], samples)
     dots = total[-8:]
     inner_first, curvature = dots[0, :samples, None], dots[1, :samples, None]

time: 148 us -> 144 us (0.973)
  starting transfers between devices: 55.3 us -> 47.8 us
  waiting for transfers between devices: 21.8 us -> 25.1 us
    ppermute x10 -> x8, starting transfers between devices: 20.5 us -> 16.7 us  [shifted(): lax.ppermute(values, axis, [(i, (i + distance) % size) for i in range(siz...]
    ppermute x33 -> x30, starting transfers between devices: 34.7 us -> 31.1 us  [swapped(): return lax.ppermute(values, axis, [(i, i ^ mask) for i in range(size)])]
    ppermute x33 -> x30, waiting for transfers between devices: 17.4 us -> 20.7 us  [swapped(): return lax.ppermute(values, axis, [(i, i ^ mask) for i in range(size)])]
    ppermute x10 -> x8, waiting for transfers between devices: 4.4 us -> 4.39 us  [shifted(): lax.ppermute(values, axis, [(i, (i + distance) % size) for i in range(siz...]
  transfers between devices with their start and end apart: 43 -> 38, of which waited for: 11 -> 15; matrix products, arithmetic and copies ran while one was open for 14% -> 13% of each run, Pallas kernels for 20% -> 21%
where the time goes in v2:
time: 144 us
  starting transfers between devices  47.8 us (33%)
  Pallas kernels  34.8 us (24%)
  waiting for transfers between devices  25.1 us (17%)
  matrix products  14 us (10%)
  blocking collectives  11.9 us (8%)
  other arithmetic  4.74 us (3%)
  local copies, waits for them, and re-layouts  4.38 us (3%)
    pallas_call x3, Pallas kernels, kernel_call(): pl.pallas_call(kernel, out_shape=tuple((jax.ShapeDtypeStruct(shape, jnp.f...  33 us
    ppermute x30, starting transfers between devices, swapped(): return lax.ppermute(values, axis, [(i, i ^ mask) for i in range(size)])  31.1 us
    ppermute x30, waiting for transfers between devices, swapped(): return lax.ppermute(values, axis, [(i, i ^ mask) for i in range(size)])  20.7 us
    ppermute x8, starting transfers between devices, shifted(): lax.ppermute(values, axis, [(i, (i + distance) % size) for i in range(siz...  16.7 us
    dot_general x15, matrix products, mm(): jnp.dot(left, right, precision=HIGHEST, preferred_element_type=jnp.float32)  13.6 us
    all_to_all x1, blocking collectives, exchange(): return lax.all_to_all(values, POINT_AXES, 0, 0, tiled=True)  11.9 us
    ppermute x8, waiting for transfers between devices, shifted(): lax.ppermute(values, axis, [(i, (i + distance) % size) for i in range(siz...  4.39 us
  transfers between devices with their start and end apart: 38, of which 15 were waited for; matrix products, arithmetic and copies ran while one was open for 13% of the time, Pallas kernels for 21%

profile of v2, /device:TPU:0, one launch (start us, length us, event | category | flops | bytes accessed | tf_op | source)
XLA Modules:
  0.0 144.1 jit_solution(10327669346455487847)
XLA Ops:
  0.6 1.8 %prepare.1 = (f32[168,256]{1,0:T(8,128)}, f32[128,256]{1,0:T(8,128)}, f32[8,256]{1,0:T(8,128)}) custom-call(s32[1]{0:T(128)} %bitcast.core_ref, f32[3,256]{1,0:T(4,128)} %points_ref.1, s32[1,8]{1,0:T(1,128)} %neighbors_ref.1, f32[512,256]{1,0:T(8,128)} %omega_ref.1, f32[1,256]{1,0:T(1,128)} %bitcast.139, f32[32,256]{1,0:T(8,128)} %prior_ref.1), custom_call_target="tpu_custom_call" | custom-call | flops 1000000 | bytes 524288 | tf_op jit(solution)/shard_map/prepare/pallas_call | solution.py:298
  2.4 5.1 %collective-permute-start.3 = (f32[8,256]{1,0:T(8,128)}, f32[8,256]{1,0:T(8,128)S(1)}, u32[]{:S(2)}, u32[]{:S(2)}) collective-permute-start(f32[8,256]{1,0:T(8,128)} %get-tuple-element.38), channel_id=1, source_target_pairs={{0,24},{8,0},{16,8},{24,16},{1,25},{9,1},{17,9},{25,17},{2,26},{10... | collective-permute-start | bytes 24584 | tf_op jit(solution)/shard_map/ppermute | solution.py:366
  7.5 1.5 %collective-permute-start = (f32[168,256]{1,0:T(8,128)}, f32[168,256]{1,0:T(8,128)S(1)}, u32[]{:S(2)}, u32[]{:S(2)}) collective-permute-start(f32[168,256]{1,0:T(8,128)} %get-tuple-element.36), channel_id=1, source_target_pairs={{0,2},{2,0},{4,6},{6,4},{1,3},{3,1},{5,7},{7,5},{8,10},{10,8},{12,... | collective-permute-start | bytes 516104 | tf_op jit(solution)/shard_map/ppermute | solution.py:371
  9.0 1.5 %collective-permute-start.1 = (f32[168,256]{1,0:T(8,128)}, f32[168,256]{1,0:T(8,128)S(1)}, u32[]{:S(2)}, u32[]{:S(2)}) collective-permute-start(f32[168,256]{1,0:T(8,128)} %get-tuple-element.36), channel_id=1, source_target_pairs={{0,4},{2,6},{4,0},{6,2},{1,5},{3,7},{5,1},{7,3},{8,12},{10,14},{12... | collective-permute-start | bytes 516104 | tf_op jit(solution)/shard_map/ppermute | solution.py:371
  15.0 1.6 %collective-permute-start.7 = (f32[128,256]{1,0:T(8,128)}, f32[128,256]{1,0:T(8,128)S(1)}, u32[]{:S(2)}, u32[]{:S(2)}) collective-permute-start(f32[128,256]{1,0:T(8,128)} %get-tuple-element.39), channel_id=1, source_target_pairs={{0,2},{2,0},{4,6},{6,4},{1,3},{3,1},{5,7},{7,5},{8,10},{10,8},{12,... | collective-permute-start | bytes 393224 | tf_op jit(solution)/shard_map/ppermute | solution.py:371
  16.6 1.5 %collective-permute-start.8 = (f32[128,256]{1,0:T(8,128)}, f32[128,256]{1,0:T(8,128)S(1)}, u32[]{:S(2)}, u32[]{:S(2)}) collective-permute-start(f32[128,256]{1,0:T(8,128)} %get-tuple-element.39), channel_id=1, source_target_pairs={{0,4},{2,6},{4,0},{6,2},{1,5},{3,7},{5,1},{7,3},{8,12},{10,14},{12... | collective-permute-start | bytes 393224 | tf_op jit(solution)/shard_map/ppermute | solution.py:371
  21.5 3.9 %collective-permute-start.6 = (f32[160,256]{1,0:T(8,128)S(1)}, f32[160,256]{1,0:T(8,128)S(1)}, u32[]{:S(2)}, u32[]{:S(2)}) collective-permute-start(f32[160,256]{1,0:T(8,128)S(1)} %fusion.25), channel_id=1, source_target_pairs={{0,24},{8,0},{16,8},{24,16},{1,25},{9,1},{17,9},{25,17},{2,26},{10... | collective-permute-start | bytes 491528 | tf_op jit(solution)/shard_map/ppermute | solution.py:366
  28.6 4.0 %collective-permute-start.11 = (f32[128,256]{1,0:T(8,128)S(1)}, f32[128,256]{1,0:T(8,128)S(1)}, u32[]{:S(2)}, u32[]{:S(2)}) collective-permute-start(f32[128,256]{1,0:T(8,128)S(1)} %fusion.57), channel_id=1, source_target_pairs={{0,24},{8,0},{16,8},{24,16},{1,25},{9,1},{17,9},{25,17},{2,26},{10... | collective-permute-start | bytes 393224 | tf_op jit(solution)/shard_map/ppermute | solution.py:366
  33.6 3.2 %collective-permute-done.10 = f32[128,256]{1,0:T(8,128)S(1)} collective-permute-done((f32[128,256]{1,0:T(8,128)S(1)}, f32[128,256]{1,0:T(8,128)S(1)}, u32[]{:S(2)}, u32[]{:S(2)}) %collective-permute-start.10) | collective-permute-done | bytes 131104 | tf_op jit(solution)/shard_map/ppermute | solution.py:366
  39.6 1.4 collective-permute-done.12.other_ref
  41.0 1.6 %payload.1 = (f32[512,256]{1,0:T(8,128)S(1)}, f32[192,128]{1,0:T(8,128)S(1)}, f32[192,128]{1,0:T(8,128)S(1)}, f32[192,128]{1,0:T(8,128)S(1)}, f32[192,128]{1,0:T(8,128)S(1)}) custom-call(s32[2]{0:T(128)S(1)} %pad_add_fusion.place_ref, f32[256,256]{1,0:T(8,128)S(1)} %get-tuple-element.77.omega_ref, f32[256,256]{1,0:T(8,128)S(1)} %get-tuple-element.51.own_ref, ...), custom_call_target="tpu_custom_call" | custom-call | flops 1000000000 | bytes 1048576 | tf_op jit(solution)/shard_map/payload/pallas_call | solution.py:352
  42.7 1.5 %collective-permute-start.13 = (f32[192,128]{1,0:T(8,128)S(1)}, f32[192,128]{1,0:T(8,128)S(1)}, u32[]{:S(2)}, u32[]{:S(2)}) collective-permute-start(f32[192,128]{1,0:T(8,128)S(1)} %get-tuple-element.48), channel_id=1, source_target_pairs={{0,2},{2,0},{4,6},{6,4},{1,3},{3,1},{5,7},{7,5},{8,10},{10,8},{12,... | collective-permute-start | bytes 294920 | tf_op jit(solution)/shard_map/ppermute | solution.py:371
  44.2 1.5 %collective-permute-start.14 = (f32[192,128]{1,0:T(8,128)S(1)}, f32[192,128]{1,0:T(8,128)S(1)}, u32[]{:S(2)}, u32[]{:S(2)}) collective-permute-start(f32[192,128]{1,0:T(8,128)S(1)} %get-tuple-element.49), channel_id=1, source_target_pairs={{0,4},{2,6},{4,0},{6,2},{1,5},{3,7},{5,1},{7,3},{8,12},{10,14},{12... | collective-permute-start | bytes 294920 | tf_op jit(solution)/shard_map/ppermute | solution.py:371
  46.2 1.4 collective-permute-start.22
  47.7 1.7 %collective-permute-done.14 = f32[192,128]{1,0:T(8,128)S(1)} collective-permute-done((f32[192,128]{1,0:T(8,128)S(1)}, f32[192,128]{1,0:T(8,128)S(1)}, u32[]{:S(2)}, u32[]{:S(2)}) %collective-permute-start.14) | collective-permute-done | bytes 98336 | tf_op jit(solution)/shard_map/ppermute | solution.py:371
  49.4 2.9 %collective-permute-done.15 = f32[192,128]{1,0:T(8,128)S(1)} collective-permute-done((f32[192,128]{1,0:T(8,128)S(1)}, f32[192,128]{1,0:T(8,128)S(1)}, u32[]{:S(2)}, u32[]{:S(2)}) %collective-permute-start.15) | collective-permute-done | bytes 98336 | tf_op jit(solution)/shard_map/ppermute | solution.py:371
  53.1 2.0 %collective-permute-start.17 = (f32[192,128]{1,0:T(8,128)S(1)}, f32[192,128]{1,0:T(8,128)S(1)}, u32[]{:S(2)}, u32[]{:S(2)}) collective-permute-start(f32[192,128]{1,0:T(8,128)S(1)} %add_add_fusion.2), channel_id=1, source_target_pairs={{0,16},{8,24},{16,0},{24,8},{1,17},{9,25},{17,1},{25,9},{2,18},{10... | collective-permute-start | bytes 294920 | tf_op jit(solution)/shard_map/ppermute | solution.py:371
  55.1 1.7 %collective-permute-start.18 = (f32[192,128]{1,0:T(8,128)S(1)}, f32[192,128]{1,0:T(8,128)S(1)}, u32[]{:S(2)}, u32[]{:S(2)}) collective-permute-start(f32[192,128]{1,0:T(8,128)S(1)} %add_add_fusion.2), channel_id=1, source_target_pairs={{0,24},{8,16},{16,8},{24,0},{1,25},{9,17},{17,9},{25,1},{2,26},{10... | collective-permute-start | bytes 294920 | tf_op jit(solution)/shard_map/ppermute | solution.py:371
  60.1 1.6 %collective-permute-done.18 = f32[192,128]{1,0:T(8,128)S(1)} collective-permute-done((f32[192,128]{1,0:T(8,128)S(1)}, f32[192,128]{1,0:T(8,128)S(1)}, u32[]{:S(2)}, u32[]{:S(2)}) %collective-permute-start.18) | collective-permute-done | bytes 98336 | tf_op jit(solution)/shard_map/ppermute | solution.py:371
  63.3 1.9 %collective-permute-start.21 = (f32[192,128]{1,0:T(8,128)S(1)}, f32[192,128]{1,0:T(8,128)S(1)}, u32[]{:S(2)}, u32[]{:S(2)}) collective-permute-start(f32[192,128]{1,0:T(8,128)S(1)} %add_add_fusion.1.refs_0_), channel_id=1, source_target_pairs={{0,6},{2,4},{4,2},{6,0},{1,7},{3,5},{5,3},{7,1},{8,14},{10,12},{12... | collective-permute-start | bytes 294920 | tf_op jit(solution)/shard_map/ppermute | solution.py:371
  65.3 5.1 %collective-permute-done.23 = f32[256,256]{1,0:T(8,128)S(1)} collective-permute-done((f32[256,256]{1,0:T(8,128)S(1)}, f32[256,256]{1,0:T(8,128)S(1)}, u32[]{:S(2)}, u32[]{:S(2)}) %collective-permute-start.23) | collective-permute-done | bytes 262176 | tf_op jit(solution)/shard_map/ppermute | solution.py:371
  75.0 3.5 %collective-permute-start.26 = (f32[256,256]{1,0:T(8,128)S(1)}, f32[256,256]{1,0:T(8,128)S(1)}, u32[]{:S(2)}, u32[]{:S(2)}) collective-permute-start(f32[256,256]{1,0:T(8,128)S(1)} %fusion.59), channel_id=1, source_target_pairs={{0,24},{8,0},{16,8},{24,16},{1,25},{9,1},{17,9},{25,17},{2,26},{10... | collective-permute-start | bytes 786440 | tf_op jit(solution)/shard_map/ppermute | solution.py:366
  78.6 30.0 %inverse_and_solve.1 = (f32[512,512]{1,0:T(8,128)S(1)}, f32[512,512]{1,0:T(8,128)S(1)}, f32[32,512]{1,0:T(8,128)S(1)}) custom-call(s32[2]{0:T(128)S(1)} %pad_add_fusion.place_ref, f32[192,128]{1,0:T(8,128)S(1)} %add_add_fusion.1.refs_0_, f32[192,128]{1,0:T(8,128)S(1)} %collective-permute-done.19.refs_1_, f32[192,128]{1,0:T(8,128)S(1)} %collective-permute-done.20.refs_2_, ...), custom_call_target="tpu_custom_call" | custom-call | flops 30000001024 | bytes 1048576 | tf_op jit(solution)/shard_map/inverse_and_solve/pallas_call | solution.py:352
  108.8 1.5 %collective-permute-done.31.other_ref = f32[256,256]{1,0:T(8,128)S(1)} collective-permute-done((f32[256,256]{1,0:T(8,128)S(1)}, f32[256,256]{1,0:T(8,128)S(1)}, u32[]{:S(2)}, u32[]{:S(2)}) %collective-permute-start.31) | collective-permute-done | bytes 262176 | tf_op jit(solution)/shard_map/ppermute | solution.py:371
  110.3 1.3 image.1
  111.6 1.8 %collective-permute-start.32 = (f32[200,128]{1,0:T(8,128)S(1)}, f32[200,128]{1,0:T(8,128)S(1)}, u32[]{:S(2)}, u32[]{:S(2)}) collective-permute-start(f32[200,128]{1,0:T(8,128)S(1)} %get-tuple-element.64), channel_id=1, source_target_pairs={{0,2},{2,0},{4,6},{6,4},{1,3},{3,1},{5,7},{7,5},{8,10},{10,8},{12,... | collective-permute-start | bytes 307208 | tf_op jit(solution)/shard_map/ppermute | solution.py:371
  113.8 1.3 collective-permute-start.34
  115.1 1.9 %fusion.61 = f32[512,512]{1,0:T(8,128)S(1)} fusion(f32[512,512]{1,0:T(8,128)S(1)} %get-tuple-element.67, f32[512,512]{1,0:T(8,128)S(1)} %get-tuple-element.68), kind=kOutput, calls=%fused_computation.144 | convolution fusion | flops 1610612736 | bytes 3145728 | tf_op jit(solution)/shard_map/dot_general | solution.py:20
  117.0 1.9 %convolution_subtract_fusion = bf16[512,512]{1,0:T(8,128)(2,1)S(1)} fusion(f32[512,512]{1,0:T(8,128)S(1)} %get-tuple-element.68, f32[512,512]{1,0:T(8,128)S(1)} %get-tuple-element.69, f32[512,512]{1,0:T(8,128)S(1)} %fusion.61), kind=kOutput, calls=%fused_computation.10 | convolution fusion | flops 1611137024 | bytes 3670016 | tf_op jit(solution)/shard_map/dot_general | solution.py:20
  122.7 3.4 %collective-permute-start.37 = (f32[200,128]{1,0:T(8,128)S(1)}, f32[200,128]{1,0:T(8,128)S(1)}, u32[]{:S(2)}, u32[]{:S(2)}) collective-permute-start(f32[200,128]{1,0:T(8,128)S(1)} %get-tuple-element.89), channel_id=1, source_target_pairs={{0,24},{8,16},{16,8},{24,0},{1,25},{9,17},{17,9},{25,1},{2,26},{10... | collective-permute-start | bytes 307208 | tf_op jit(solution)/shard_map/ppermute | solution.py:371
  128.2 1.7 %collective-permute-done.37 = f32[200,128]{1,0:T(8,128)S(1)} collective-permute-done((f32[200,128]{1,0:T(8,128)S(1)}, f32[200,128]{1,0:T(8,128)S(1)}, u32[]{:S(2)}, u32[]{:S(2)}) %collective-permute-start.37) | collective-permute-done | bytes 102432 | tf_op jit(solution)/shard_map/ppermute | solution.py:371
  131.4 11.9 %all_to_all.6 = f32[16,8,128]{2,1,0:T(8,128)S(1)} all-to-all(f32[16,8,128]{2,1,0:T(8,128)S(1)} %broadcast_in_dim.14), channel_id=1, replica_groups=mesh['blk'=4,'leaf'=4,'samp'=2] {'blk','leaf'}, dimensions={0} | all-to-all | bytes 131072 | tf_op jit(solution)/shard_map/all_to_all | solution.py:383
  (147 shorter events, 34.0 us)
Async XLA Ops:
  2.4 12.6 %collective-permute-start.3 = (f32[8,256]{1,0:T(8,128)}, f32[8,256]{1,0:T(8,128)S(1)}, u32[]{:S(2)}, u32[]{:S(2)}) collective-permute-start(f32[8,256]{1,0:T(8,128)} %get-tuple-element.38), channel_id=1, source_target_pairs={{0,24},{8,0},{16,8},{24,16},{1,25},{9,1},{17,9},{25,17},{2,26},{10... | collective-permute-start | bytes 24584 | tf_op jit(solution)/shard_map/ppermute | solution.py:366
  7.5 9.1 %collective-permute-start.4 = (f32[8,256]{1,0:T(8,128)}, f32[8,256]{1,0:T(8,128)S(1)}, u32[]{:S(2)}, u32[]{:S(2)}) collective-permute-start(f32[8,256]{1,0:T(8,128)} %get-tuple-element.38), channel_id=1, source_target_pairs={{0,8},{8,16},{16,24},{24,0},{1,9},{9,17},{17,25},{25,1},{2,10},{10... | collective-permute-start | bytes 24584 | tf_op jit(solution)/shard_map/ppermute | solution.py:366
  7.5 10.9 %collective-permute-start = (f32[168,256]{1,0:T(8,128)}, f32[168,256]{1,0:T(8,128)S(1)}, u32[]{:S(2)}, u32[]{:S(2)}) collective-permute-start(f32[168,256]{1,0:T(8,128)} %get-tuple-element.36), channel_id=1, source_target_pairs={{0,2},{2,0},{4,6},{6,4},{1,3},{3,1},{5,7},{7,5},{8,10},{10,8},{12,... | collective-permute-start | bytes 516104 | tf_op jit(solution)/shard_map/ppermute | solution.py:371
  9.0 10.0 %collective-permute-start.1 = (f32[168,256]{1,0:T(8,128)}, f32[168,256]{1,0:T(8,128)S(1)}, u32[]{:S(2)}, u32[]{:S(2)}) collective-permute-start(f32[168,256]{1,0:T(8,128)} %get-tuple-element.36), channel_id=1, source_target_pairs={{0,4},{2,6},{4,0},{6,2},{1,5},{3,7},{5,1},{7,3},{8,12},{10,14},{12... | collective-permute-start | bytes 516104 | tf_op jit(solution)/shard_map/ppermute | solution.py:371
  10.5 8.5 %collective-permute-start.2 = (f32[168,256]{1,0:T(8,128)}, f32[168,256]{1,0:T(8,128)S(1)}, u32[]{:S(2)}, u32[]{:S(2)}) collective-permute-start(f32[168,256]{1,0:T(8,128)} %get-tuple-element.36), channel_id=1, source_target_pairs={{0,6},{2,4},{4,2},{6,0},{1,7},{3,5},{5,3},{7,1},{8,14},{10,12},{12... | collective-permute-start | bytes 516104 | tf_op jit(solution)/shard_map/ppermute | solution.py:371
  15.0 12.1 %collective-permute-start.7 = (f32[128,256]{1,0:T(8,128)}, f32[128,256]{1,0:T(8,128)S(1)}, u32[]{:S(2)}, u32[]{:S(2)}) collective-permute-start(f32[128,256]{1,0:T(8,128)} %get-tuple-element.39), channel_id=1, source_target_pairs={{0,2},{2,0},{4,6},{6,4},{1,3},{3,1},{5,7},{7,5},{8,10},{10,8},{12,... | collective-permute-start | bytes 393224 | tf_op jit(solution)/shard_map/ppermute | solution.py:371
  16.6 10.5 %collective-permute-start.8 = (f32[128,256]{1,0:T(8,128)}, f32[128,256]{1,0:T(8,128)S(1)}, u32[]{:S(2)}, u32[]{:S(2)}) collective-permute-start(f32[128,256]{1,0:T(8,128)} %get-tuple-element.39), channel_id=1, source_target_pairs={{0,4},{2,6},{4,0},{6,2},{1,5},{3,7},{5,1},{7,3},{8,12},{10,14},{12... | collective-permute-start | bytes 393224 | tf_op jit(solution)/shard_map/ppermute | solution.py:371
  18.5 8.7 %collective-permute-start.9 = (f32[128,256]{1,0:T(8,128)}, f32[128,256]{1,0:T(8,128)S(1)}, u32[]{:S(2)}, u32[]{:S(2)}) collective-permute-start(f32[128,256]{1,0:T(8,128)} %get-tuple-element.39), channel_id=1, source_target_pairs={{0,6},{2,4},{4,2},{6,0},{1,7},{3,5},{5,3},{7,1},{8,14},{10,12},{12... | collective-permute-start | bytes 393224 | tf_op jit(solution)/shard_map/ppermute | solution.py:371
  21.5 17.1 %collective-permute-start.6 = (f32[160,256]{1,0:T(8,128)S(1)}, f32[160,256]{1,0:T(8,128)S(1)}, u32[]{:S(2)}, u32[]{:S(2)}) collective-permute-start(f32[160,256]{1,0:T(8,128)S(1)} %fusion.25), channel_id=1, source_target_pairs={{0,24},{8,0},{16,8},{24,16},{1,25},{9,1},{17,9},{25,17},{2,26},{10... | collective-permute-start | bytes 491528 | tf_op jit(solution)/shard_map/ppermute | solution.py:366
  27.0 11.5 %collective-permute-start.5 = (f32[160,256]{1,0:T(8,128)S(1)}, f32[160,256]{1,0:T(8,128)S(1)}, u32[]{:S(2)}, u32[]{:S(2)}) collective-permute-start(f32[160,256]{1,0:T(8,128)S(1)} %fusion.26), channel_id=1, source_target_pairs={{0,8},{8,16},{16,24},{24,0},{1,9},{9,17},{17,25},{25,1},{2,10},{10... | collective-permute-start | bytes 491528 | tf_op jit(solution)/shard_map/ppermute | solution.py:366
  28.5 8.2 %collective-permute-start.10 = (f32[128,256]{1,0:T(8,128)S(1)}, f32[128,256]{1,0:T(8,128)S(1)}, u32[]{:S(2)}, u32[]{:S(2)}) collective-permute-start(f32[128,256]{1,0:T(8,128)S(1)} %fusion.56), channel_id=1, source_target_pairs={{0,8},{8,16},{16,24},{24,0},{1,9},{9,17},{17,25},{25,1},{2,10},{10... | collective-permute-start | bytes 393224 | tf_op jit(solution)/shard_map/ppermute | solution.py:366
  28.6 9.3 %collective-permute-start.11 = (f32[128,256]{1,0:T(8,128)S(1)}, f32[128,256]{1,0:T(8,128)S(1)}, u32[]{:S(2)}, u32[]{:S(2)}) collective-permute-start(f32[128,256]{1,0:T(8,128)S(1)} %fusion.57), channel_id=1, source_target_pairs={{0,24},{8,0},{16,8},{24,16},{1,25},{9,1},{17,9},{25,17},{2,26},{10... | collective-permute-start | bytes 393224 | tf_op jit(solution)/shard_map/ppermute | solution.py:366
  42.7 5.0 %collective-permute-start.13 = (f32[192,128]{1,0:T(8,128)S(1)}, f32[192,128]{1,0:T(8,128)S(1)}, u32[]{:S(2)}, u32[]{:S(2)}) collective-permute-start(f32[192,128]{1,0:T(8,128)S(1)} %get-tuple-element.48), channel_id=1, source_target_pairs={{0,2},{2,0},{4,6},{6,4},{1,3},{3,1},{5,7},{7,5},{8,10},{10,8},{12,... | collective-permute-start | bytes 294920 | tf_op jit(solution)/shard_map/ppermute | solution.py:371
  44.2 5.2 %collective-permute-start.14 = (f32[192,128]{1,0:T(8,128)S(1)}, f32[192,128]{1,0:T(8,128)S(1)}, u32[]{:S(2)}, u32[]{:S(2)}) collective-permute-start(f32[192,128]{1,0:T(8,128)S(1)} %get-tuple-element.49), channel_id=1, source_target_pairs={{0,4},{2,6},{4,0},{6,2},{1,5},{3,7},{5,1},{7,3},{8,12},{10,14},{12... | collective-permute-start | bytes 294920 | tf_op jit(solution)/shard_map/ppermute | solution.py:371
  45.7 6.6 %collective-permute-start.15 = (f32[192,128]{1,0:T(8,128)S(1)}, f32[192,128]{1,0:T(8,128)S(1)}, u32[]{:S(2)}, u32[]{:S(2)}) collective-permute-start(f32[192,128]{1,0:T(8,128)S(1)} %get-tuple-element.50), channel_id=1, source_target_pairs={{0,6},{2,4},{4,2},{6,0},{1,7},{3,5},{5,3},{7,1},{8,14},{10,12},{12... | collective-permute-start | bytes 294920 | tf_op jit(solution)/shard_map/ppermute | solution.py:371
  46.2 17.1 %collective-permute-start.22 = (f32[256,256]{1,0:T(8,128)S(1)}, f32[256,256]{1,0:T(8,128)S(1)}, u32[]{:S(2)}, u32[]{:S(2)}) collective-permute-start(f32[256,256]{1,0:T(8,128)S(1)} %get-tuple-element.51.own_ref), channel_id=1, source_target_pairs={{0,2},{2,0},{4,6},{6,4},{1,3},{3,1},{5,7},{7,5},{8,10},{10,8},{12,... | collective-permute-start | bytes 786440 | tf_op jit(solution)/shard_map/ppermute | solution.py:371
  52.3 5.3 %collective-permute-start.16 = (f32[192,128]{1,0:T(8,128)S(1)}, f32[192,128]{1,0:T(8,128)S(1)}, u32[]{:S(2)}, u32[]{:S(2)}) collective-permute-start(f32[192,128]{1,0:T(8,128)S(1)} %add_add_fusion.2), channel_id=1, source_target_pairs={{0,8},{8,0},{16,24},{24,16},{1,9},{9,1},{17,25},{25,17},{2,10},{10... | collective-permute-start | bytes 294920 | tf_op jit(solution)/shard_map/ppermute | solution.py:371
  53.1 7.0 %collective-permute-start.17 = (f32[192,128]{1,0:T(8,128)S(1)}, f32[192,128]{1,0:T(8,128)S(1)}, u32[]{:S(2)}, u32[]{:S(2)}) collective-permute-start(f32[192,128]{1,0:T(8,128)S(1)} %add_add_fusion.2), channel_id=1, source_target_pairs={{0,16},{8,24},{16,0},{24,8},{1,17},{9,25},{17,1},{25,9},{2,18},{10... | collective-permute-start | bytes 294920 | tf_op jit(solution)/shard_map/ppermute | solution.py:371
  55.1 6.5 %collective-permute-start.18 = (f32[192,128]{1,0:T(8,128)S(1)}, f32[192,128]{1,0:T(8,128)S(1)}, u32[]{:S(2)}, u32[]{:S(2)}) collective-permute-start(f32[192,128]{1,0:T(8,128)S(1)} %add_add_fusion.2), channel_id=1, source_target_pairs={{0,24},{8,16},{16,8},{24,0},{1,25},{9,17},{17,9},{25,1},{2,26},{10... | collective-permute-start | bytes 294920 | tf_op jit(solution)/shard_map/ppermute | solution.py:371
  56.8 13.6 %collective-permute-start.23 = (f32[256,256]{1,0:T(8,128)S(1)}, f32[256,256]{1,0:T(8,128)S(1)}, u32[]{:S(2)}, u32[]{:S(2)}) collective-permute-start(f32[256,256]{1,0:T(8,128)S(1)} %get-tuple-element.51.own_ref), channel_id=1, source_target_pairs={{0,4},{2,6},{4,0},{6,2},{1,5},{3,7},{5,1},{7,3},{8,12},{10,14},{12... | collective-permute-start | bytes 786440 | tf_op jit(solution)/shard_map/ppermute | solution.py:371
  57.6 12.8 %collective-permute-start.24 = (f32[256,256]{1,0:T(8,128)S(1)}, f32[256,256]{1,0:T(8,128)S(1)}, u32[]{:S(2)}, u32[]{:S(2)}) collective-permute-start(f32[256,256]{1,0:T(8,128)S(1)} %get-tuple-element.51.own_ref), channel_id=1, source_target_pairs={{0,6},{2,4},{4,2},{6,0},{1,7},{3,5},{5,3},{7,1},{8,14},{10,12},{12... | collective-permute-start | bytes 786440 | tf_op jit(solution)/shard_map/ppermute | solution.py:371
  61.7 11.9 %collective-permute-start.19 = (f32[192,128]{1,0:T(8,128)S(1)}, f32[192,128]{1,0:T(8,128)S(1)}, u32[]{:S(2)}, u32[]{:S(2)}) collective-permute-start(f32[192,128]{1,0:T(8,128)S(1)} %add_add_fusion.1.refs_0_), channel_id=1, source_target_pairs={{0,2},{2,0},{4,6},{6,4},{1,3},{3,1},{5,7},{7,5},{8,10},{10,8},{12,... | collective-permute-start | bytes 294920 | tf_op jit(solution)/shard_map/ppermute | solution.py:371
  62.9 10.7 %collective-permute-start.20 = (f32[192,128]{1,0:T(8,128)S(1)}, f32[192,128]{1,0:T(8,128)S(1)}, u32[]{:S(2)}, u32[]{:S(2)}) collective-permute-start(f32[192,128]{1,0:T(8,128)S(1)} %add_add_fusion.1.refs_0_), channel_id=1, source_target_pairs={{0,4},{2,6},{4,0},{6,2},{1,5},{3,7},{5,1},{7,3},{8,12},{10,14},{12... | collective-permute-start | bytes 294920 | tf_op jit(solution)/shard_map/ppermute | solution.py:371
  63.3 10.3 %collective-permute-start.21 = (f32[192,128]{1,0:T(8,128)S(1)}, f32[192,128]{1,0:T(8,128)S(1)}, u32[]{:S(2)}, u32[]{:S(2)}) collective-permute-start(f32[192,128]{1,0:T(8,128)S(1)} %add_add_fusion.1.refs_0_), channel_id=1, source_target_pairs={{0,6},{2,4},{4,2},{6,0},{1,7},{3,5},{5,3},{7,1},{8,14},{10,12},{12... | collective-permute-start | bytes 294920 | tf_op jit(solution)/shard_map/ppermute | solution.py:371
  74.7 33.9 %collective-permute-start.25 = (f32[256,256]{1,0:T(8,128)S(1)}, f32[256,256]{1,0:T(8,128)S(1)}, u32[]{:S(2)}, u32[]{:S(2)}) collective-permute-start(f32[256,256]{1,0:T(8,128)S(1)} %fusion.58), channel_id=1, source_target_pairs={{0,8},{8,16},{16,24},{24,0},{1,9},{9,17},{17,25},{25,1},{2,10},{10... | collective-permute-start | bytes 786440 | tf_op jit(solution)/shard_map/ppermute | solution.py:366
  75.0 33.6 %collective-permute-start.26 = (f32[256,256]{1,0:T(8,128)S(1)}, f32[256,256]{1,0:T(8,128)S(1)}, u32[]{:S(2)}, u32[]{:S(2)}) collective-permute-start(f32[256,256]{1,0:T(8,128)S(1)} %fusion.59), channel_id=1, source_target_pairs={{0,24},{8,0},{16,8},{24,16},{1,25},{9,1},{17,9},{25,17},{2,26},{10... | collective-permute-start | bytes 786440 | tf_op jit(solution)/shard_map/ppermute | solution.py:366
  111.6 7.3 %collective-permute-start.32 = (f32[200,128]{1,0:T(8,128)S(1)}, f32[200,128]{1,0:T(8,128)S(1)}, u32[]{:S(2)}, u32[]{:S(2)}) collective-permute-start(f32[200,128]{1,0:T(8,128)S(1)} %get-tuple-element.64), channel_id=1, source_target_pairs={{0,2},{2,0},{4,6},{6,4},{1,3},{3,1},{5,7},{7,5},{8,10},{10,8},{12,... | collective-permute-start | bytes 307208 | tf_op jit(solution)/shard_map/ppermute | solution.py:371
  113.4 6.8 %collective-permute-start.33 = (f32[200,128]{1,0:T(8,128)S(1)}, f32[200,128]{1,0:T(8,128)S(1)}, u32[]{:S(2)}, u32[]{:S(2)}) collective-permute-start(f32[200,128]{1,0:T(8,128)S(1)} %get-tuple-element.64), channel_id=1, source_target_pairs={{0,4},{2,6},{4,0},{6,2},{1,5},{3,7},{5,1},{7,3},{8,12},{10,14},{12... | collective-permute-start | bytes 307208 | tf_op jit(solution)/shard_map/ppermute | solution.py:371
  113.8 6.4 %collective-permute-start.34 = (f32[200,128]{1,0:T(8,128)S(1)}, f32[200,128]{1,0:T(8,128)S(1)}, u32[]{:S(2)}, u32[]{:S(2)}) collective-permute-start(f32[200,128]{1,0:T(8,128)S(1)} %get-tuple-element.64), channel_id=1, source_target_pairs={{0,6},{2,4},{4,2},{6,0},{1,7},{3,5},{5,3},{7,1},{8,14},{10,12},{12... | collective-permute-start | bytes 307208 | tf_op jit(solution)/shard_map/ppermute | solution.py:371
  121.5 6.2 %collective-permute-start.36 = (f32[136,128]{1,0:T(8,128)S(1)}, f32[136,128]{1,0:T(8,128)S(1)}, u32[]{:S(2)}, u32[]{:S(2)}) collective-permute-start(f32[136,128]{1,0:T(8,128)S(1)} %fusion.30), channel_id=1, source_target_pairs={{0,16},{8,24},{16,0},{24,8},{1,17},{9,25},{17,1},{25,9},{2,18},{10... | collective-permute-start | bytes 208904 | tf_op jit(solution)/shard_map/ppermute | solution.py:371
  121.6 6.6 %collective-permute-start.35 = (f32[200,128]{1,0:T(8,128)S(1)}, f32[200,128]{1,0:T(8,128)S(1)}, u32[]{:S(2)}, u32[]{:S(2)}) collective-permute-start(f32[200,128]{1,0:T(8,128)S(1)} %get-tuple-element.88), channel_id=1, source_target_pairs={{0,8},{8,0},{16,24},{24,16},{1,9},{9,1},{17,25},{25,17},{2,10},{10... | collective-permute-start | bytes 307208 | tf_op jit(solution)/shard_map/ppermute | solution.py:371
  122.7 7.2 %collective-permute-start.37 = (f32[200,128]{1,0:T(8,128)S(1)}, f32[200,128]{1,0:T(8,128)S(1)}, u32[]{:S(2)}, u32[]{:S(2)}) collective-permute-start(f32[200,128]{1,0:T(8,128)S(1)} %get-tuple-element.89), channel_id=1, source_target_pairs={{0,24},{8,16},{16,8},{24,0},{1,25},{9,17},{17,9},{25,1},{2,26},{10... | collective-permute-start | bytes 307208 | tf_op jit(solution)/shard_map/ppermute | solution.py:371
  (14 other events, 182.0 us)

commit v3 on v2

--- a/solution.py
+++ b/solution.py
@@ -259,7 +259,7 @@
 
 
 def prepare_kernel(
-    core_ref, points_ref, neighbors_ref, omega_ref, observed_ref, prior_ref, first_ref, second_ref, meta_ref,
+    core_ref, points_ref, neighbors_ref, omega_ref, observed_ref, prior_ref, first_ref, second_ref, meta_ref, own_ref, rhs_ref,
     points_vmem, neighbors_vmem, observed_vmem, prior_vmem, sems,
 ):
     split = second_ref.shape[0]
@@ -283,7 +283,10 @@
     meta_ref[...] = jnp.full(meta_ref.shape, -1.0, jnp.float32)
     for copy in copies:
         copy.wait()
-    first_ref[split : split + samples, :] = observed_vmem[...] - prior_vmem[...]
+    own_ref[0:split, :] = first_ref[0:split, :]
+    own_ref[split:, :] = second_ref[...]
+    rhs_ref[...] = observed_vmem[...] - prior_vmem[...]
+    first_ref[split : split + samples, :] = rhs_ref[...]
     meta_ref[0:3, :] = points_vmem[...]
     meta_ref[3:4, : neighbors_vmem.shape[1]] = neighbors_vmem[...].astype(jnp.float32)
     first_ref[split + samples :, :] = meta_ref[...]
@@ -294,12 +297,12 @@
     samples = prior.shape[0]
     vmem = pl.BlockSpec(memory_space=pltpu.VMEM)
     hbm = pl.BlockSpec(memory_space=pl.ANY)
-    shapes = [(split + samples + 8, width), (split, width), (8, width)]
+    shapes = [(split + samples + 8, width), (split, width), (8, width), (2 * split, width), (samples, width)]
     return pl.pallas_call(
         prepare_kernel,
         out_shape=tuple(jax.ShapeDtypeStruct(shape, jnp.float32) for shape in shapes),
         in_specs=[pl.BlockSpec(memory_space=pltpu.SMEM)] + [hbm] * 5,
-        out_specs=(vmem,) * 3,
+        out_specs=(vmem,) * 5,
         scratch_shapes=[
             pltpu.VMEM(points.shape, jnp.float32),
             pltpu.VMEM(neighbors.shape, jnp.int32),
@@ -310,6 +313,18 @@
         name="prepare",
         cost_estimate=pl.CostEstimate(flops=10**6, bytes_accessed=2**19, transcendentals=0),
     )(core, points, neighbors, omega, observed, prior)
+
+
+def targets_kernel(ids_ref, *refs):
+    count = len(refs) // 3
+    width = refs[0].shape[1]
+    for meta_ref, rows_ref, weight_ref in zip(refs[:count], refs[count : 2 * count], refs[2 * count :]):
+        rows_ref[...] = meta_ref[0:3, :]
+        listed = meta_ref[3:4, :]
+        for m in range(weight_ref.shape[1] // width):
+            same = listed == jnp.zeros((1, width), jnp.float32) + ids_ref[m].astype(jnp.float32)
+            found = jnp.sum(jnp.where(same, 1.0, 0.0), axis=1, keepdims=True)
+            weight_ref[:, m * width : (m + 1) * width] = jnp.broadcast_to(found, (1, width))
 
 
 def payload_kernel(place_ref, omega_ref, own_ref, other_ref, rhs_ref, sketch_ref, *refs):
@@ -421,7 +436,7 @@
     core = own_core.astype(jnp.int32).reshape(1)
     place = jnp.stack([own_core, own_leaf]).astype(jnp.int32)
     split = half // 2
-    first_block, second_block, meta = prepare(
+    first_block, second_block, meta, omega_half, rhs = prepare(
         core, points, neighbors, omega, observed[None, :], prior_draws, split
     )
 
@@ -432,16 +447,29 @@
         return shifted(upward, "blk", 1), shifted(downward, "blk", -1)
 
     first_blocks, second_blocks = slab(first_block), slab(second_block)
-    above, below = shifted(meta, "blk", -1), shifted(meta, "blk", 1)
+    route = [
+        (b * cores + c, (b + (1 if c == 0 else -1)) % cycle * cores + c) for b in range(cycle) for c in range(cores)
+    ]
+    arrived = lax.ppermute(meta, ("blk", "samp"), route)
+    swapped_meta = other_core(arrived)
+    above = jnp.where(own_core == 0, swapped_meta, arrived)
+    below = jnp.where(own_core == 0, arrived, swapped_meta)
     begin = split + samples
     sources = jnp.concatenate([b[begin : begin + 3] for b in first_blocks], axis=1)
-    targets = [above, meta, below]
-    source_ids = own_slab * leaves + jnp.stack([own_leaf ^ m for m in range(leaves)])
-    target_lists = jnp.stack([t[3, : neighbors.shape[1]] for t in targets])
-    usable = (target_lists[None] == source_ids[:, None, None].astype(jnp.float32)).astype(jnp.float32).sum(axis=2)
+    source_ids = (own_slab * leaves + jnp.stack([own_leaf ^ m for m in range(leaves)])).astype(jnp.int32)
+    tables = kernel_call(
+        targets_kernel,
+        "targets",
+        [(3, width)] * 3 + [(1, leaves * width)] * 3,
+        source_ids,
+        above,
+        meta,
+        below,
+    )
+    targets, weights = tables[:3], tables[3:]
 
     def kernel_columns(index):
-        offset = sources[:, :, None] - targets[index][:3, None, :]
+        offset = sources[:, :, None] - targets[index][:, None, :]
         along = offset[0]
         along = jnp.where(along >= 0.5 * period, along - period, along)
         along = jnp.where(along < -0.5 * period, along + period, along)
@@ -450,8 +478,7 @@
         remain = jnp.maximum(1.0 - radius, 0.0)
         squared_remain = remain * remain
         values = squared_remain * squared_remain * (4.0 * radius + 1.0)
-        weight = jnp.repeat(usable[:, index], width)
-        return values * weight[:, None]
+        return values * weights[index].reshape(-1, 1)
 
     columns = [kernel_columns(i) for i in range(3)]
 
@@ -466,8 +493,6 @@
     upward, downward, gathered = sums(second_blocks)
     from_below, from_above = sent(upward, downward)
     applied_second = mm(gathered, columns[1]) + from_below + from_above
-    rhs = first_block[split:begin]
-    omega_half = jnp.concatenate([first_block[:split], second_block], axis=0)
     sketch_half = jnp.concatenate([applied[:split], applied_second], axis=0) + sketch_shift * omega_half
     image_rhs = applied[split:] + noise_variance * rhs
 

time: 144 us -> 143 us (level)
  starting transfers between devices: 47.8 us -> 45.7 us
  local copies, waits for them, and re-layouts: 4.38 us -> 2.61 us
    ppermute x8 -> x6, starting transfers between devices: 16.7 us -> 10.3 us  [shifted(): lax.ppermute(values, axis, [(i, (i + distance) % size) for i in range(siz...]
    ppermute x0 -> x1, starting transfers between devices: none -> 3.08 us  [local(): arrived = lax.ppermute(meta, ('blk', 'samp'), route)]
    slice x7 -> x0, local copies, waits for them, and re-layouts: 2.31 us -> none  [the longest x1 0.91 us: local(): omega_half = jnp.concatenate([first_block[:split], second_block], axis=0)]
    ppermute x8 -> x6, waiting for transfers between devices: 4.39 us -> 5.75 us  [shifted(): lax.ppermute(values, axis, [(i, (i + distance) % size) for i in range(siz...]
    ppermute x30 -> x31, starting transfers between devices: 31.1 us -> 32.3 us  [swapped(): return lax.ppermute(values, axis, [(i, i ^ mask) for i in range(size)])]
    pallas_call x3 -> x4, Pallas kernels: 33 us -> 33.6 us  [kernel_call(): pl.pallas_call(kernel, out_shape=tuple((jax.ShapeDtypeStruct(shape, jnp.f...]
    ppermute x30 -> x31, waiting for transfers between devices: 20.7 us -> 20.4 us  [swapped(): return lax.ppermute(values, axis, [(i, i ^ mask) for i in range(size)])]
  transfers between devices with their start and end apart: 38 -> 38, of which waited for: 15 -> 14; matrix products, arithmetic and copies ran while one was open for 13% -> 12% of each run, Pallas kernels for 21% -> 22%
where the time goes in v3:
time: 143 us; the launch traced here: 142 us
  starting transfers between devices  45.7 us (32%)
  Pallas kernels  35.5 us (25%)
  waiting for transfers between devices  26.2 us (18%)
  matrix products  14 us (10%)
  blocking collectives  12.3 us (9%)
  other arithmetic  4.57 us (3%)
  local copies, waits for them, and re-layouts  2.61 us (2%)
    pallas_call x4, Pallas kernels, kernel_call(): pl.pallas_call(kernel, out_shape=tuple((jax.ShapeDtypeStruct(shape, jnp.f...  33.6 us
    ppermute x31, starting transfers between devices, swapped(): return lax.ppermute(values, axis, [(i, i ^ mask) for i in range(size)])  32.3 us
    ppermute x31, waiting for transfers between devices, swapped(): return lax.ppermute(values, axis, [(i, i ^ mask) for i in range(size)])  20.4 us
    dot_general x15, matrix products, mm(): jnp.dot(left, right, precision=HIGHEST, preferred_element_type=jnp.float32)  13.6 us
    all_to_all x1, blocking collectives, exchange(): return lax.all_to_all(values, POINT_AXES, 0, 0, tiled=True)  12.3 us
    ppermute x6, starting transfers between devices, shifted(): lax.ppermute(values, axis, [(i, (i + distance) % size) for i in range(siz...  10.3 us
    ppermute x6, waiting for transfers between devices, shifted(): lax.ppermute(values, axis, [(i, (i + distance) % size) for i in range(siz...  5.75 us
    ppermute x1, starting transfers between devices, local(): arrived = lax.ppermute(meta, ('blk', 'samp'), route)  3.08 us
  transfers between devices with their start and end apart: 38, of which 14 were waited for; matrix products, arithmetic and copies ran while one was open for 12% of the time, Pallas kernels for 22%

profile of v3, /device:TPU:0, one launch (start us, length us, event | category | flops | bytes accessed | tf_op | source)
XLA Modules:
  0.0 142.2 jit_solution(3523428393201913961)
XLA Ops:
  0.6 1.9 %prepare.1 = (f32[168,256]{1,0:T(8,128)}, f32[128,256]{1,0:T(8,128)}, f32[8,256]{1,0:T(8,128)}, f32[256,256]{1,0:T(8,128)}, f32[32,256]{1,0:T(8,128)}) custom-call(s32[1]{0:T(128)} %bitcast.core_ref, f32[3,256]{1,0:T(4,128)} %points_ref.1, s32[1,8]{1,0:T(1,128)} %neighbors_ref.1, f32[512,256]{1,0:T(8,128)} %omega_ref.1, f32[1,256]{1,0:T(1,128)} %bitcast.127, ...), custom_call_target="tpu_custom_call" | custom-call | flops 1000000 | bytes 524288 | tf_op jit(solution)/shard_map/prepare/pallas_call | solution.py:301
  2.5 3.1 %collective-permute-start.3 = (f32[8,256]{1,0:T(8,128)}, f32[8,256]{1,0:T(8,128)S(1)}, u32[]{:S(2)}, u32[]{:S(2)}) collective-permute-start(f32[8,256]{1,0:T(8,128)} %get-tuple-element.46.refs_1_), channel_id=1, source_target_pairs={{0,8},{1,25},{8,16},{9,1},{16,24},{17,9},{24,0},{25,17},{2,10},{3,... | collective-permute-start | bytes 24584 | tf_op jit(solution)/shard_map/ppermute | solution.py:453
  5.6 1.5 %collective-permute-start = (f32[168,256]{1,0:T(8,128)}, f32[168,256]{1,0:T(8,128)S(1)}, u32[]{:S(2)}, u32[]{:S(2)}) collective-permute-start(f32[168,256]{1,0:T(8,128)} %get-tuple-element.45), channel_id=1, source_target_pairs={{0,2},{2,0},{4,6},{6,4},{1,3},{3,1},{5,7},{7,5},{8,10},{10,8},{12,... | collective-permute-start | bytes 516104 | tf_op jit(solution)/shard_map/ppermute | solution.py:386
  7.1 1.5 %collective-permute-start.1 = (f32[168,256]{1,0:T(8,128)}, f32[168,256]{1,0:T(8,128)S(1)}, u32[]{:S(2)}, u32[]{:S(2)}) collective-permute-start(f32[168,256]{1,0:T(8,128)} %get-tuple-element.45), channel_id=1, source_target_pairs={{0,4},{2,6},{4,0},{6,2},{1,5},{3,7},{5,1},{7,3},{8,12},{10,14},{12... | collective-permute-start | bytes 516104 | tf_op jit(solution)/shard_map/ppermute | solution.py:386
  9.1 1.5 %collective-permute-start.7 = (f32[128,256]{1,0:T(8,128)}, f32[128,256]{1,0:T(8,128)S(1)}, u32[]{:S(2)}, u32[]{:S(2)}) collective-permute-start(f32[128,256]{1,0:T(8,128)} %get-tuple-element.54), channel_id=1, source_target_pairs={{0,2},{2,0},{4,6},{6,4},{1,3},{3,1},{5,7},{7,5},{8,10},{10,8},{12,... | collective-permute-start | bytes 393224 | tf_op jit(solution)/shard_map/ppermute | solution.py:386
  12.7 1.6 %collective-permute-start.8 = (f32[128,256]{1,0:T(8,128)}, f32[128,256]{1,0:T(8,128)S(1)}, u32[]{:S(2)}, u32[]{:S(2)}) collective-permute-start(f32[128,256]{1,0:T(8,128)} %get-tuple-element.54), channel_id=1, source_target_pairs={{0,4},{2,6},{4,0},{6,2},{1,5},{3,7},{5,1},{7,3},{8,12},{10,14},{12... | collective-permute-start | bytes 393224 | tf_op jit(solution)/shard_map/ppermute | solution.py:386
  16.2 1.2 collective-permute-done.1
  19.9 2.6 %collective-permute-start.6 = (f32[160,256]{1,0:T(8,128)S(1)}, f32[160,256]{1,0:T(8,128)S(1)}, u32[]{:S(2)}, u32[]{:S(2)}) collective-permute-start(f32[160,256]{1,0:T(8,128)S(1)} %fusion.25), channel_id=1, source_target_pairs={{0,24},{8,0},{16,8},{24,16},{1,25},{9,1},{17,9},{25,17},{2,26},{10... | collective-permute-start | bytes 491528 | tf_op jit(solution)/shard_map/ppermute | solution.py:381
  26.5 3.3 %collective-permute-start.11 = (f32[128,256]{1,0:T(8,128)S(1)}, f32[128,256]{1,0:T(8,128)S(1)}, u32[]{:S(2)}, u32[]{:S(2)}) collective-permute-start(f32[128,256]{1,0:T(8,128)S(1)} %fusion.56), channel_id=1, source_target_pairs={{0,24},{8,0},{16,8},{24,16},{1,25},{9,1},{17,9},{25,17},{2,26},{10... | collective-permute-start | bytes 393224 | tf_op jit(solution)/shard_map/ppermute | solution.py:381
  30.7 4.7 %collective-permute-done.10 = f32[128,256]{1,0:T(8,128)S(1)} collective-permute-done((f32[128,256]{1,0:T(8,128)S(1)}, f32[128,256]{1,0:T(8,128)S(1)}, u32[]{:S(2)}, u32[]{:S(2)}) %collective-permute-start.10) | collective-permute-done | bytes 131104 | tf_op jit(solution)/shard_map/ppermute | solution.py:381
  38.1 1.4 %collective-permute-done.12.other_ref = f32[256,256]{1,0:T(8,128)S(1)} collective-permute-done((f32[256,256]{1,0:T(8,128)S(1)}, f32[256,256]{1,0:T(8,128)S(1)}, u32[]{:S(2)}, u32[]{:S(2)}) %collective-permute-start.12) | collective-permute-done | bytes 262176 | tf_op jit(solution)/shard_map/ppermute | solution.py:386
  39.6 1.6 %payload.1 = (f32[512,256]{1,0:T(8,128)S(1)}, f32[192,128]{1,0:T(8,128)S(1)}, f32[192,128]{1,0:T(8,128)S(1)}, f32[192,128]{1,0:T(8,128)S(1)}, f32[192,128]{1,0:T(8,128)S(1)}) custom-call(s32[2]{0:T(128)S(1)} %pad_add_fusion.place_ref, f32[256,256]{1,0:T(8,128)S(1)} %copy-done.1, f32[256,256]{1,0:T(8,128)S(1)} %maximum_add_fusion.own_ref, ...), custom_call_target="tpu_custom_call" | custom-call | flops 1000000000 | bytes 1048576 | tf_op jit(solution)/shard_map/payload/pallas_call | solution.py:367
  43.3 1.4 %collective-permute-start.15 = (f32[192,128]{1,0:T(8,128)S(1)}, f32[192,128]{1,0:T(8,128)S(1)}, u32[]{:S(2)}, u32[]{:S(2)}) collective-permute-start(f32[192,128]{1,0:T(8,128)S(1)} %get-tuple-element.66), channel_id=1, source_target_pairs={{0,6},{2,4},{4,2},{6,0},{1,7},{3,5},{5,3},{7,1},{8,14},{10,12},{12... | collective-permute-start | bytes 294920 | tf_op jit(solution)/shard_map/ppermute | solution.py:386
  47.3 2.7 %collective-permute-done.15 = f32[192,128]{1,0:T(8,128)S(1)} collective-permute-done((f32[192,128]{1,0:T(8,128)S(1)}, f32[192,128]{1,0:T(8,128)S(1)}, u32[]{:S(2)}, u32[]{:S(2)}) %collective-permute-start.15) | collective-permute-done | bytes 98336 | tf_op jit(solution)/shard_map/ppermute | solution.py:386
  50.6 2.2 %collective-permute-start.17 = (f32[192,128]{1,0:T(8,128)S(1)}, f32[192,128]{1,0:T(8,128)S(1)}, u32[]{:S(2)}, u32[]{:S(2)}) collective-permute-start(f32[192,128]{1,0:T(8,128)S(1)} %add_add_fusion.2), channel_id=1, source_target_pairs={{0,16},{8,24},{16,0},{24,8},{1,17},{9,25},{17,1},{25,9},{2,18},{10... | collective-permute-start | bytes 294920 | tf_op jit(solution)/shard_map/ppermute | solution.py:386
  52.8 1.6 %collective-permute-start.18 = (f32[192,128]{1,0:T(8,128)S(1)}, f32[192,128]{1,0:T(8,128)S(1)}, u32[]{:S(2)}, u32[]{:S(2)}) collective-permute-start(f32[192,128]{1,0:T(8,128)S(1)} %add_add_fusion.2), channel_id=1, source_target_pairs={{0,24},{8,16},{16,8},{24,0},{1,25},{9,17},{17,9},{25,1},{2,26},{10... | collective-permute-start | bytes 294920 | tf_op jit(solution)/shard_map/ppermute | solution.py:386
  55.4 2.1 %collective-permute-start.24 = (f32[256,256]{1,0:T(8,128)S(1)}, f32[256,256]{1,0:T(8,128)S(1)}, u32[]{:S(2)}, u32[]{:S(2)}) collective-permute-start(f32[256,256]{1,0:T(8,128)S(1)} %maximum_add_fusion.own_ref), channel_id=1, source_target_pairs={{0,6},{2,4},{4,2},{6,0},{1,7},{3,5},{5,3},{7,1},{8,14},{10,12},{12... | collective-permute-start | bytes 786440 | tf_op jit(solution)/shard_map/ppermute | solution.py:386
  57.5 2.3 %collective-permute-done.17 = f32[192,128]{1,0:T(8,128)S(1)} collective-permute-done((f32[192,128]{1,0:T(8,128)S(1)}, f32[192,128]{1,0:T(8,128)S(1)}, u32[]{:S(2)}, u32[]{:S(2)}) %collective-permute-start.17) | collective-permute-done | bytes 98336 | tf_op jit(solution)/shard_map/ppermute | solution.py:386
  61.5 1.8 %collective-permute-start.21 = (f32[192,128]{1,0:T(8,128)S(1)}, f32[192,128]{1,0:T(8,128)S(1)}, u32[]{:S(2)}, u32[]{:S(2)}) collective-permute-start(f32[192,128]{1,0:T(8,128)S(1)} %add_add_fusion.1.refs_0_), channel_id=1, source_target_pairs={{0,6},{2,4},{4,2},{6,0},{1,7},{3,5},{5,3},{7,1},{8,14},{10,12},{12... | collective-permute-start | bytes 294920 | tf_op jit(solution)/shard_map/ppermute | solution.py:386
  63.4 5.9 %collective-permute-done.23 = f32[256,256]{1,0:T(8,128)S(1)} collective-permute-done((f32[256,256]{1,0:T(8,128)S(1)}, f32[256,256]{1,0:T(8,128)S(1)}, u32[]{:S(2)}, u32[]{:S(2)}) %collective-permute-start.23) | collective-permute-done | bytes 262176 | tf_op jit(solution)/shard_map/ppermute | solution.py:386
  73.9 3.5 %collective-permute-start.26 = (f32[256,256]{1,0:T(8,128)S(1)}, f32[256,256]{1,0:T(8,128)S(1)}, u32[]{:S(2)}, u32[]{:S(2)}) collective-permute-start(f32[256,256]{1,0:T(8,128)S(1)} %fusion.58), channel_id=1, source_target_pairs={{0,24},{8,0},{16,8},{24,16},{1,25},{9,1},{17,9},{25,17},{2,26},{10... | collective-permute-start | bytes 786440 | tf_op jit(solution)/shard_map/ppermute | solution.py:381
  77.4 30.0 %inverse_and_solve.1 = (f32[512,512]{1,0:T(8,128)S(1)}, f32[512,512]{1,0:T(8,128)S(1)}, f32[32,512]{1,0:T(8,128)S(1)}) custom-call(s32[2]{0:T(128)S(1)} %pad_add_fusion.place_ref, f32[192,128]{1,0:T(8,128)S(1)} %add_add_fusion.1.refs_0_, f32[192,128]{1,0:T(8,128)S(1)} %collective-permute-done.19.refs_1_, f32[192,128]{1,0:T(8,128)S(1)} %collective-permute-done.20.refs_2_, ...), custom_call_target="tpu_custom_call" | custom-call | flops 30000001024 | bytes 1048576 | tf_op jit(solution)/shard_map/inverse_and_solve/pallas_call | solution.py:367
  107.6 1.5 %collective-permute-done.31.other_ref = f32[256,256]{1,0:T(8,128)S(1)} collective-permute-done((f32[256,256]{1,0:T(8,128)S(1)}, f32[256,256]{1,0:T(8,128)S(1)}, u32[]{:S(2)}, u32[]{:S(2)}) %collective-permute-start.31) | collective-permute-done | bytes 262176 | tf_op jit(solution)/shard_map/ppermute | solution.py:386
  109.1 1.3 image.1
  111.5 2.5 %collective-permute-start.34 = (f32[200,128]{1,0:T(8,128)S(1)}, f32[200,128]{1,0:T(8,128)S(1)}, u32[]{:S(2)}, u32[]{:S(2)}) collective-permute-start(f32[200,128]{1,0:T(8,128)S(1)} %get-tuple-element.80), channel_id=1, source_target_pairs={{0,6},{2,4},{4,2},{6,0},{1,7},{3,5},{5,3},{7,1},{8,14},{10,12},{12... | collective-permute-start | bytes 307208 | tf_op jit(solution)/shard_map/ppermute | solution.py:386
  114.0 1.9 %fusion.60 = f32[512,512]{1,0:T(8,128)S(1)} fusion(f32[512,512]{1,0:T(8,128)S(1)} %get-tuple-element.83, f32[512,512]{1,0:T(8,128)S(1)} %get-tuple-element.84), kind=kOutput, calls=%fused_computation.136 | convolution fusion | flops 1610612736 | bytes 3145728 | tf_op jit(solution)/shard_map/dot_general | solution.py:20
  115.9 1.9 %convolution_subtract_fusion = bf16[512,512]{1,0:T(8,128)(2,1)S(1)} fusion(f32[512,512]{1,0:T(8,128)S(1)} %get-tuple-element.84, f32[512,512]{1,0:T(8,128)S(1)} %get-tuple-element.85, f32[512,512]{1,0:T(8,128)S(1)} %fusion.60), kind=kOutput, calls=%fused_computation.10 | convolution fusion | flops 1611137024 | bytes 3670016 | tf_op jit(solution)/shard_map/dot_general | solution.py:20
  119.2 1.2 collective-permute-start.35
  120.4 3.2 %collective-permute-start.37 = (f32[200,128]{1,0:T(8,128)S(1)}, f32[200,128]{1,0:T(8,128)S(1)}, u32[]{:S(2)}, u32[]{:S(2)}) collective-permute-start(f32[200,128]{1,0:T(8,128)S(1)} %get-tuple-element.101), channel_id=1, source_target_pairs={{0,24},{8,16},{16,8},{24,0},{1,25},{9,17},{17,9},{25,1},{2,26},{10... | collective-permute-start | bytes 307208 | tf_op jit(solution)/shard_map/ppermute | solution.py:386
  124.4 1.6 %collective-permute-done.35 = f32[200,128]{1,0:T(8,128)S(1)} collective-permute-done((f32[200,128]{1,0:T(8,128)S(1)}, f32[200,128]{1,0:T(8,128)S(1)}, u32[]{:S(2)}, u32[]{:S(2)}) %collective-permute-start.35) | collective-permute-done | bytes 102432 | tf_op jit(solution)/shard_map/ppermute | solution.py:386
  126.0 1.7 %collective-permute-done.37 = f32[200,128]{1,0:T(8,128)S(1)} collective-permute-done((f32[200,128]{1,0:T(8,128)S(1)}, f32[200,128]{1,0:T(8,128)S(1)}, u32[]{:S(2)}, u32[]{:S(2)}) %collective-permute-start.37) | collective-permute-done | bytes 102432 | tf_op jit(solution)/shard_map/ppermute | solution.py:386
  129.2 12.3 %all_to_all.6 = f32[16,8,128]{2,1,0:T(8,128)S(1)} all-to-all(f32[16,8,128]{2,1,0:T(8,128)S(1)} %broadcast_in_dim.5), channel_id=1, replica_groups=mesh['blk'=4,'leaf'=4,'samp'=2] {'blk','leaf'}, dimensions={0} | all-to-all | bytes 131072 | tf_op jit(solution)/shard_map/all_to_all | solution.py:398
  (137 shorter events, 32.4 us)
Async XLA Ops:
  2.5 8.1 %collective-permute-start.3 = (f32[8,256]{1,0:T(8,128)}, f32[8,256]{1,0:T(8,128)S(1)}, u32[]{:S(2)}, u32[]{:S(2)}) collective-permute-start(f32[8,256]{1,0:T(8,128)} %get-tuple-element.46.refs_1_), channel_id=1, source_target_pairs={{0,8},{1,25},{8,16},{9,1},{16,24},{17,9},{24,0},{25,17},{2,10},{3,... | collective-permute-start | bytes 24584 | tf_op jit(solution)/shard_map/ppermute | solution.py:453
  5.6 10.1 %collective-permute-start = (f32[168,256]{1,0:T(8,128)}, f32[168,256]{1,0:T(8,128)S(1)}, u32[]{:S(2)}, u32[]{:S(2)}) collective-permute-start(f32[168,256]{1,0:T(8,128)} %get-tuple-element.45), channel_id=1, source_target_pairs={{0,2},{2,0},{4,6},{6,4},{1,3},{3,1},{5,7},{7,5},{8,10},{10,8},{12,... | collective-permute-start | bytes 516104 | tf_op jit(solution)/shard_map/ppermute | solution.py:386
  7.1 10.4 %collective-permute-start.1 = (f32[168,256]{1,0:T(8,128)}, f32[168,256]{1,0:T(8,128)S(1)}, u32[]{:S(2)}, u32[]{:S(2)}) collective-permute-start(f32[168,256]{1,0:T(8,128)} %get-tuple-element.45), channel_id=1, source_target_pairs={{0,4},{2,6},{4,0},{6,2},{1,5},{3,7},{5,1},{7,3},{8,12},{10,14},{12... | collective-permute-start | bytes 516104 | tf_op jit(solution)/shard_map/ppermute | solution.py:386
  8.6 8.9 %collective-permute-start.2 = (f32[168,256]{1,0:T(8,128)}, f32[168,256]{1,0:T(8,128)S(1)}, u32[]{:S(2)}, u32[]{:S(2)}) collective-permute-start(f32[168,256]{1,0:T(8,128)} %get-tuple-element.45), channel_id=1, source_target_pairs={{0,6},{2,4},{4,2},{6,0},{1,7},{3,5},{5,3},{7,1},{8,14},{10,12},{12... | collective-permute-start | bytes 516104 | tf_op jit(solution)/shard_map/ppermute | solution.py:386
  9.1 15.2 %collective-permute-start.7 = (f32[128,256]{1,0:T(8,128)}, f32[128,256]{1,0:T(8,128)S(1)}, u32[]{:S(2)}, u32[]{:S(2)}) collective-permute-start(f32[128,256]{1,0:T(8,128)} %get-tuple-element.54), channel_id=1, source_target_pairs={{0,2},{2,0},{4,6},{6,4},{1,3},{3,1},{5,7},{7,5},{8,10},{10,8},{12,... | collective-permute-start | bytes 393224 | tf_op jit(solution)/shard_map/ppermute | solution.py:386
  12.7 11.5 %collective-permute-start.8 = (f32[128,256]{1,0:T(8,128)}, f32[128,256]{1,0:T(8,128)S(1)}, u32[]{:S(2)}, u32[]{:S(2)}) collective-permute-start(f32[128,256]{1,0:T(8,128)} %get-tuple-element.54), channel_id=1, source_target_pairs={{0,4},{2,6},{4,0},{6,2},{1,5},{3,7},{5,1},{7,3},{8,12},{10,14},{12... | collective-permute-start | bytes 393224 | tf_op jit(solution)/shard_map/ppermute | solution.py:386
  15.7 8.6 %collective-permute-start.9 = (f32[128,256]{1,0:T(8,128)}, f32[128,256]{1,0:T(8,128)S(1)}, u32[]{:S(2)}, u32[]{:S(2)}) collective-permute-start(f32[128,256]{1,0:T(8,128)} %get-tuple-element.54), channel_id=1, source_target_pairs={{0,6},{2,4},{4,2},{6,0},{1,7},{3,5},{5,3},{7,1},{8,14},{10,12},{12... | collective-permute-start | bytes 393224 | tf_op jit(solution)/shard_map/ppermute | solution.py:386
  19.9 17.2 %collective-permute-start.6 = (f32[160,256]{1,0:T(8,128)S(1)}, f32[160,256]{1,0:T(8,128)S(1)}, u32[]{:S(2)}, u32[]{:S(2)}) collective-permute-start(f32[160,256]{1,0:T(8,128)S(1)} %fusion.25), channel_id=1, source_target_pairs={{0,24},{8,0},{16,8},{24,16},{1,25},{9,1},{17,9},{25,17},{2,26},{10... | collective-permute-start | bytes 491528 | tf_op jit(solution)/shard_map/ppermute | solution.py:381
  24.2 12.9 %collective-permute-start.5 = (f32[160,256]{1,0:T(8,128)S(1)}, f32[160,256]{1,0:T(8,128)S(1)}, u32[]{:S(2)}, u32[]{:S(2)}) collective-permute-start(f32[160,256]{1,0:T(8,128)S(1)} %fusion.26), channel_id=1, source_target_pairs={{0,8},{8,16},{16,24},{24,0},{1,9},{9,17},{17,25},{25,1},{2,10},{10... | collective-permute-start | bytes 491528 | tf_op jit(solution)/shard_map/ppermute | solution.py:381
  25.7 9.7 %collective-permute-start.10 = (f32[128,256]{1,0:T(8,128)S(1)}, f32[128,256]{1,0:T(8,128)S(1)}, u32[]{:S(2)}, u32[]{:S(2)}) collective-permute-start(f32[128,256]{1,0:T(8,128)S(1)} %fusion.55), channel_id=1, source_target_pairs={{0,8},{8,16},{16,24},{24,0},{1,9},{9,17},{17,25},{25,1},{2,10},{10... | collective-permute-start | bytes 393224 | tf_op jit(solution)/shard_map/ppermute | solution.py:381
  26.5 10.0 %collective-permute-start.11 = (f32[128,256]{1,0:T(8,128)S(1)}, f32[128,256]{1,0:T(8,128)S(1)}, u32[]{:S(2)}, u32[]{:S(2)}) collective-permute-start(f32[128,256]{1,0:T(8,128)S(1)} %fusion.56), channel_id=1, source_target_pairs={{0,24},{8,0},{16,8},{24,16},{1,25},{9,1},{17,9},{25,17},{2,26},{10... | collective-permute-start | bytes 393224 | tf_op jit(solution)/shard_map/ppermute | solution.py:381
  41.2 5.2 %collective-permute-start.13 = (f32[192,128]{1,0:T(8,128)S(1)}, f32[192,128]{1,0:T(8,128)S(1)}, u32[]{:S(2)}, u32[]{:S(2)}) collective-permute-start(f32[192,128]{1,0:T(8,128)S(1)} %get-tuple-element.64), channel_id=1, source_target_pairs={{0,2},{2,0},{4,6},{6,4},{1,3},{3,1},{5,7},{7,5},{8,10},{10,8},{12,... | collective-permute-start | bytes 294920 | tf_op jit(solution)/shard_map/ppermute | solution.py:386
  42.2 5.1 %collective-permute-start.14 = (f32[192,128]{1,0:T(8,128)S(1)}, f32[192,128]{1,0:T(8,128)S(1)}, u32[]{:S(2)}, u32[]{:S(2)}) collective-permute-start(f32[192,128]{1,0:T(8,128)S(1)} %get-tuple-element.65), channel_id=1, source_target_pairs={{0,4},{2,6},{4,0},{6,2},{1,5},{3,7},{5,1},{7,3},{8,12},{10,14},{12... | collective-permute-start | bytes 294920 | tf_op jit(solution)/shard_map/ppermute | solution.py:386
  43.3 6.6 %collective-permute-start.15 = (f32[192,128]{1,0:T(8,128)S(1)}, f32[192,128]{1,0:T(8,128)S(1)}, u32[]{:S(2)}, u32[]{:S(2)}) collective-permute-start(f32[192,128]{1,0:T(8,128)S(1)} %get-tuple-element.66), channel_id=1, source_target_pairs={{0,6},{2,4},{4,2},{6,0},{1,7},{3,5},{5,3},{7,1},{8,14},{10,12},{12... | collective-permute-start | bytes 294920 | tf_op jit(solution)/shard_map/ppermute | solution.py:386
  44.8 16.7 %collective-permute-start.22 = (f32[256,256]{1,0:T(8,128)S(1)}, f32[256,256]{1,0:T(8,128)S(1)}, u32[]{:S(2)}, u32[]{:S(2)}) collective-permute-start(f32[256,256]{1,0:T(8,128)S(1)} %maximum_add_fusion.own_ref), channel_id=1, source_target_pairs={{0,2},{2,0},{4,6},{6,4},{1,3},{3,1},{5,7},{7,5},{8,10},{10,8},{12,... | collective-permute-start | bytes 786440 | tf_op jit(solution)/shard_map/ppermute | solution.py:386
  50.0 5.4 %collective-permute-start.16 = (f32[192,128]{1,0:T(8,128)S(1)}, f32[192,128]{1,0:T(8,128)S(1)}, u32[]{:S(2)}, u32[]{:S(2)}) collective-permute-start(f32[192,128]{1,0:T(8,128)S(1)} %add_add_fusion.2), channel_id=1, source_target_pairs={{0,8},{8,0},{16,24},{24,16},{1,9},{9,1},{17,25},{25,17},{2,10},{10... | collective-permute-start | bytes 294920 | tf_op jit(solution)/shard_map/ppermute | solution.py:386
  50.6 9.1 %collective-permute-start.17 = (f32[192,128]{1,0:T(8,128)S(1)}, f32[192,128]{1,0:T(8,128)S(1)}, u32[]{:S(2)}, u32[]{:S(2)}) collective-permute-start(f32[192,128]{1,0:T(8,128)S(1)} %add_add_fusion.2), channel_id=1, source_target_pairs={{0,16},{8,24},{16,0},{24,8},{1,17},{9,25},{17,1},{25,9},{2,18},{10... | collective-permute-start | bytes 294920 | tf_op jit(solution)/shard_map/ppermute | solution.py:386
  52.8 6.9 %collective-permute-start.18 = (f32[192,128]{1,0:T(8,128)S(1)}, f32[192,128]{1,0:T(8,128)S(1)}, u32[]{:S(2)}, u32[]{:S(2)}) collective-permute-start(f32[192,128]{1,0:T(8,128)S(1)} %add_add_fusion.2), channel_id=1, source_target_pairs={{0,24},{8,16},{16,8},{24,0},{1,25},{9,17},{17,9},{25,1},{2,26},{10... | collective-permute-start | bytes 294920 | tf_op jit(solution)/shard_map/ppermute | solution.py:386
  54.5 14.8 %collective-permute-start.23 = (f32[256,256]{1,0:T(8,128)S(1)}, f32[256,256]{1,0:T(8,128)S(1)}, u32[]{:S(2)}, u32[]{:S(2)}) collective-permute-start(f32[256,256]{1,0:T(8,128)S(1)} %maximum_add_fusion.own_ref), channel_id=1, source_target_pairs={{0,4},{2,6},{4,0},{6,2},{1,5},{3,7},{5,1},{7,3},{8,12},{10,14},{12... | collective-permute-start | bytes 786440 | tf_op jit(solution)/shard_map/ppermute | solution.py:386
  55.4 13.8 %collective-permute-start.24 = (f32[256,256]{1,0:T(8,128)S(1)}, f32[256,256]{1,0:T(8,128)S(1)}, u32[]{:S(2)}, u32[]{:S(2)}) collective-permute-start(f32[256,256]{1,0:T(8,128)S(1)} %maximum_add_fusion.own_ref), channel_id=1, source_target_pairs={{0,6},{2,4},{4,2},{6,0},{1,7},{3,5},{5,3},{7,1},{8,14},{10,12},{12... | collective-permute-start | bytes 786440 | tf_op jit(solution)/shard_map/ppermute | solution.py:386
  59.8 12.7 %collective-permute-start.19 = (f32[192,128]{1,0:T(8,128)S(1)}, f32[192,128]{1,0:T(8,128)S(1)}, u32[]{:S(2)}, u32[]{:S(2)}) collective-permute-start(f32[192,128]{1,0:T(8,128)S(1)} %add_add_fusion.1.refs_0_), channel_id=1, source_target_pairs={{0,2},{2,0},{4,6},{6,4},{1,3},{3,1},{5,7},{7,5},{8,10},{10,8},{12,... | collective-permute-start | bytes 294920 | tf_op jit(solution)/shard_map/ppermute | solution.py:386
  60.8 11.7 %collective-permute-start.20 = (f32[192,128]{1,0:T(8,128)S(1)}, f32[192,128]{1,0:T(8,128)S(1)}, u32[]{:S(2)}, u32[]{:S(2)}) collective-permute-start(f32[192,128]{1,0:T(8,128)S(1)} %add_add_fusion.1.refs_0_), channel_id=1, source_target_pairs={{0,4},{2,6},{4,0},{6,2},{1,5},{3,7},{5,1},{7,3},{8,12},{10,14},{12... | collective-permute-start | bytes 294920 | tf_op jit(solution)/shard_map/ppermute | solution.py:386
  61.5 11.0 %collective-permute-start.21 = (f32[192,128]{1,0:T(8,128)S(1)}, f32[192,128]{1,0:T(8,128)S(1)}, u32[]{:S(2)}, u32[]{:S(2)}) collective-permute-start(f32[192,128]{1,0:T(8,128)S(1)} %add_add_fusion.1.refs_0_), channel_id=1, source_target_pairs={{0,6},{2,4},{4,2},{6,0},{1,7},{3,5},{5,3},{7,1},{8,14},{10,12},{12... | collective-permute-start | bytes 294920 | tf_op jit(solution)/shard_map/ppermute | solution.py:386
  72.6 4.8 %collective-permute-start.28 = (f32[192,128]{1,0:T(8,128)S(1)}, f32[192,128]{1,0:T(8,128)S(1)}, u32[]{:S(2)}, u32[]{:S(2)}) collective-permute-start(f32[192,128]{1,0:T(8,128)S(1)} %collective-permute-done.19.refs_1_), channel_id=1, source_target_pairs={{0,1},{1,0},{2,3},{3,2},{4,5},{5,4},{6,7},{7,6},{8,9},{9,8},{10,11... | collective-permute-start | bytes 294920 | tf_op jit(solution)/shard_map/ppermute | solution.py:386
  73.6 33.9 %collective-permute-start.25 = (f32[256,256]{1,0:T(8,128)S(1)}, f32[256,256]{1,0:T(8,128)S(1)}, u32[]{:S(2)}, u32[]{:S(2)}) collective-permute-start(f32[256,256]{1,0:T(8,128)S(1)} %fusion.57), channel_id=1, source_target_pairs={{0,8},{8,16},{16,24},{24,0},{1,9},{9,17},{17,25},{25,1},{2,10},{10... | collective-permute-start | bytes 786440 | tf_op jit(solution)/shard_map/ppermute | solution.py:381
  73.9 33.6 %collective-permute-start.26 = (f32[256,256]{1,0:T(8,128)S(1)}, f32[256,256]{1,0:T(8,128)S(1)}, u32[]{:S(2)}, u32[]{:S(2)}) collective-permute-start(f32[256,256]{1,0:T(8,128)S(1)} %fusion.58), channel_id=1, source_target_pairs={{0,24},{8,0},{16,8},{24,16},{1,25},{9,1},{17,9},{25,17},{2,26},{10... | collective-permute-start | bytes 786440 | tf_op jit(solution)/shard_map/ppermute | solution.py:381
  110.5 7.3 %collective-permute-start.32 = (f32[200,128]{1,0:T(8,128)S(1)}, f32[200,128]{1,0:T(8,128)S(1)}, u32[]{:S(2)}, u32[]{:S(2)}) collective-permute-start(f32[200,128]{1,0:T(8,128)S(1)} %get-tuple-element.80), channel_id=1, source_target_pairs={{0,2},{2,0},{4,6},{6,4},{1,3},{3,1},{5,7},{7,5},{8,10},{10,8},{12,... | collective-permute-start | bytes 307208 | tf_op jit(solution)/shard_map/ppermute | solution.py:386
  110.8 7.0 %collective-permute-start.33 = (f32[200,128]{1,0:T(8,128)S(1)}, f32[200,128]{1,0:T(8,128)S(1)}, u32[]{:S(2)}, u32[]{:S(2)}) collective-permute-start(f32[200,128]{1,0:T(8,128)S(1)} %get-tuple-element.80), channel_id=1, source_target_pairs={{0,4},{2,6},{4,0},{6,2},{1,5},{3,7},{5,1},{7,3},{8,12},{10,14},{12... | collective-permute-start | bytes 307208 | tf_op jit(solution)/shard_map/ppermute | solution.py:386
  111.5 6.4 %collective-permute-start.34 = (f32[200,128]{1,0:T(8,128)S(1)}, f32[200,128]{1,0:T(8,128)S(1)}, u32[]{:S(2)}, u32[]{:S(2)}) collective-permute-start(f32[200,128]{1,0:T(8,128)S(1)} %get-tuple-element.80), channel_id=1, source_target_pairs={{0,6},{2,4},{4,2},{6,0},{1,7},{3,5},{5,3},{7,1},{8,14},{10,12},{12... | collective-permute-start | bytes 307208 | tf_op jit(solution)/shard_map/ppermute | solution.py:386
  118.5 5.9 %collective-permute-start.36 = (f32[136,128]{1,0:T(8,128)S(1)}, f32[136,128]{1,0:T(8,128)S(1)}, u32[]{:S(2)}, u32[]{:S(2)}) collective-permute-start(f32[136,128]{1,0:T(8,128)S(1)} %fusion.30), channel_id=1, source_target_pairs={{0,16},{8,24},{16,0},{24,8},{1,17},{9,25},{17,1},{25,9},{2,18},{10... | collective-permute-start | bytes 208904 | tf_op jit(solution)/shard_map/ppermute | solution.py:386
  119.2 6.7 %collective-permute-start.35 = (f32[200,128]{1,0:T(8,128)S(1)}, f32[200,128]{1,0:T(8,128)S(1)}, u32[]{:S(2)}, u32[]{:S(2)}) collective-permute-start(f32[200,128]{1,0:T(8,128)S(1)} %get-tuple-element.100), channel_id=1, source_target_pairs={{0,8},{8,0},{16,24},{24,16},{1,9},{9,1},{17,25},{25,17},{2,10},{10... | collective-permute-start | bytes 307208 | tf_op jit(solution)/shard_map/ppermute | solution.py:386
  120.4 7.2 %collective-permute-start.37 = (f32[200,128]{1,0:T(8,128)S(1)}, f32[200,128]{1,0:T(8,128)S(1)}, u32[]{:S(2)}, u32[]{:S(2)}) collective-permute-start(f32[200,128]{1,0:T(8,128)S(1)} %get-tuple-element.101), channel_id=1, source_target_pairs={{0,24},{8,16},{16,8},{24,0},{1,25},{9,17},{17,9},{25,1},{2,26},{10... | collective-permute-start | bytes 307208 | tf_op jit(solution)/shard_map/ppermute | solution.py:386
  (16 other events, 190.2 us)

commit v4 on v3

--- a/solution.py
+++ b/solution.py
@@ -13,7 +13,7 @@
 HIGHEST = lax.Precision.HIGHEST
 POINT_AXES = ("blk", "leaf")
 TILE = 128
-PIVOT, BASE, AHEAD, REFINES = 8, 128, False, 1
+BASE, REFINES = 128, 1
 
 
 def mm(left, right):
@@ -46,36 +46,33 @@
     return guess
 
 
-def small_inverse(entries, size):
-    def at(table, a, b):
-        return table[(min(a, b), max(a, b))]
-
-    if size == 1:
-        return {(0, 0): reciprocal(entries[(0, 0)])}
-    if size == 2:
-        det = entries[(0, 0)] * entries[(1, 1)] - entries[(0, 1)] * entries[(0, 1)]
-        inv = reciprocal(det)
-        return {(0, 0): entries[(1, 1)] * inv, (1, 1): entries[(0, 0)] * inv, (0, 1): -entries[(0, 1)] * inv}
-    half = size // 2
-    idx = range(half)
-    upper = [(a, b) for a in idx for b in range(a, half)]
-    first = small_inverse({(a, b): entries[(a, b)] for a, b in upper}, half)
-    cross = [[entries[(a, half + b)] for b in idx] for a in idx]
-    lift = [[tree_sum(at(first, a, c) * cross[c][b] for c in idx) for b in idx] for a in idx]
-    schur = {
-        (a, b): entries[(half + a, half + b)] - tree_sum(cross[c][a] * lift[c][b] for c in idx)
-        for a, b in upper
-    }
-    last = small_inverse(schur, half)
-    mixed = [[tree_sum(lift[a][c] * at(last, c, b) for c in idx) for b in idx] for a in idx]
-    result = {}
-    for a, b in upper:
-        result[(half + a, half + b)] = last[(a, b)]
-        result[(a, b)] = first[(a, b)] + tree_sum(mixed[a][c] * lift[b][c] for c in idx)
-    for a in idx:
-        for b in idx:
-            result[(a, half + b)] = -mixed[a][b]
-    return result
+def pair_inverse(a, b, c):
+    inv = reciprocal(a * c - b * b)
+    return c * inv, -(b * inv), a * inv
+
+
+def quad_solve(entries, rows):
+    a0, a1, a2 = pair_inverse(entries[(0, 0)], entries[(0, 1)], entries[(1, 1)])
+    cross = [[entries[(a, 2 + b)] for b in (0, 1)] for a in (0, 1)]
+    lift = [
+        [a0 * cross[0][b] + a1 * cross[1][b] for b in (0, 1)],
+        [a1 * cross[0][b] + a2 * cross[1][b] for b in (0, 1)],
+    ]
+    s0, s1, s2 = pair_inverse(
+        *(
+            entries[(2 + a, 2 + b)] - (cross[0][a] * lift[0][b] + cross[1][a] * lift[1][b])
+            for a, b in ((0, 0), (0, 1), (1, 1))
+        )
+    )
+    solved = []
+    for r0, r1, r2, r3 in zip(*rows):
+        u0 = r2 - (lift[0][0] * r0 + lift[1][0] * r1)
+        u1 = r3 - (lift[0][1] * r0 + lift[1][1] * r1)
+        x2, x3 = s0 * u0 + s1 * u1, s1 * u0 + s2 * u1
+        x0 = (a0 * r0 + a1 * r1) - (lift[0][0] * x2 + lift[0][1] * x3)
+        x1 = (a1 * r0 + a2 * r1) - (lift[1][0] * x2 + lift[1][1] * x3)
+        solved.append((x0, x1, x2, x3))
+    return [list(row) for row in zip(*solved)]
 
 
 def pivot_inverse(matrix):
@@ -83,51 +80,43 @@
     lane = lax.broadcasted_iota(jnp.int32, (8, size), 1)
     sub = lax.broadcasted_iota(jnp.int32, (8, size), 0)
     parts = [matrix[8 * i : 8 * i + 8, :] for i in range(size // 8)]
-    idx = range(PIVOT)
-    upper = [(a, b) for a in idx for b in range(a, PIVOT)]
-
-    def row(r):
-        return jnp.broadcast_to(parts[r // 8][r % 8 : r % 8 + 1, :], (8, size))
-
-    def entry(values, c):
+    four = range(4)
+
+    def row(values, r):
+        return jnp.broadcast_to(values[r : r + 1, :], (8, size))
+
+    def column(values, c):
         return jnp.broadcast_to(values[:, c : c + 1], (8, size))
 
-    entries = None
-    for k in range(0, size, PIVOT):
-        home, first = k // 8, k % 8
-        rows = [row(k + a) for a in idx]
-        if entries is None:
-            entries = {(a, b): entry(rows[a], k + b) for a, b in upper}
-        ahead = AHEAD and k + PIVOT < size
-        if ahead:
-            later = k + PIVOT
-            side = [[entry(rows[a], later + b) for b in idx] for a in idx]
-            later_rows = [row(later + a) for a in idx]
-            later_entries = {(a, b): entry(later_rows[a], later + b) for a, b in upper}
-        inverse = small_inverse(entries, PIVOT)
-        full = [[inverse[(min(a, b), max(a, b))] for b in idx] for a in idx]
-        entries = None
-        if ahead:
-            lift = [[tree_sum(full[a][c] * side[c][b] for c in idx) for b in idx] for a in idx]
-            entries = {
-                (a, b): later_entries[(a, b)] - tree_sum(side[c][a] * lift[c][b] for c in idx)
-                for a, b in upper
-            }
-        here = (lane >= k) & (lane < k + PIVOT)
-        rows = [jnp.where(here, jnp.where(lane == k + a, 1.0, 0.0), rows[a]) for a in idx]
-        scaled = [tree_sum(full[a][b] * rows[b] for b in idx) for a in idx]
+    for home in range(size // 8):
+        k = 8 * home
+        here = (lane >= k) & (lane < k + 8)
+        pivots = [column(parts[home], k + b) for b in range(8)]
+        entries = {(a, b): row(pivots[b], a) for a in range(8) for b in range(a, 8)}
+        rows = [
+            jnp.where(here, jnp.where(lane == k + a, 1.0, 0.0), row(parts[home], a)) for a in range(8)
+        ]
+        cross = [[entries[(a, 4 + b)] for b in four] for a in four]
+        first = quad_solve(entries, [cross[a] + [rows[a]] for a in four])
+        lift = [first[a][:4] for a in four]
+        schur = {
+            (a, b): entries[(4 + a, 4 + b)] - tree_sum(cross[c][a] * lift[c][b] for c in four)
+            for a in four
+            for b in range(a, 4)
+        }
+        last = [[rows[4 + a] - tree_sum(lift[c][a] * rows[c] for c in four)] for a in four]
+        last = [values[0] for values in quad_solve(schur, last)]
+        scaled = [first[a][4] - tree_sum(lift[a][c] * last[c] for c in four) for a in four] + last
         updated = []
         for i, part in enumerate(parts):
-            columns = [entry(part, k + a) for a in idx]
-            base = jnp.where(here, 0.0, part)
             if i == home:
-                inside = (sub >= first) & (sub < first + PIVOT)
-                base = jnp.where(inside, 0.0, base)
-                columns = [
-                    jnp.where(inside, jnp.where(sub == first + a, -1.0, 0.0), column)
-                    for a, column in enumerate(columns)
-                ]
-            updated.append(base - tree_sum(columns[a] * scaled[a] for a in idx))
+                fresh = scaled[7]
+                for a in range(7):
+                    fresh = jnp.where(sub == a, scaled[a], fresh)
+                updated.append(fresh)
+            else:
+                taken = tree_sum(column(part, k + a) * scaled[a] for a in range(8))
+                updated.append(jnp.where(here, 0.0, part) - taken)
         parts = updated
     return jnp.concatenate(parts, axis=0)
 
@@ -516,8 +505,12 @@
     share = shares[0]
     for m in range(1, leaves):
         share = share + swapped(shares[m], "leaf", m)
-    upward, downward, gathered = sums(slab(late_sketch))
-    here = mm(gathered, columns[1]) + noise_variance * late_sketch
+    blocks = slab(late_sketch)
+    near = jnp.concatenate(blocks[: leaves // 2], axis=1)
+    far = jnp.concatenate(blocks[leaves // 2 :], axis=1)
+    cut = near.shape[1]
+    upward, here, downward = (mm(near, c[:cut]) + mm(far, c[cut:]) for c in columns)
+    here = here + noise_variance * late_sketch
     shares = slab(axis_sum(share, "blk"))
     *shares, upward, downward, here = lax.optimization_barrier((*shares, upward, downward, here))
     other_shares = [other_core(s) for s in shares]

time: 143 us -> 143 us (level)
    dot_general x15 -> x18, matrix products: 13.6 us -> 14.1 us  [mm(): jnp.dot(left, right, precision=HIGHEST, preferred_element_type=jnp.float32)]
  transfers between devices with their start and end apart: 38 -> 38, of which waited for: 14 -> 14; matrix products, arithmetic and copies ran while one was open for 12% -> 12% of each run, Pallas kernels for 22% -> 21%
where the time goes in v4:
time: 143 us; the launch traced here: 142 us
  starting transfers between devices  45.3 us (32%)
  Pallas kernels  35.2 us (25%)
  waiting for transfers between devices  26.5 us (19%)
  matrix products  14.5 us (10%)
  blocking collectives  12.1 us (8%)
  other arithmetic  4.57 us (3%)
  local copies, waits for them, and re-layouts  2.6 us (2%)
    pallas_call x4, Pallas kernels, kernel_call(): pl.pallas_call(kernel, out_shape=tuple((jax.ShapeDtypeStruct(shape, jnp.f...  33.4 us
    ppermute x31, starting transfers between devices, swapped(): return lax.ppermute(values, axis, [(i, i ^ mask) for i in range(size)])  31.7 us
    ppermute x31, waiting for transfers between devices, swapped(): return lax.ppermute(values, axis, [(i, i ^ mask) for i in range(size)])  20.7 us
    dot_general x18, matrix products, mm(): jnp.dot(left, right, precision=HIGHEST, preferred_element_type=jnp.float32)  14.1 us
    all_to_all x1, blocking collectives, exchange(): return lax.all_to_all(values, POINT_AXES, 0, 0, tiled=True)  12.1 us
    ppermute x6, starting transfers between devices, shifted(): lax.ppermute(values, axis, [(i, (i + distance) % size) for i in range(siz...  10.5 us
    ppermute x6, waiting for transfers between devices, shifted(): lax.ppermute(values, axis, [(i, (i + distance) % size) for i in range(siz...  5.75 us
    ppermute x1, starting transfers between devices, local(): arrived = lax.ppermute(meta, ('blk', 'samp'), route)  3.08 us
  transfers between devices with their start and end apart: 38, of which 14 were waited for; matrix products, arithmetic and copies ran while one was open for 12% of the time, Pallas kernels for 21%

profile of v4, /device:TPU:0, one launch (start us, length us, event | category | flops | bytes accessed | tf_op | source)
XLA Modules:
  0.0 142.2 jit_solution(15473225823889802576)
XLA Ops:
  0.6 1.9 %prepare.1 = (f32[168,256]{1,0:T(8,128)}, f32[128,256]{1,0:T(8,128)}, f32[8,256]{1,0:T(8,128)}, f32[256,256]{1,0:T(8,128)}, f32[32,256]{1,0:T(8,128)}) custom-call(s32[1]{0:T(128)} %bitcast.core_ref, f32[3,256]{1,0:T(4,128)} %points_ref.1, s32[1,8]{1,0:T(1,128)} %neighbors_ref.1, f32[512,256]{1,0:T(8,128)} %omega_ref.1, f32[1,256]{1,0:T(1,128)} %bitcast.127, ...), custom_call_target="tpu_custom_call" | custom-call | flops 1000000 | bytes 524288 | tf_op jit(solution)/shard_map/prepare/pallas_call | solution.py:290
  2.5 3.1 %collective-permute-start.3 = (f32[8,256]{1,0:T(8,128)}, f32[8,256]{1,0:T(8,128)S(1)}, u32[]{:S(2)}, u32[]{:S(2)}) collective-permute-start(f32[8,256]{1,0:T(8,128)} %get-tuple-element.46.refs_1_), channel_id=1, source_target_pairs={{0,8},{1,25},{8,16},{9,1},{16,24},{17,9},{24,0},{25,17},{2,10},{3,... | collective-permute-start | bytes 24584 | tf_op jit(solution)/shard_map/ppermute | solution.py:442
  5.6 1.5 %collective-permute-start = (f32[168,256]{1,0:T(8,128)}, f32[168,256]{1,0:T(8,128)S(1)}, u32[]{:S(2)}, u32[]{:S(2)}) collective-permute-start(f32[168,256]{1,0:T(8,128)} %get-tuple-element.45), channel_id=1, source_target_pairs={{0,2},{2,0},{4,6},{6,4},{1,3},{3,1},{5,7},{7,5},{8,10},{10,8},{12,... | collective-permute-start | bytes 516104 | tf_op jit(solution)/shard_map/ppermute | solution.py:375
  7.1 1.5 %collective-permute-start.1 = (f32[168,256]{1,0:T(8,128)}, f32[168,256]{1,0:T(8,128)S(1)}, u32[]{:S(2)}, u32[]{:S(2)}) collective-permute-start(f32[168,256]{1,0:T(8,128)} %get-tuple-element.45), channel_id=1, source_target_pairs={{0,4},{2,6},{4,0},{6,2},{1,5},{3,7},{5,1},{7,3},{8,12},{10,14},{12... | collective-permute-start | bytes 516104 | tf_op jit(solution)/shard_map/ppermute | solution.py:375
  9.1 1.5 %collective-permute-start.7 = (f32[128,256]{1,0:T(8,128)}, f32[128,256]{1,0:T(8,128)S(1)}, u32[]{:S(2)}, u32[]{:S(2)}) collective-permute-start(f32[128,256]{1,0:T(8,128)} %get-tuple-element.54), channel_id=1, source_target_pairs={{0,2},{2,0},{4,6},{6,4},{1,3},{3,1},{5,7},{7,5},{8,10},{10,8},{12,... | collective-permute-start | bytes 393224 | tf_op jit(solution)/shard_map/ppermute | solution.py:375
  12.7 1.6 %collective-permute-start.8 = (f32[128,256]{1,0:T(8,128)}, f32[128,256]{1,0:T(8,128)S(1)}, u32[]{:S(2)}, u32[]{:S(2)}) collective-permute-start(f32[128,256]{1,0:T(8,128)} %get-tuple-element.54), channel_id=1, source_target_pairs={{0,4},{2,6},{4,0},{6,2},{1,5},{3,7},{5,1},{7,3},{8,12},{10,14},{12... | collective-permute-start | bytes 393224 | tf_op jit(solution)/shard_map/ppermute | solution.py:375
  16.2 1.2 collective-permute-done.1
  19.9 2.6 %collective-permute-start.6 = (f32[160,256]{1,0:T(8,128)S(1)}, f32[160,256]{1,0:T(8,128)S(1)}, u32[]{:S(2)}, u32[]{:S(2)}) collective-permute-start(f32[160,256]{1,0:T(8,128)S(1)} %fusion.35), channel_id=1, source_target_pairs={{0,24},{8,0},{16,8},{24,16},{1,25},{9,1},{17,9},{25,17},{2,26},{10... | collective-permute-start | bytes 491528 | tf_op jit(solution)/shard_map/ppermute | solution.py:370
  26.5 3.3 %collective-permute-start.11 = (f32[128,256]{1,0:T(8,128)S(1)}, f32[128,256]{1,0:T(8,128)S(1)}, u32[]{:S(2)}, u32[]{:S(2)}) collective-permute-start(f32[128,256]{1,0:T(8,128)S(1)} %fusion.66), channel_id=1, source_target_pairs={{0,24},{8,0},{16,8},{24,16},{1,25},{9,1},{17,9},{25,17},{2,26},{10... | collective-permute-start | bytes 393224 | tf_op jit(solution)/shard_map/ppermute | solution.py:370
  30.7 4.7 %collective-permute-done.10 = f32[128,256]{1,0:T(8,128)S(1)} collective-permute-done((f32[128,256]{1,0:T(8,128)S(1)}, f32[128,256]{1,0:T(8,128)S(1)}, u32[]{:S(2)}, u32[]{:S(2)}) %collective-permute-start.10) | collective-permute-done | bytes 131104 | tf_op jit(solution)/shard_map/ppermute | solution.py:370
  38.1 1.4 %collective-permute-done.12.other_ref = f32[256,256]{1,0:T(8,128)S(1)} collective-permute-done((f32[256,256]{1,0:T(8,128)S(1)}, f32[256,256]{1,0:T(8,128)S(1)}, u32[]{:S(2)}, u32[]{:S(2)}) %collective-permute-start.12) | collective-permute-done | bytes 262176 | tf_op jit(solution)/shard_map/ppermute | solution.py:375
  39.6 1.6 %payload.1 = (f32[512,256]{1,0:T(8,128)S(1)}, f32[192,128]{1,0:T(8,128)S(1)}, f32[192,128]{1,0:T(8,128)S(1)}, f32[192,128]{1,0:T(8,128)S(1)}, f32[192,128]{1,0:T(8,128)S(1)}) custom-call(s32[2]{0:T(128)S(1)} %pad_add_fusion.place_ref, f32[256,256]{1,0:T(8,128)S(1)} %copy-done.1, f32[256,256]{1,0:T(8,128)S(1)} %maximum_add_fusion.own_ref, ...), custom_call_target="tpu_custom_call" | custom-call | flops 1000000000 | bytes 1048576 | tf_op jit(solution)/shard_map/payload/pallas_call | solution.py:356
  43.3 1.4 %collective-permute-start.15 = (f32[192,128]{1,0:T(8,128)S(1)}, f32[192,128]{1,0:T(8,128)S(1)}, u32[]{:S(2)}, u32[]{:S(2)}) collective-permute-start(f32[192,128]{1,0:T(8,128)S(1)} %get-tuple-element.66), channel_id=1, source_target_pairs={{0,6},{2,4},{4,2},{6,0},{1,7},{3,5},{5,3},{7,1},{8,14},{10,12},{12... | collective-permute-start | bytes 294920 | tf_op jit(solution)/shard_map/ppermute | solution.py:375
  44.8 1.5 %collective-permute-start.23 = (f32[256,256]{1,0:T(8,128)S(1)}, f32[256,256]{1,0:T(8,128)S(1)}, u32[]{:S(2)}, u32[]{:S(2)}) collective-permute-start(f32[256,256]{1,0:T(8,128)S(1)} %maximum_add_fusion.own_ref), channel_id=1, source_target_pairs={{0,4},{2,6},{4,0},{6,2},{1,5},{3,7},{5,1},{7,3},{8,12},{10,14},{12... | collective-permute-start | bytes 786440 | tf_op jit(solution)/shard_map/ppermute | solution.py:375
  47.2 7.4 %collective-permute-done.14 = f32[192,128]{1,0:T(8,128)S(1)} collective-permute-done((f32[192,128]{1,0:T(8,128)S(1)}, f32[192,128]{1,0:T(8,128)S(1)}, u32[]{:S(2)}, u32[]{:S(2)}) %collective-permute-start.14) | collective-permute-done | bytes 98336 | tf_op jit(solution)/shard_map/ppermute | solution.py:375
  55.2 3.6 %collective-permute-start.17 = (f32[192,128]{1,0:T(8,128)S(1)}, f32[192,128]{1,0:T(8,128)S(1)}, u32[]{:S(2)}, u32[]{:S(2)}) collective-permute-start(f32[192,128]{1,0:T(8,128)S(1)} %add_add_fusion.2), channel_id=1, source_target_pairs={{0,16},{8,24},{16,0},{24,8},{1,17},{9,25},{17,1},{25,9},{2,18},{10... | collective-permute-start | bytes 294920 | tf_op jit(solution)/shard_map/ppermute | solution.py:375
  60.3 2.2 %collective-permute-done.17 = f32[192,128]{1,0:T(8,128)S(1)} collective-permute-done((f32[192,128]{1,0:T(8,128)S(1)}, f32[192,128]{1,0:T(8,128)S(1)}, u32[]{:S(2)}, u32[]{:S(2)}) %collective-permute-start.17) | collective-permute-done | bytes 98336 | tf_op jit(solution)/shard_map/ppermute | solution.py:375
  62.5 2.8 %collective-permute-done.18 = f32[192,128]{1,0:T(8,128)S(1)} collective-permute-done((f32[192,128]{1,0:T(8,128)S(1)}, f32[192,128]{1,0:T(8,128)S(1)}, u32[]{:S(2)}, u32[]{:S(2)}) %collective-permute-start.18) | collective-permute-done | bytes 98336 | tf_op jit(solution)/shard_map/ppermute | solution.py:375
  65.4 1.8 %collective-permute-start.20 = (f32[192,128]{1,0:T(8,128)S(1)}, f32[192,128]{1,0:T(8,128)S(1)}, u32[]{:S(2)}, u32[]{:S(2)}) collective-permute-start(f32[192,128]{1,0:T(8,128)S(1)} %add_add_fusion.1.refs_0_), channel_id=1, source_target_pairs={{0,4},{2,6},{4,0},{6,2},{1,5},{3,7},{5,1},{7,3},{8,12},{10,14},{12... | collective-permute-start | bytes 294920 | tf_op jit(solution)/shard_map/ppermute | solution.py:375
  67.2 1.6 %collective-permute-start.21 = (f32[192,128]{1,0:T(8,128)S(1)}, f32[192,128]{1,0:T(8,128)S(1)}, u32[]{:S(2)}, u32[]{:S(2)}) collective-permute-start(f32[192,128]{1,0:T(8,128)S(1)} %add_add_fusion.1.refs_0_), channel_id=1, source_target_pairs={{0,6},{2,4},{4,2},{6,0},{1,7},{3,5},{5,3},{7,1},{8,14},{10,12},{12... | collective-permute-start | bytes 294920 | tf_op jit(solution)/shard_map/ppermute | solution.py:375
  74.6 3.1 %collective-permute-start.26 = (f32[256,256]{1,0:T(8,128)S(1)}, f32[256,256]{1,0:T(8,128)S(1)}, u32[]{:S(2)}, u32[]{:S(2)}) collective-permute-start(f32[256,256]{1,0:T(8,128)S(1)} %convolution_add_fusion.2), channel_id=1, source_target_pairs={{0,24},{8,0},{16,8},{24,16},{1,25},{9,1},{17,9},{25,17},{2,26},{10... | collective-permute-start | bytes 786440 | tf_op jit(solution)/shard_map/ppermute | solution.py:370
  77.6 29.8 %inverse_and_solve.1 = (f32[512,512]{1,0:T(8,128)S(1)}, f32[512,512]{1,0:T(8,128)S(1)}, f32[32,512]{1,0:T(8,128)S(1)}) custom-call(s32[2]{0:T(128)S(1)} %pad_add_fusion.place_ref, f32[192,128]{1,0:T(8,128)S(1)} %add_add_fusion.1.refs_0_, f32[192,128]{1,0:T(8,128)S(1)} %collective-permute-done.19.refs_1_, f32[192,128]{1,0:T(8,128)S(1)} %collective-permute-done.20.refs_2_, ...), custom_call_target="tpu_custom_call" | custom-call | flops 30000001024 | bytes 1048576 | tf_op jit(solution)/shard_map/inverse_and_solve/pallas_call | solution.py:356
  107.6 1.5 %collective-permute-done.31.other_ref = f32[256,256]{1,0:T(8,128)S(1)} collective-permute-done((f32[256,256]{1,0:T(8,128)S(1)}, f32[256,256]{1,0:T(8,128)S(1)}, u32[]{:S(2)}, u32[]{:S(2)}) %collective-permute-start.31) | collective-permute-done | bytes 262176 | tf_op jit(solution)/shard_map/ppermute | solution.py:375
  109.1 1.3 image.1
  110.8 1.9 %collective-permute-start.33 = (f32[200,128]{1,0:T(8,128)S(1)}, f32[200,128]{1,0:T(8,128)S(1)}, u32[]{:S(2)}, u32[]{:S(2)}) collective-permute-start(f32[200,128]{1,0:T(8,128)S(1)} %get-tuple-element.80), channel_id=1, source_target_pairs={{0,4},{2,6},{4,0},{6,2},{1,5},{3,7},{5,1},{7,3},{8,12},{10,14},{12... | collective-permute-start | bytes 307208 | tf_op jit(solution)/shard_map/ppermute | solution.py:375
  112.7 1.3 collective-permute-start.34
  114.0 1.8 %fusion.68 = f32[512,512]{1,0:T(8,128)S(1)} fusion(f32[512,512]{1,0:T(8,128)S(1)} %get-tuple-element.83, f32[512,512]{1,0:T(8,128)S(1)} %get-tuple-element.84), kind=kOutput, calls=%fused_computation.146 | convolution fusion | flops 1610612736 | bytes 3145728 | tf_op jit(solution)/shard_map/dot_general | solution.py:20
  115.8 1.9 %convolution_subtract_fusion = bf16[512,512]{1,0:T(8,128)(2,1)S(1)} fusion(f32[512,512]{1,0:T(8,128)S(1)} %get-tuple-element.84, f32[512,512]{1,0:T(8,128)S(1)} %get-tuple-element.85, f32[512,512]{1,0:T(8,128)S(1)} %fusion.68), kind=kOutput, calls=%fused_computation.10 | convolution fusion | flops 1611137024 | bytes 3670016 | tf_op jit(solution)/shard_map/dot_general | solution.py:20
  120.2 3.8 %collective-permute-start.37 = (f32[200,128]{1,0:T(8,128)S(1)}, f32[200,128]{1,0:T(8,128)S(1)}, u32[]{:S(2)}, u32[]{:S(2)}) collective-permute-start(f32[200,128]{1,0:T(8,128)S(1)} %get-tuple-element.101), channel_id=1, source_target_pairs={{0,24},{8,16},{16,8},{24,0},{1,25},{9,17},{17,9},{25,1},{2,26},{10... | collective-permute-start | bytes 307208 | tf_op jit(solution)/shard_map/ppermute | solution.py:375
  124.4 1.4 collective-permute-done.36
  126.1 1.7 %collective-permute-done.37 = f32[200,128]{1,0:T(8,128)S(1)} collective-permute-done((f32[200,128]{1,0:T(8,128)S(1)}, f32[200,128]{1,0:T(8,128)S(1)}, u32[]{:S(2)}, u32[]{:S(2)}) %collective-permute-start.37) | collective-permute-done | bytes 102432 | tf_op jit(solution)/shard_map/ppermute | solution.py:375
  129.4 12.1 %all_to_all.6 = f32[16,8,128]{2,1,0:T(8,128)S(1)} all-to-all(f32[16,8,128]{2,1,0:T(8,128)S(1)} %broadcast_in_dim.5), channel_id=1, replica_groups=mesh['blk'=4,'leaf'=4,'samp'=2] {'blk','leaf'}, dimensions={0} | all-to-all | bytes 131072 | tf_op jit(solution)/shard_map/all_to_all | solution.py:387
  (140 shorter events, 30.9 us)
Async XLA Ops:
  2.5 8.1 %collective-permute-start.3 = (f32[8,256]{1,0:T(8,128)}, f32[8,256]{1,0:T(8,128)S(1)}, u32[]{:S(2)}, u32[]{:S(2)}) collective-permute-start(f32[8,256]{1,0:T(8,128)} %get-tuple-element.46.refs_1_), channel_id=1, source_target_pairs={{0,8},{1,25},{8,16},{9,1},{16,24},{17,9},{24,0},{25,17},{2,10},{3,... | collective-permute-start | bytes 24584 | tf_op jit(solution)/shard_map/ppermute | solution.py:442
  5.6 10.1 %collective-permute-start = (f32[168,256]{1,0:T(8,128)}, f32[168,256]{1,0:T(8,128)S(1)}, u32[]{:S(2)}, u32[]{:S(2)}) collective-permute-start(f32[168,256]{1,0:T(8,128)} %get-tuple-element.45), channel_id=1, source_target_pairs={{0,2},{2,0},{4,6},{6,4},{1,3},{3,1},{5,7},{7,5},{8,10},{10,8},{12,... | collective-permute-start | bytes 516104 | tf_op jit(solution)/shard_map/ppermute | solution.py:375
  7.1 10.4 %collective-permute-start.1 = (f32[168,256]{1,0:T(8,128)}, f32[168,256]{1,0:T(8,128)S(1)}, u32[]{:S(2)}, u32[]{:S(2)}) collective-permute-start(f32[168,256]{1,0:T(8,128)} %get-tuple-element.45), channel_id=1, source_target_pairs={{0,4},{2,6},{4,0},{6,2},{1,5},{3,7},{5,1},{7,3},{8,12},{10,14},{12... | collective-permute-start | bytes 516104 | tf_op jit(solution)/shard_map/ppermute | solution.py:375
  8.6 8.9 %collective-permute-start.2 = (f32[168,256]{1,0:T(8,128)}, f32[168,256]{1,0:T(8,128)S(1)}, u32[]{:S(2)}, u32[]{:S(2)}) collective-permute-start(f32[168,256]{1,0:T(8,128)} %get-tuple-element.45), channel_id=1, source_target_pairs={{0,6},{2,4},{4,2},{6,0},{1,7},{3,5},{5,3},{7,1},{8,14},{10,12},{12... | collective-permute-start | bytes 516104 | tf_op jit(solution)/shard_map/ppermute | solution.py:375
  9.1 15.2 %collective-permute-start.7 = (f32[128,256]{1,0:T(8,128)}, f32[128,256]{1,0:T(8,128)S(1)}, u32[]{:S(2)}, u32[]{:S(2)}) collective-permute-start(f32[128,256]{1,0:T(8,128)} %get-tuple-element.54), channel_id=1, source_target_pairs={{0,2},{2,0},{4,6},{6,4},{1,3},{3,1},{5,7},{7,5},{8,10},{10,8},{12,... | collective-permute-start | bytes 393224 | tf_op jit(solution)/shard_map/ppermute | solution.py:375
  12.7 11.5 %collective-permute-start.8 = (f32[128,256]{1,0:T(8,128)}, f32[128,256]{1,0:T(8,128)S(1)}, u32[]{:S(2)}, u32[]{:S(2)}) collective-permute-start(f32[128,256]{1,0:T(8,128)} %get-tuple-element.54), channel_id=1, source_target_pairs={{0,4},{2,6},{4,0},{6,2},{1,5},{3,7},{5,1},{7,3},{8,12},{10,14},{12... | collective-permute-start | bytes 393224 | tf_op jit(solution)/shard_map/ppermute | solution.py:375
  15.7 8.6 %collective-permute-start.9 = (f32[128,256]{1,0:T(8,128)}, f32[128,256]{1,0:T(8,128)S(1)}, u32[]{:S(2)}, u32[]{:S(2)}) collective-permute-start(f32[128,256]{1,0:T(8,128)} %get-tuple-element.54), channel_id=1, source_target_pairs={{0,6},{2,4},{4,2},{6,0},{1,7},{3,5},{5,3},{7,1},{8,14},{10,12},{12... | collective-permute-start | bytes 393224 | tf_op jit(solution)/shard_map/ppermute | solution.py:375
  19.9 17.2 %collective-permute-start.6 = (f32[160,256]{1,0:T(8,128)S(1)}, f32[160,256]{1,0:T(8,128)S(1)}, u32[]{:S(2)}, u32[]{:S(2)}) collective-permute-start(f32[160,256]{1,0:T(8,128)S(1)} %fusion.35), channel_id=1, source_target_pairs={{0,24},{8,0},{16,8},{24,16},{1,25},{9,1},{17,9},{25,17},{2,26},{10... | collective-permute-start | bytes 491528 | tf_op jit(solution)/shard_map/ppermute | solution.py:370
  24.2 12.9 %collective-permute-start.5 = (f32[160,256]{1,0:T(8,128)S(1)}, f32[160,256]{1,0:T(8,128)S(1)}, u32[]{:S(2)}, u32[]{:S(2)}) collective-permute-start(f32[160,256]{1,0:T(8,128)S(1)} %fusion.36), channel_id=1, source_target_pairs={{0,8},{8,16},{16,24},{24,0},{1,9},{9,17},{17,25},{25,1},{2,10},{10... | collective-permute-start | bytes 491528 | tf_op jit(solution)/shard_map/ppermute | solution.py:370
  25.7 9.7 %collective-permute-start.10 = (f32[128,256]{1,0:T(8,128)S(1)}, f32[128,256]{1,0:T(8,128)S(1)}, u32[]{:S(2)}, u32[]{:S(2)}) collective-permute-start(f32[128,256]{1,0:T(8,128)S(1)} %fusion.65), channel_id=1, source_target_pairs={{0,8},{8,16},{16,24},{24,0},{1,9},{9,17},{17,25},{25,1},{2,10},{10... | collective-permute-start | bytes 393224 | tf_op jit(solution)/shard_map/ppermute | solution.py:370
  26.5 10.0 %collective-permute-start.11 = (f32[128,256]{1,0:T(8,128)S(1)}, f32[128,256]{1,0:T(8,128)S(1)}, u32[]{:S(2)}, u32[]{:S(2)}) collective-permute-start(f32[128,256]{1,0:T(8,128)S(1)} %fusion.66), channel_id=1, source_target_pairs={{0,24},{8,0},{16,8},{24,16},{1,25},{9,1},{17,9},{25,17},{2,26},{10... | collective-permute-start | bytes 393224 | tf_op jit(solution)/shard_map/ppermute | solution.py:370
  41.2 5.9 %collective-permute-start.13 = (f32[192,128]{1,0:T(8,128)S(1)}, f32[192,128]{1,0:T(8,128)S(1)}, u32[]{:S(2)}, u32[]{:S(2)}) collective-permute-start(f32[192,128]{1,0:T(8,128)S(1)} %get-tuple-element.64), channel_id=1, source_target_pairs={{0,2},{2,0},{4,6},{6,4},{1,3},{3,1},{5,7},{7,5},{8,10},{10,8},{12,... | collective-permute-start | bytes 294920 | tf_op jit(solution)/shard_map/ppermute | solution.py:375
  42.2 12.4 %collective-permute-start.14 = (f32[192,128]{1,0:T(8,128)S(1)}, f32[192,128]{1,0:T(8,128)S(1)}, u32[]{:S(2)}, u32[]{:S(2)}) collective-permute-start(f32[192,128]{1,0:T(8,128)S(1)} %get-tuple-element.65), channel_id=1, source_target_pairs={{0,4},{2,6},{4,0},{6,2},{1,5},{3,7},{5,1},{7,3},{8,12},{10,14},{12... | collective-permute-start | bytes 294920 | tf_op jit(solution)/shard_map/ppermute | solution.py:375
  43.3 11.2 %collective-permute-start.15 = (f32[192,128]{1,0:T(8,128)S(1)}, f32[192,128]{1,0:T(8,128)S(1)}, u32[]{:S(2)}, u32[]{:S(2)}) collective-permute-start(f32[192,128]{1,0:T(8,128)S(1)} %get-tuple-element.66), channel_id=1, source_target_pairs={{0,6},{2,4},{4,2},{6,0},{1,7},{3,5},{5,3},{7,1},{8,14},{10,12},{12... | collective-permute-start | bytes 294920 | tf_op jit(solution)/shard_map/ppermute | solution.py:375
  44.8 22.5 %collective-permute-start.23 = (f32[256,256]{1,0:T(8,128)S(1)}, f32[256,256]{1,0:T(8,128)S(1)}, u32[]{:S(2)}, u32[]{:S(2)}) collective-permute-start(f32[256,256]{1,0:T(8,128)S(1)} %maximum_add_fusion.own_ref), channel_id=1, source_target_pairs={{0,4},{2,6},{4,0},{6,2},{1,5},{3,7},{5,1},{7,3},{8,12},{10,14},{12... | collective-permute-start | bytes 786440 | tf_op jit(solution)/shard_map/ppermute | solution.py:375
  46.3 22.6 %collective-permute-start.24 = (f32[256,256]{1,0:T(8,128)S(1)}, f32[256,256]{1,0:T(8,128)S(1)}, u32[]{:S(2)}, u32[]{:S(2)}) collective-permute-start(f32[256,256]{1,0:T(8,128)S(1)} %maximum_add_fusion.own_ref), channel_id=1, source_target_pairs={{0,6},{2,4},{4,2},{6,0},{1,7},{3,5},{5,3},{7,1},{8,14},{10,12},{12... | collective-permute-start | bytes 786440 | tf_op jit(solution)/shard_map/ppermute | solution.py:375
  54.6 4.7 %collective-permute-start.16 = (f32[192,128]{1,0:T(8,128)S(1)}, f32[192,128]{1,0:T(8,128)S(1)}, u32[]{:S(2)}, u32[]{:S(2)}) collective-permute-start(f32[192,128]{1,0:T(8,128)S(1)} %add_add_fusion.2), channel_id=1, source_target_pairs={{0,8},{8,0},{16,24},{24,16},{1,9},{9,1},{17,25},{25,17},{2,10},{10... | collective-permute-start | bytes 294920 | tf_op jit(solution)/shard_map/ppermute | solution.py:375
  55.2 7.3 %collective-permute-start.17 = (f32[192,128]{1,0:T(8,128)S(1)}, f32[192,128]{1,0:T(8,128)S(1)}, u32[]{:S(2)}, u32[]{:S(2)}) collective-permute-start(f32[192,128]{1,0:T(8,128)S(1)} %add_add_fusion.2), channel_id=1, source_target_pairs={{0,16},{8,24},{16,0},{24,8},{1,17},{9,25},{17,1},{25,9},{2,18},{10... | collective-permute-start | bytes 294920 | tf_op jit(solution)/shard_map/ppermute | solution.py:375
  58.9 6.4 %collective-permute-start.18 = (f32[192,128]{1,0:T(8,128)S(1)}, f32[192,128]{1,0:T(8,128)S(1)}, u32[]{:S(2)}, u32[]{:S(2)}) collective-permute-start(f32[192,128]{1,0:T(8,128)S(1)} %add_add_fusion.2), channel_id=1, source_target_pairs={{0,24},{8,16},{16,8},{24,0},{1,25},{9,17},{17,9},{25,1},{2,26},{10... | collective-permute-start | bytes 294920 | tf_op jit(solution)/shard_map/ppermute | solution.py:375
  59.3 11.5 %collective-permute-start.22 = (f32[256,256]{1,0:T(8,128)S(1)}, f32[256,256]{1,0:T(8,128)S(1)}, u32[]{:S(2)}, u32[]{:S(2)}) collective-permute-start(f32[256,256]{1,0:T(8,128)S(1)} %maximum_add_fusion.own_ref), channel_id=1, source_target_pairs={{0,2},{2,0},{4,6},{6,4},{1,3},{3,1},{5,7},{7,5},{8,10},{10,8},{12,... | collective-permute-start | bytes 786440 | tf_op jit(solution)/shard_map/ppermute | solution.py:375
  65.3 7.3 %collective-permute-start.19 = (f32[192,128]{1,0:T(8,128)S(1)}, f32[192,128]{1,0:T(8,128)S(1)}, u32[]{:S(2)}, u32[]{:S(2)}) collective-permute-start(f32[192,128]{1,0:T(8,128)S(1)} %add_add_fusion.1.refs_0_), channel_id=1, source_target_pairs={{0,2},{2,0},{4,6},{6,4},{1,3},{3,1},{5,7},{7,5},{8,10},{10,8},{12,... | collective-permute-start | bytes 294920 | tf_op jit(solution)/shard_map/ppermute | solution.py:375
  65.4 7.3 %collective-permute-start.20 = (f32[192,128]{1,0:T(8,128)S(1)}, f32[192,128]{1,0:T(8,128)S(1)}, u32[]{:S(2)}, u32[]{:S(2)}) collective-permute-start(f32[192,128]{1,0:T(8,128)S(1)} %add_add_fusion.1.refs_0_), channel_id=1, source_target_pairs={{0,4},{2,6},{4,0},{6,2},{1,5},{3,7},{5,1},{7,3},{8,12},{10,14},{12... | collective-permute-start | bytes 294920 | tf_op jit(solution)/shard_map/ppermute | solution.py:375
  67.2 5.5 %collective-permute-start.21 = (f32[192,128]{1,0:T(8,128)S(1)}, f32[192,128]{1,0:T(8,128)S(1)}, u32[]{:S(2)}, u32[]{:S(2)}) collective-permute-start(f32[192,128]{1,0:T(8,128)S(1)} %add_add_fusion.1.refs_0_), channel_id=1, source_target_pairs={{0,6},{2,4},{4,2},{6,0},{1,7},{3,5},{5,3},{7,1},{8,14},{10,12},{12... | collective-permute-start | bytes 294920 | tf_op jit(solution)/shard_map/ppermute | solution.py:375
  72.8 4.8 %collective-permute-start.28 = (f32[192,128]{1,0:T(8,128)S(1)}, f32[192,128]{1,0:T(8,128)S(1)}, u32[]{:S(2)}, u32[]{:S(2)}) collective-permute-start(f32[192,128]{1,0:T(8,128)S(1)} %collective-permute-done.19.refs_1_), channel_id=1, source_target_pairs={{0,1},{1,0},{2,3},{3,2},{4,5},{5,4},{6,7},{7,6},{8,9},{9,8},{10,11... | collective-permute-start | bytes 294920 | tf_op jit(solution)/shard_map/ppermute | solution.py:375
  73.8 33.6 %collective-permute-start.25 = (f32[256,256]{1,0:T(8,128)S(1)}, f32[256,256]{1,0:T(8,128)S(1)}, u32[]{:S(2)}, u32[]{:S(2)}) collective-permute-start(f32[256,256]{1,0:T(8,128)S(1)} %convolution_add_fusion.3), channel_id=1, source_target_pairs={{0,8},{8,16},{16,24},{24,0},{1,9},{9,17},{17,25},{25,1},{2,10},{10... | collective-permute-start | bytes 786440 | tf_op jit(solution)/shard_map/ppermute | solution.py:370
  74.6 32.9 %collective-permute-start.26 = (f32[256,256]{1,0:T(8,128)S(1)}, f32[256,256]{1,0:T(8,128)S(1)}, u32[]{:S(2)}, u32[]{:S(2)}) collective-permute-start(f32[256,256]{1,0:T(8,128)S(1)} %convolution_add_fusion.2), channel_id=1, source_target_pairs={{0,24},{8,0},{16,8},{24,16},{1,25},{9,1},{17,9},{25,17},{2,26},{10... | collective-permute-start | bytes 786440 | tf_op jit(solution)/shard_map/ppermute | solution.py:370
  110.4 7.3 %collective-permute-start.32 = (f32[200,128]{1,0:T(8,128)S(1)}, f32[200,128]{1,0:T(8,128)S(1)}, u32[]{:S(2)}, u32[]{:S(2)}) collective-permute-start(f32[200,128]{1,0:T(8,128)S(1)} %get-tuple-element.80), channel_id=1, source_target_pairs={{0,2},{2,0},{4,6},{6,4},{1,3},{3,1},{5,7},{7,5},{8,10},{10,8},{12,... | collective-permute-start | bytes 307208 | tf_op jit(solution)/shard_map/ppermute | solution.py:375
  110.8 7.0 %collective-permute-start.33 = (f32[200,128]{1,0:T(8,128)S(1)}, f32[200,128]{1,0:T(8,128)S(1)}, u32[]{:S(2)}, u32[]{:S(2)}) collective-permute-start(f32[200,128]{1,0:T(8,128)S(1)} %get-tuple-element.80), channel_id=1, source_target_pairs={{0,4},{2,6},{4,0},{6,2},{1,5},{3,7},{5,1},{7,3},{8,12},{10,14},{12... | collective-permute-start | bytes 307208 | tf_op jit(solution)/shard_map/ppermute | solution.py:375
  112.7 5.6 %collective-permute-start.34 = (f32[200,128]{1,0:T(8,128)S(1)}, f32[200,128]{1,0:T(8,128)S(1)}, u32[]{:S(2)}, u32[]{:S(2)}) collective-permute-start(f32[200,128]{1,0:T(8,128)S(1)} %get-tuple-element.80), channel_id=1, source_target_pairs={{0,6},{2,4},{4,2},{6,0},{1,7},{3,5},{5,3},{7,1},{8,14},{10,12},{12... | collective-permute-start | bytes 307208 | tf_op jit(solution)/shard_map/ppermute | solution.py:375
  118.8 7.0 %collective-permute-start.36 = (f32[136,128]{1,0:T(8,128)S(1)}, f32[136,128]{1,0:T(8,128)S(1)}, u32[]{:S(2)}, u32[]{:S(2)}) collective-permute-start(f32[136,128]{1,0:T(8,128)S(1)} %fusion.40), channel_id=1, source_target_pairs={{0,16},{8,24},{16,0},{24,8},{1,17},{9,25},{17,1},{25,9},{2,18},{10... | collective-permute-start | bytes 208904 | tf_op jit(solution)/shard_map/ppermute | solution.py:375
  119.6 6.6 %collective-permute-start.35 = (f32[200,128]{1,0:T(8,128)S(1)}, f32[200,128]{1,0:T(8,128)S(1)}, u32[]{:S(2)}, u32[]{:S(2)}) collective-permute-start(f32[200,128]{1,0:T(8,128)S(1)} %get-tuple-element.100), channel_id=1, source_target_pairs={{0,8},{8,0},{16,24},{24,16},{1,9},{9,1},{17,25},{25,17},{2,10},{10... | collective-permute-start | bytes 307208 | tf_op jit(solution)/shard_map/ppermute | solution.py:375
  120.2 7.6 %collective-permute-start.37 = (f32[200,128]{1,0:T(8,128)S(1)}, f32[200,128]{1,0:T(8,128)S(1)}, u32[]{:S(2)}, u32[]{:S(2)}) collective-permute-start(f32[200,128]{1,0:T(8,128)S(1)} %get-tuple-element.101), channel_id=1, source_target_pairs={{0,24},{8,16},{16,8},{24,0},{1,25},{9,17},{17,9},{25,1},{2,26},{10... | collective-permute-start | bytes 307208 | tf_op jit(solution)/shard_map/ppermute | solution.py:375
  (16 other events, 194.4 us)

commit v5 on v4

--- a/solution.py
+++ b/solution.py
@@ -475,7 +475,7 @@
         gathered = jnp.concatenate(values, axis=1)
         return mm(gathered, columns[0]), mm(gathered, columns[2]), gathered
 
-    upward, downward, gathered = sums([b[:begin] for b in first_blocks])
+    upward, downward, gathered = sums(first_blocks)
     _, _, *second_blocks = lax.optimization_barrier((upward, downward, *second_blocks))
     from_below, from_above = sent(upward, downward)
     applied = mm(gathered, columns[1]) + from_below + from_above
@@ -483,7 +483,7 @@
     from_below, from_above = sent(upward, downward)
     applied_second = mm(gathered, columns[1]) + from_below + from_above
     sketch_half = jnp.concatenate([applied[:split], applied_second], axis=0) + sketch_shift * omega_half
-    image_rhs = applied[split:] + noise_variance * rhs
+    image_rhs = applied[split:begin] + noise_variance * rhs
 
     count = half // TILE
     matrix_rows = (count * (count + 1) // 2 + count * count // 2) * TILE

time: 143 us -> 144 us (level)
  starting transfers between devices: 45.3 us -> 47.5 us
    ppermute x31, starting transfers between devices: 31.7 us -> 35.9 us  [swapped(): return lax.ppermute(values, axis, [(i, i ^ mask) for i in range(size)])]
    ppermute x31, waiting for transfers between devices: 20.7 us -> 17.8 us  [swapped(): return lax.ppermute(values, axis, [(i, i ^ mask) for i in range(size)])]
  transfers between devices with their start and end apart: 38 -> 38, of which waited for: 14 -> 16; matrix products, arithmetic and copies ran while one was open for 12% -> 12% of each run, Pallas kernels for 21% -> 21%
where the time goes in v5:
time: 144 us
  starting transfers between devices  47.5 us (33%)
  Pallas kernels  35.2 us (24%)
  waiting for transfers between devices  25.8 us (18%)
  matrix products  14.6 us (10%)
  blocking collectives  12.3 us (9%)
  other arithmetic  4.58 us (3%)
  local copies, waits for them, and re-layouts  2.62 us (2%)
    ppermute x31, starting transfers between devices, swapped(): return lax.ppermute(values, axis, [(i, i ^ mask) for i in range(size)])  35.9 us
    pallas_call x4, Pallas kernels, kernel_call(): pl.pallas_call(kernel, out_shape=tuple((jax.ShapeDtypeStruct(shape, jnp.f...  33.4 us
    ppermute x31, waiting for transfers between devices, swapped(): return lax.ppermute(values, axis, [(i, i ^ mask) for i in range(size)])  17.8 us
    dot_general x18, matrix products, mm(): jnp.dot(left, right, precision=HIGHEST, preferred_element_type=jnp.float32)  14.1 us
    all_to_all x1, blocking collectives, exchange(): return lax.all_to_all(values, POINT_AXES, 0, 0, tiled=True)  12.3 us
    ppermute x6, starting transfers between devices, shifted(): lax.ppermute(values, axis, [(i, (i + distance) % size) for i in range(siz...  9.61 us
    ppermute x6, waiting for transfers between devices, shifted(): lax.ppermute(values, axis, [(i, (i + distance) % size) for i in range(siz...  6.49 us
  transfers between devices with their start and end apart: 38, of which 16 were waited for; matrix products, arithmetic and copies ran while one was open for 12% of the time, Pallas kernels for 21%

profile of v5, /device:TPU:0, one launch (start us, length us, event | category | flops | bytes accessed | tf_op | source)
XLA Modules:
  0.0 144.0 jit_solution(276284397244863422)
XLA Ops:
  0.6 1.9 %prepare.1 = (f32[168,256]{1,0:T(8,128)}, f32[128,256]{1,0:T(8,128)}, f32[8,256]{1,0:T(8,128)}, f32[256,256]{1,0:T(8,128)}, f32[32,256]{1,0:T(8,128)}) custom-call(s32[1]{0:T(128)} %bitcast.core_ref, f32[3,256]{1,0:T(4,128)} %points_ref.1, s32[1,8]{1,0:T(1,128)} %neighbors_ref.1, f32[512,256]{1,0:T(8,128)} %omega_ref.1, f32[1,256]{1,0:T(1,128)} %bitcast.130, ...), custom_call_target="tpu_custom_call" | custom-call | flops 1000000 | bytes 524288 | tf_op jit(solution)/shard_map/prepare/pallas_call | solution.py:290
  2.5 3.0 %collective-permute-start = (f32[168,256]{1,0:T(8,128)}, f32[168,256]{1,0:T(8,128)S(1)}, u32[]{:S(2)}, u32[]{:S(2)}) collective-permute-start(f32[168,256]{1,0:T(8,128)} %get-tuple-element.45), channel_id=1, source_target_pairs={{0,2},{2,0},{4,6},{6,4},{1,3},{3,1},{5,7},{7,5},{8,10},{10,8},{12,... | collective-permute-start | bytes 516104 | tf_op jit(solution)/shard_map/ppermute | solution.py:375
  5.5 1.5 %collective-permute-start.1 = (f32[168,256]{1,0:T(8,128)}, f32[168,256]{1,0:T(8,128)S(1)}, u32[]{:S(2)}, u32[]{:S(2)}) collective-permute-start(f32[168,256]{1,0:T(8,128)} %get-tuple-element.45), channel_id=1, source_target_pairs={{0,4},{2,6},{4,0},{6,2},{1,5},{3,7},{5,1},{7,3},{8,12},{10,14},{12... | collective-permute-start | bytes 516104 | tf_op jit(solution)/shard_map/ppermute | solution.py:375
  7.0 2.0 %collective-permute-start.3 = (f32[8,256]{1,0:T(8,128)}, f32[8,256]{1,0:T(8,128)S(1)}, u32[]{:S(2)}, u32[]{:S(2)}) collective-permute-start(f32[8,256]{1,0:T(8,128)} %get-tuple-element.46.refs_1_), channel_id=1, source_target_pairs={{0,8},{1,25},{8,16},{9,1},{16,24},{17,9},{24,0},{25,17},{2,10},{3,... | collective-permute-start | bytes 24584 | tf_op jit(solution)/shard_map/ppermute | solution.py:442
  9.1 1.5 %collective-permute-start.7 = (f32[128,256]{1,0:T(8,128)}, f32[128,256]{1,0:T(8,128)S(1)}, u32[]{:S(2)}, u32[]{:S(2)}) collective-permute-start(f32[128,256]{1,0:T(8,128)} %get-tuple-element.54), channel_id=1, source_target_pairs={{0,2},{2,0},{4,6},{6,4},{1,3},{3,1},{5,7},{7,5},{8,10},{10,8},{12,... | collective-permute-start | bytes 393224 | tf_op jit(solution)/shard_map/ppermute | solution.py:375
  14.1 1.7 %collective-permute-start.8 = (f32[128,256]{1,0:T(8,128)}, f32[128,256]{1,0:T(8,128)S(1)}, u32[]{:S(2)}, u32[]{:S(2)}) collective-permute-start(f32[128,256]{1,0:T(8,128)} %get-tuple-element.54), channel_id=1, source_target_pairs={{0,4},{2,6},{4,0},{6,2},{1,5},{3,7},{5,1},{7,3},{8,12},{10,14},{12... | collective-permute-start | bytes 393224 | tf_op jit(solution)/shard_map/ppermute | solution.py:375
  17.2 1.5 %collective-permute-start.9 = (f32[128,256]{1,0:T(8,128)}, f32[128,256]{1,0:T(8,128)S(1)}, u32[]{:S(2)}, u32[]{:S(2)}) collective-permute-start(f32[128,256]{1,0:T(8,128)} %get-tuple-element.54), channel_id=1, source_target_pairs={{0,6},{2,4},{4,2},{6,0},{1,7},{3,5},{5,3},{7,1},{8,14},{10,12},{12... | collective-permute-start | bytes 393224 | tf_op jit(solution)/shard_map/ppermute | solution.py:375
  21.2 1.9 %collective-permute-start.6 = (f32[168,256]{1,0:T(8,128)S(1)}, f32[168,256]{1,0:T(8,128)S(1)}, u32[]{:S(2)}, u32[]{:S(2)}) collective-permute-start(f32[168,256]{1,0:T(8,128)S(1)} %fusion.61), channel_id=1, source_target_pairs={{0,24},{8,0},{16,8},{24,16},{1,25},{9,1},{17,9},{25,17},{2,26},{10... | collective-permute-start | bytes 516104 | tf_op jit(solution)/shard_map/ppermute | solution.py:370
  26.5 3.8 %collective-permute-start.11 = (f32[128,256]{1,0:T(8,128)S(1)}, f32[128,256]{1,0:T(8,128)S(1)}, u32[]{:S(2)}, u32[]{:S(2)}) collective-permute-start(f32[128,256]{1,0:T(8,128)S(1)} %fusion.63), channel_id=1, source_target_pairs={{0,24},{8,0},{16,8},{24,16},{1,25},{9,1},{17,9},{25,17},{2,26},{10... | collective-permute-start | bytes 393224 | tf_op jit(solution)/shard_map/ppermute | solution.py:370
  31.3 5.3 %collective-permute-done.10 = f32[128,256]{1,0:T(8,128)S(1)} collective-permute-done((f32[128,256]{1,0:T(8,128)S(1)}, f32[128,256]{1,0:T(8,128)S(1)}, u32[]{:S(2)}, u32[]{:S(2)}) %collective-permute-start.10) | collective-permute-done | bytes 131104 | tf_op jit(solution)/shard_map/ppermute | solution.py:370
  40.9 1.6 %payload.1 = (f32[512,256]{1,0:T(8,128)S(1)}, f32[192,128]{1,0:T(8,128)S(1)}, f32[192,128]{1,0:T(8,128)S(1)}, f32[192,128]{1,0:T(8,128)S(1)}, f32[192,128]{1,0:T(8,128)S(1)}) custom-call(s32[2]{0:T(128)S(1)} %pad_add_fusion.place_ref, f32[256,256]{1,0:T(8,128)S(1)} %copy-done.1, f32[256,256]{1,0:T(8,128)S(1)} %maximum_add_fusion.own_ref, ...), custom_call_target="tpu_custom_call" | custom-call | flops 1000000000 | bytes 1048576 | tf_op jit(solution)/shard_map/payload/pallas_call | solution.py:356
  43.2 1.5 %collective-permute-start.14 = (f32[192,128]{1,0:T(8,128)S(1)}, f32[192,128]{1,0:T(8,128)S(1)}, u32[]{:S(2)}, u32[]{:S(2)}) collective-permute-start(f32[192,128]{1,0:T(8,128)S(1)} %get-tuple-element.65), channel_id=1, source_target_pairs={{0,4},{2,6},{4,0},{6,2},{1,5},{3,7},{5,1},{7,3},{8,12},{10,14},{12... | collective-permute-start | bytes 294920 | tf_op jit(solution)/shard_map/ppermute | solution.py:375
  46.2 1.5 %collective-permute-start.23 = (f32[256,256]{1,0:T(8,128)S(1)}, f32[256,256]{1,0:T(8,128)S(1)}, u32[]{:S(2)}, u32[]{:S(2)}) collective-permute-start(f32[256,256]{1,0:T(8,128)S(1)} %maximum_add_fusion.own_ref), channel_id=1, source_target_pairs={{0,4},{2,6},{4,0},{6,2},{1,5},{3,7},{5,1},{7,3},{8,12},{10,14},{12... | collective-permute-start | bytes 786440 | tf_op jit(solution)/shard_map/ppermute | solution.py:375
  48.2 6.6 %collective-permute-done.14 = f32[192,128]{1,0:T(8,128)S(1)} collective-permute-done((f32[192,128]{1,0:T(8,128)S(1)}, f32[192,128]{1,0:T(8,128)S(1)}, u32[]{:S(2)}, u32[]{:S(2)}) %collective-permute-start.14) | collective-permute-done | bytes 98336 | tf_op jit(solution)/shard_map/ppermute | solution.py:375
  55.6 2.2 %collective-permute-start.17 = (f32[192,128]{1,0:T(8,128)S(1)}, f32[192,128]{1,0:T(8,128)S(1)}, u32[]{:S(2)}, u32[]{:S(2)}) collective-permute-start(f32[192,128]{1,0:T(8,128)S(1)} %add_add_fusion.2), channel_id=1, source_target_pairs={{0,16},{8,24},{16,0},{24,8},{1,17},{9,25},{17,1},{25,9},{2,18},{10... | collective-permute-start | bytes 294920 | tf_op jit(solution)/shard_map/ppermute | solution.py:375
  57.8 1.5 %collective-permute-start.18 = (f32[192,128]{1,0:T(8,128)S(1)}, f32[192,128]{1,0:T(8,128)S(1)}, u32[]{:S(2)}, u32[]{:S(2)}) collective-permute-start(f32[192,128]{1,0:T(8,128)S(1)} %add_add_fusion.2), channel_id=1, source_target_pairs={{0,24},{8,16},{16,8},{24,0},{1,25},{9,17},{17,9},{25,1},{2,26},{10... | collective-permute-start | bytes 294920 | tf_op jit(solution)/shard_map/ppermute | solution.py:375
  59.5 2.7 %collective-permute-start.22 = (f32[256,256]{1,0:T(8,128)S(1)}, f32[256,256]{1,0:T(8,128)S(1)}, u32[]{:S(2)}, u32[]{:S(2)}) collective-permute-start(f32[256,256]{1,0:T(8,128)S(1)} %maximum_add_fusion.own_ref), channel_id=1, source_target_pairs={{0,2},{2,0},{4,6},{6,4},{1,3},{3,1},{5,7},{7,5},{8,10},{10,8},{12,... | collective-permute-start | bytes 786440 | tf_op jit(solution)/shard_map/ppermute | solution.py:375
  62.3 2.0 %collective-permute-done.18 = f32[192,128]{1,0:T(8,128)S(1)} collective-permute-done((f32[192,128]{1,0:T(8,128)S(1)}, f32[192,128]{1,0:T(8,128)S(1)}, u32[]{:S(2)}, u32[]{:S(2)}) %collective-permute-start.18) | collective-permute-done | bytes 98336 | tf_op jit(solution)/shard_map/ppermute | solution.py:375
  64.3 2.8 %collective-permute-start.19 = (f32[192,128]{1,0:T(8,128)S(1)}, f32[192,128]{1,0:T(8,128)S(1)}, u32[]{:S(2)}, u32[]{:S(2)}) collective-permute-start(f32[192,128]{1,0:T(8,128)S(1)} %add_add_fusion.1.refs_0_), channel_id=1, source_target_pairs={{0,2},{2,0},{4,6},{6,4},{1,3},{3,1},{5,7},{7,5},{8,10},{10,8},{12,... | collective-permute-start | bytes 294920 | tf_op jit(solution)/shard_map/ppermute | solution.py:375
  67.1 2.0 %collective-permute-start.20 = (f32[192,128]{1,0:T(8,128)S(1)}, f32[192,128]{1,0:T(8,128)S(1)}, u32[]{:S(2)}, u32[]{:S(2)}) collective-permute-start(f32[192,128]{1,0:T(8,128)S(1)} %add_add_fusion.1.refs_0_), channel_id=1, source_target_pairs={{0,4},{2,6},{4,0},{6,2},{1,5},{3,7},{5,1},{7,3},{8,12},{10,14},{12... | collective-permute-start | bytes 294920 | tf_op jit(solution)/shard_map/ppermute | solution.py:375
  72.8 1.7 %collective-permute-done.21.refs_3_ = f32[192,128]{1,0:T(8,128)S(1)} collective-permute-done((f32[192,128]{1,0:T(8,128)S(1)}, f32[192,128]{1,0:T(8,128)S(1)}, u32[]{:S(2)}, u32[]{:S(2)}) %collective-permute-start.21) | collective-permute-done | bytes 98336 | tf_op jit(solution)/shard_map/ppermute | solution.py:375
  75.9 3.5 %collective-permute-start.26 = (f32[256,256]{1,0:T(8,128)S(1)}, f32[256,256]{1,0:T(8,128)S(1)}, u32[]{:S(2)}, u32[]{:S(2)}) collective-permute-start(f32[256,256]{1,0:T(8,128)S(1)} %convolution_add_fusion.2), channel_id=1, source_target_pairs={{0,24},{8,0},{16,8},{24,16},{1,25},{9,1},{17,9},{25,17},{2,26},{10... | collective-permute-start | bytes 786440 | tf_op jit(solution)/shard_map/ppermute | solution.py:370
  79.4 29.8 %inverse_and_solve.1 = (f32[512,512]{1,0:T(8,128)S(1)}, f32[512,512]{1,0:T(8,128)S(1)}, f32[32,512]{1,0:T(8,128)S(1)}) custom-call(s32[2]{0:T(128)S(1)} %pad_add_fusion.place_ref, f32[192,128]{1,0:T(8,128)S(1)} %add_add_fusion.1.refs_0_, f32[192,128]{1,0:T(8,128)S(1)} %collective-permute-done.19.refs_1_, f32[192,128]{1,0:T(8,128)S(1)} %collective-permute-done.20.refs_2_, ...), custom_call_target="tpu_custom_call" | custom-call | flops 30000001024 | bytes 1048576 | tf_op jit(solution)/shard_map/inverse_and_solve/pallas_call | solution.py:356
  109.4 1.5 %collective-permute-done.31.other_ref = f32[256,256]{1,0:T(8,128)S(1)} collective-permute-done((f32[256,256]{1,0:T(8,128)S(1)}, f32[256,256]{1,0:T(8,128)S(1)}, u32[]{:S(2)}, u32[]{:S(2)}) %collective-permute-start.31) | collective-permute-done | bytes 262176 | tf_op jit(solution)/shard_map/ppermute | solution.py:375
  112.3 1.8 %collective-permute-start.33 = (f32[200,128]{1,0:T(8,128)S(1)}, f32[200,128]{1,0:T(8,128)S(1)}, u32[]{:S(2)}, u32[]{:S(2)}) collective-permute-start(f32[200,128]{1,0:T(8,128)S(1)} %get-tuple-element.80), channel_id=1, source_target_pairs={{0,4},{2,6},{4,0},{6,2},{1,5},{3,7},{5,1},{7,3},{8,12},{10,14},{12... | collective-permute-start | bytes 307208 | tf_op jit(solution)/shard_map/ppermute | solution.py:375
  114.1 1.6 %collective-permute-start.34 = (f32[200,128]{1,0:T(8,128)S(1)}, f32[200,128]{1,0:T(8,128)S(1)}, u32[]{:S(2)}, u32[]{:S(2)}) collective-permute-start(f32[200,128]{1,0:T(8,128)S(1)} %get-tuple-element.80), channel_id=1, source_target_pairs={{0,6},{2,4},{4,2},{6,0},{1,7},{3,5},{5,3},{7,1},{8,14},{10,12},{12... | collective-permute-start | bytes 307208 | tf_op jit(solution)/shard_map/ppermute | solution.py:375
  115.8 1.8 %fusion.65 = f32[512,512]{1,0:T(8,128)S(1)} fusion(f32[512,512]{1,0:T(8,128)S(1)} %get-tuple-element.83, f32[512,512]{1,0:T(8,128)S(1)} %get-tuple-element.84), kind=kOutput, calls=%fused_computation.146 | convolution fusion | flops 1610612736 | bytes 3145728 | tf_op jit(solution)/shard_map/dot_general | solution.py:20
  117.6 1.9 %convolution_subtract_fusion = bf16[512,512]{1,0:T(8,128)(2,1)S(1)} fusion(f32[512,512]{1,0:T(8,128)S(1)} %get-tuple-element.84, f32[512,512]{1,0:T(8,128)S(1)} %get-tuple-element.85, f32[512,512]{1,0:T(8,128)S(1)} %fusion.65), kind=kOutput, calls=%fused_computation.10 | convolution fusion | flops 1611137024 | bytes 3670016 | tf_op jit(solution)/shard_map/dot_general | solution.py:20
  121.7 3.8 %collective-permute-start.37 = (f32[200,128]{1,0:T(8,128)S(1)}, f32[200,128]{1,0:T(8,128)S(1)}, u32[]{:S(2)}, u32[]{:S(2)}) collective-permute-start(f32[200,128]{1,0:T(8,128)S(1)} %get-tuple-element.101), channel_id=1, source_target_pairs={{0,24},{8,16},{16,8},{24,0},{1,25},{9,17},{17,9},{25,1},{2,26},{10... | collective-permute-start | bytes 307208 | tf_op jit(solution)/shard_map/ppermute | solution.py:375
  126.2 1.5 %collective-permute-done.35 = f32[200,128]{1,0:T(8,128)S(1)} collective-permute-done((f32[200,128]{1,0:T(8,128)S(1)}, f32[200,128]{1,0:T(8,128)S(1)}, u32[]{:S(2)}, u32[]{:S(2)}) %collective-permute-start.35) | collective-permute-done | bytes 102432 | tf_op jit(solution)/shard_map/ppermute | solution.py:375
  127.7 1.7 %collective-permute-done.37 = f32[200,128]{1,0:T(8,128)S(1)} collective-permute-done((f32[200,128]{1,0:T(8,128)S(1)}, f32[200,128]{1,0:T(8,128)S(1)}, u32[]{:S(2)}, u32[]{:S(2)}) %collective-permute-start.37) | collective-permute-done | bytes 102432 | tf_op jit(solution)/shard_map/ppermute | solution.py:375
  130.9 12.3 %all_to_all.6 = f32[16,8,128]{2,1,0:T(8,128)S(1)} all-to-all(f32[16,8,128]{2,1,0:T(8,128)S(1)} %broadcast_in_dim.5), channel_id=1, replica_groups=mesh['blk'=4,'leaf'=4,'samp'=2] {'blk','leaf'}, dimensions={0} | all-to-all | bytes 131072 | tf_op jit(solution)/shard_map/all_to_all | solution.py:387
  (140 shorter events, 31.0 us)
Async XLA Ops:
  2.5 14.7 %collective-permute-start = (f32[168,256]{1,0:T(8,128)}, f32[168,256]{1,0:T(8,128)S(1)}, u32[]{:S(2)}, u32[]{:S(2)}) collective-permute-start(f32[168,256]{1,0:T(8,128)} %get-tuple-element.45), channel_id=1, source_target_pairs={{0,2},{2,0},{4,6},{6,4},{1,3},{3,1},{5,7},{7,5},{8,10},{10,8},{12,... | collective-permute-start | bytes 516104 | tf_op jit(solution)/shard_map/ppermute | solution.py:375
  5.5 13.2 %collective-permute-start.1 = (f32[168,256]{1,0:T(8,128)}, f32[168,256]{1,0:T(8,128)S(1)}, u32[]{:S(2)}, u32[]{:S(2)}) collective-permute-start(f32[168,256]{1,0:T(8,128)} %get-tuple-element.45), channel_id=1, source_target_pairs={{0,4},{2,6},{4,0},{6,2},{1,5},{3,7},{5,1},{7,3},{8,12},{10,14},{12... | collective-permute-start | bytes 516104 | tf_op jit(solution)/shard_map/ppermute | solution.py:375
  7.0 11.7 %collective-permute-start.2 = (f32[168,256]{1,0:T(8,128)}, f32[168,256]{1,0:T(8,128)S(1)}, u32[]{:S(2)}, u32[]{:S(2)}) collective-permute-start(f32[168,256]{1,0:T(8,128)} %get-tuple-element.45), channel_id=1, source_target_pairs={{0,6},{2,4},{4,2},{6,0},{1,7},{3,5},{5,3},{7,1},{8,14},{10,12},{12... | collective-permute-start | bytes 516104 | tf_op jit(solution)/shard_map/ppermute | solution.py:375
  7.0 5.9 %collective-permute-start.3 = (f32[8,256]{1,0:T(8,128)}, f32[8,256]{1,0:T(8,128)S(1)}, u32[]{:S(2)}, u32[]{:S(2)}) collective-permute-start(f32[8,256]{1,0:T(8,128)} %get-tuple-element.46.refs_1_), channel_id=1, source_target_pairs={{0,8},{1,25},{8,16},{9,1},{16,24},{17,9},{24,0},{25,17},{2,10},{3,... | collective-permute-start | bytes 24584 | tf_op jit(solution)/shard_map/ppermute | solution.py:442
  9.1 16.0 %collective-permute-start.7 = (f32[128,256]{1,0:T(8,128)}, f32[128,256]{1,0:T(8,128)S(1)}, u32[]{:S(2)}, u32[]{:S(2)}) collective-permute-start(f32[128,256]{1,0:T(8,128)} %get-tuple-element.54), channel_id=1, source_target_pairs={{0,2},{2,0},{4,6},{6,4},{1,3},{3,1},{5,7},{7,5},{8,10},{10,8},{12,... | collective-permute-start | bytes 393224 | tf_op jit(solution)/shard_map/ppermute | solution.py:375
  14.1 11.0 %collective-permute-start.8 = (f32[128,256]{1,0:T(8,128)}, f32[128,256]{1,0:T(8,128)S(1)}, u32[]{:S(2)}, u32[]{:S(2)}) collective-permute-start(f32[128,256]{1,0:T(8,128)} %get-tuple-element.54), channel_id=1, source_target_pairs={{0,4},{2,6},{4,0},{6,2},{1,5},{3,7},{5,1},{7,3},{8,12},{10,14},{12... | collective-permute-start | bytes 393224 | tf_op jit(solution)/shard_map/ppermute | solution.py:375
  17.2 7.9 %collective-permute-start.9 = (f32[128,256]{1,0:T(8,128)}, f32[128,256]{1,0:T(8,128)S(1)}, u32[]{:S(2)}, u32[]{:S(2)}) collective-permute-start(f32[128,256]{1,0:T(8,128)} %get-tuple-element.54), channel_id=1, source_target_pairs={{0,6},{2,4},{4,2},{6,0},{1,7},{3,5},{5,3},{7,1},{8,14},{10,12},{12... | collective-permute-start | bytes 393224 | tf_op jit(solution)/shard_map/ppermute | solution.py:375
  21.2 17.3 %collective-permute-start.6 = (f32[168,256]{1,0:T(8,128)S(1)}, f32[168,256]{1,0:T(8,128)S(1)}, u32[]{:S(2)}, u32[]{:S(2)}) collective-permute-start(f32[168,256]{1,0:T(8,128)S(1)} %fusion.61), channel_id=1, source_target_pairs={{0,24},{8,0},{16,8},{24,16},{1,25},{9,1},{17,9},{25,17},{2,26},{10... | collective-permute-start | bytes 516104 | tf_op jit(solution)/shard_map/ppermute | solution.py:370
  24.8 13.7 %collective-permute-start.5 = (f32[168,256]{1,0:T(8,128)S(1)}, f32[168,256]{1,0:T(8,128)S(1)}, u32[]{:S(2)}, u32[]{:S(2)}) collective-permute-start(f32[168,256]{1,0:T(8,128)S(1)} %fusion.60), channel_id=1, source_target_pairs={{0,8},{8,16},{16,24},{24,0},{1,9},{9,17},{17,25},{25,1},{2,10},{10... | collective-permute-start | bytes 516104 | tf_op jit(solution)/shard_map/ppermute | solution.py:370
  26.5 10.2 %collective-permute-start.10 = (f32[128,256]{1,0:T(8,128)S(1)}, f32[128,256]{1,0:T(8,128)S(1)}, u32[]{:S(2)}, u32[]{:S(2)}) collective-permute-start(f32[128,256]{1,0:T(8,128)S(1)} %fusion.62), channel_id=1, source_target_pairs={{0,8},{8,16},{16,24},{24,0},{1,9},{9,17},{17,25},{25,1},{2,10},{10... | collective-permute-start | bytes 393224 | tf_op jit(solution)/shard_map/ppermute | solution.py:370
  26.5 11.3 %collective-permute-start.11 = (f32[128,256]{1,0:T(8,128)S(1)}, f32[128,256]{1,0:T(8,128)S(1)}, u32[]{:S(2)}, u32[]{:S(2)}) collective-permute-start(f32[128,256]{1,0:T(8,128)S(1)} %fusion.63), channel_id=1, source_target_pairs={{0,24},{8,0},{16,8},{24,16},{1,25},{9,1},{17,9},{25,17},{2,26},{10... | collective-permute-start | bytes 393224 | tf_op jit(solution)/shard_map/ppermute | solution.py:370
  42.6 5.6 %collective-permute-start.13 = (f32[192,128]{1,0:T(8,128)S(1)}, f32[192,128]{1,0:T(8,128)S(1)}, u32[]{:S(2)}, u32[]{:S(2)}) collective-permute-start(f32[192,128]{1,0:T(8,128)S(1)} %get-tuple-element.64), channel_id=1, source_target_pairs={{0,2},{2,0},{4,6},{6,4},{1,3},{3,1},{5,7},{7,5},{8,10},{10,8},{12,... | collective-permute-start | bytes 294920 | tf_op jit(solution)/shard_map/ppermute | solution.py:375
  43.2 11.6 %collective-permute-start.14 = (f32[192,128]{1,0:T(8,128)S(1)}, f32[192,128]{1,0:T(8,128)S(1)}, u32[]{:S(2)}, u32[]{:S(2)}) collective-permute-start(f32[192,128]{1,0:T(8,128)S(1)} %get-tuple-element.65), channel_id=1, source_target_pairs={{0,4},{2,6},{4,0},{6,2},{1,5},{3,7},{5,1},{7,3},{8,12},{10,14},{12... | collective-permute-start | bytes 294920 | tf_op jit(solution)/shard_map/ppermute | solution.py:375
  44.7 10.1 %collective-permute-start.15 = (f32[192,128]{1,0:T(8,128)S(1)}, f32[192,128]{1,0:T(8,128)S(1)}, u32[]{:S(2)}, u32[]{:S(2)}) collective-permute-start(f32[192,128]{1,0:T(8,128)S(1)} %get-tuple-element.66), channel_id=1, source_target_pairs={{0,6},{2,4},{4,2},{6,0},{1,7},{3,5},{5,3},{7,1},{8,14},{10,12},{12... | collective-permute-start | bytes 294920 | tf_op jit(solution)/shard_map/ppermute | solution.py:375
  46.2 22.9 %collective-permute-start.23 = (f32[256,256]{1,0:T(8,128)S(1)}, f32[256,256]{1,0:T(8,128)S(1)}, u32[]{:S(2)}, u32[]{:S(2)}) collective-permute-start(f32[256,256]{1,0:T(8,128)S(1)} %maximum_add_fusion.own_ref), channel_id=1, source_target_pairs={{0,4},{2,6},{4,0},{6,2},{1,5},{3,7},{5,1},{7,3},{8,12},{10,14},{12... | collective-permute-start | bytes 786440 | tf_op jit(solution)/shard_map/ppermute | solution.py:375
  47.7 21.4 %collective-permute-start.24 = (f32[256,256]{1,0:T(8,128)S(1)}, f32[256,256]{1,0:T(8,128)S(1)}, u32[]{:S(2)}, u32[]{:S(2)}) collective-permute-start(f32[256,256]{1,0:T(8,128)S(1)} %maximum_add_fusion.own_ref), channel_id=1, source_target_pairs={{0,6},{2,4},{4,2},{6,0},{1,7},{3,5},{5,3},{7,1},{8,14},{10,12},{12... | collective-permute-start | bytes 786440 | tf_op jit(solution)/shard_map/ppermute | solution.py:375
  54.9 4.7 %collective-permute-start.16 = (f32[192,128]{1,0:T(8,128)S(1)}, f32[192,128]{1,0:T(8,128)S(1)}, u32[]{:S(2)}, u32[]{:S(2)}) collective-permute-start(f32[192,128]{1,0:T(8,128)S(1)} %add_add_fusion.2), channel_id=1, source_target_pairs={{0,8},{8,0},{16,24},{24,16},{1,9},{9,1},{17,25},{25,17},{2,10},{10... | collective-permute-start | bytes 294920 | tf_op jit(solution)/shard_map/ppermute | solution.py:375
  55.6 6.6 %collective-permute-start.17 = (f32[192,128]{1,0:T(8,128)S(1)}, f32[192,128]{1,0:T(8,128)S(1)}, u32[]{:S(2)}, u32[]{:S(2)}) collective-permute-start(f32[192,128]{1,0:T(8,128)S(1)} %add_add_fusion.2), channel_id=1, source_target_pairs={{0,16},{8,24},{16,0},{24,8},{1,17},{9,25},{17,1},{25,9},{2,18},{10... | collective-permute-start | bytes 294920 | tf_op jit(solution)/shard_map/ppermute | solution.py:375
  57.8 6.5 %collective-permute-start.18 = (f32[192,128]{1,0:T(8,128)S(1)}, f32[192,128]{1,0:T(8,128)S(1)}, u32[]{:S(2)}, u32[]{:S(2)}) collective-permute-start(f32[192,128]{1,0:T(8,128)S(1)} %add_add_fusion.2), channel_id=1, source_target_pairs={{0,24},{8,16},{16,8},{24,0},{1,25},{9,17},{17,9},{25,1},{2,26},{10... | collective-permute-start | bytes 294920 | tf_op jit(solution)/shard_map/ppermute | solution.py:375
  59.5 11.4 %collective-permute-start.22 = (f32[256,256]{1,0:T(8,128)S(1)}, f32[256,256]{1,0:T(8,128)S(1)}, u32[]{:S(2)}, u32[]{:S(2)}) collective-permute-start(f32[256,256]{1,0:T(8,128)S(1)} %maximum_add_fusion.own_ref), channel_id=1, source_target_pairs={{0,2},{2,0},{4,6},{6,4},{1,3},{3,1},{5,7},{7,5},{8,10},{10,8},{12,... | collective-permute-start | bytes 786440 | tf_op jit(solution)/shard_map/ppermute | solution.py:375
  64.3 8.5 %collective-permute-start.19 = (f32[192,128]{1,0:T(8,128)S(1)}, f32[192,128]{1,0:T(8,128)S(1)}, u32[]{:S(2)}, u32[]{:S(2)}) collective-permute-start(f32[192,128]{1,0:T(8,128)S(1)} %add_add_fusion.1.refs_0_), channel_id=1, source_target_pairs={{0,2},{2,0},{4,6},{6,4},{1,3},{3,1},{5,7},{7,5},{8,10},{10,8},{12,... | collective-permute-start | bytes 294920 | tf_op jit(solution)/shard_map/ppermute | solution.py:375
  67.1 5.8 %collective-permute-start.20 = (f32[192,128]{1,0:T(8,128)S(1)}, f32[192,128]{1,0:T(8,128)S(1)}, u32[]{:S(2)}, u32[]{:S(2)}) collective-permute-start(f32[192,128]{1,0:T(8,128)S(1)} %add_add_fusion.1.refs_0_), channel_id=1, source_target_pairs={{0,4},{2,6},{4,0},{6,2},{1,5},{3,7},{5,1},{7,3},{8,12},{10,14},{12... | collective-permute-start | bytes 294920 | tf_op jit(solution)/shard_map/ppermute | solution.py:375
  69.0 5.5 %collective-permute-start.21 = (f32[192,128]{1,0:T(8,128)S(1)}, f32[192,128]{1,0:T(8,128)S(1)}, u32[]{:S(2)}, u32[]{:S(2)}) collective-permute-start(f32[192,128]{1,0:T(8,128)S(1)} %add_add_fusion.1.refs_0_), channel_id=1, source_target_pairs={{0,6},{2,4},{4,2},{6,0},{1,7},{3,5},{5,3},{7,1},{8,14},{10,12},{12... | collective-permute-start | bytes 294920 | tf_op jit(solution)/shard_map/ppermute | solution.py:375
  74.6 4.9 %collective-permute-start.28 = (f32[192,128]{1,0:T(8,128)S(1)}, f32[192,128]{1,0:T(8,128)S(1)}, u32[]{:S(2)}, u32[]{:S(2)}) collective-permute-start(f32[192,128]{1,0:T(8,128)S(1)} %collective-permute-done.19.refs_1_), channel_id=1, source_target_pairs={{0,1},{1,0},{2,3},{3,2},{4,5},{5,4},{6,7},{7,6},{8,9},{9,8},{10,11... | collective-permute-start | bytes 294920 | tf_op jit(solution)/shard_map/ppermute | solution.py:375
  75.6 33.6 %collective-permute-start.25 = (f32[256,256]{1,0:T(8,128)S(1)}, f32[256,256]{1,0:T(8,128)S(1)}, u32[]{:S(2)}, u32[]{:S(2)}) collective-permute-start(f32[256,256]{1,0:T(8,128)S(1)} %convolution_add_fusion.3), channel_id=1, source_target_pairs={{0,8},{8,16},{16,24},{24,0},{1,9},{9,17},{17,25},{25,1},{2,10},{10... | collective-permute-start | bytes 786440 | tf_op jit(solution)/shard_map/ppermute | solution.py:370
  75.9 33.4 %collective-permute-start.26 = (f32[256,256]{1,0:T(8,128)S(1)}, f32[256,256]{1,0:T(8,128)S(1)}, u32[]{:S(2)}, u32[]{:S(2)}) collective-permute-start(f32[256,256]{1,0:T(8,128)S(1)} %convolution_add_fusion.2), channel_id=1, source_target_pairs={{0,24},{8,0},{16,8},{24,16},{1,25},{9,1},{17,9},{25,17},{2,26},{10... | collective-permute-start | bytes 786440 | tf_op jit(solution)/shard_map/ppermute | solution.py:370
  112.2 7.3 %collective-permute-start.32 = (f32[200,128]{1,0:T(8,128)S(1)}, f32[200,128]{1,0:T(8,128)S(1)}, u32[]{:S(2)}, u32[]{:S(2)}) collective-permute-start(f32[200,128]{1,0:T(8,128)S(1)} %get-tuple-element.80), channel_id=1, source_target_pairs={{0,2},{2,0},{4,6},{6,4},{1,3},{3,1},{5,7},{7,5},{8,10},{10,8},{12,... | collective-permute-start | bytes 307208 | tf_op jit(solution)/shard_map/ppermute | solution.py:375
  112.3 7.2 %collective-permute-start.33 = (f32[200,128]{1,0:T(8,128)S(1)}, f32[200,128]{1,0:T(8,128)S(1)}, u32[]{:S(2)}, u32[]{:S(2)}) collective-permute-start(f32[200,128]{1,0:T(8,128)S(1)} %get-tuple-element.80), channel_id=1, source_target_pairs={{0,4},{2,6},{4,0},{6,2},{1,5},{3,7},{5,1},{7,3},{8,12},{10,14},{12... | collective-permute-start | bytes 307208 | tf_op jit(solution)/shard_map/ppermute | solution.py:375
  114.1 5.6 %collective-permute-start.34 = (f32[200,128]{1,0:T(8,128)S(1)}, f32[200,128]{1,0:T(8,128)S(1)}, u32[]{:S(2)}, u32[]{:S(2)}) collective-permute-start(f32[200,128]{1,0:T(8,128)S(1)} %get-tuple-element.80), channel_id=1, source_target_pairs={{0,6},{2,4},{4,2},{6,0},{1,7},{3,5},{5,3},{7,1},{8,14},{10,12},{12... | collective-permute-start | bytes 307208 | tf_op jit(solution)/shard_map/ppermute | solution.py:375
  120.3 5.9 %collective-permute-start.36 = (f32[136,128]{1,0:T(8,128)S(1)}, f32[136,128]{1,0:T(8,128)S(1)}, u32[]{:S(2)}, u32[]{:S(2)}) collective-permute-start(f32[136,128]{1,0:T(8,128)S(1)} %fusion.38), channel_id=1, source_target_pairs={{0,16},{8,24},{16,0},{24,8},{1,17},{9,25},{17,1},{25,9},{2,18},{10... | collective-permute-start | bytes 208904 | tf_op jit(solution)/shard_map/ppermute | solution.py:375
  121.0 6.7 %collective-permute-start.35 = (f32[200,128]{1,0:T(8,128)S(1)}, f32[200,128]{1,0:T(8,128)S(1)}, u32[]{:S(2)}, u32[]{:S(2)}) collective-permute-start(f32[200,128]{1,0:T(8,128)S(1)} %get-tuple-element.100), channel_id=1, source_target_pairs={{0,8},{8,0},{16,24},{24,16},{1,9},{9,1},{17,25},{25,17},{2,10},{10... | collective-permute-start | bytes 307208 | tf_op jit(solution)/shard_map/ppermute | solution.py:375
  121.7 7.7 %collective-permute-start.37 = (f32[200,128]{1,0:T(8,128)S(1)}, f32[200,128]{1,0:T(8,128)S(1)}, u32[]{:S(2)}, u32[]{:S(2)}) collective-permute-start(f32[200,128]{1,0:T(8,128)S(1)} %get-tuple-element.101), channel_id=1, source_target_pairs={{0,24},{8,16},{16,8},{24,0},{1,25},{9,17},{17,9},{25,1},{2,26},{10... | collective-permute-start | bytes 307208 | tf_op jit(solution)/shard_map/ppermute | solution.py:375
  (16 other events, 191.5 us)

commit v6 on v4

--- a/solution.py
+++ b/solution.py
@@ -506,10 +506,8 @@
     for m in range(1, leaves):
         share = share + swapped(shares[m], "leaf", m)
     blocks = slab(late_sketch)
-    near = jnp.concatenate(blocks[: leaves // 2], axis=1)
-    far = jnp.concatenate(blocks[leaves // 2 :], axis=1)
-    cut = near.shape[1]
-    upward, here, downward = (mm(near, c[:cut]) + mm(far, c[cut:]) for c in columns)
+    upward, downward, gathered = sums(blocks)
+    here = mm(gathered, columns[1])
     here = here + noise_variance * late_sketch
     shares = slab(axis_sum(share, "blk"))
     *shares, upward, downward, here = lax.optimization_barrier((*shares, upward, downward, here))

time: 143 us -> 142 us (level)
    dot_general x18 -> x15, matrix products: 14.1 us -> 13.6 us  [mm(): jnp.dot(left, right, precision=HIGHEST, preferred_element_type=jnp.float32)]
where the time goes in v6:
time: 142 us
  starting transfers between devices  45.7 us (32%)
  Pallas kernels  35.2 us (25%)
  waiting for transfers between devices  26.2 us (18%)
  matrix products  14 us (10%)
  blocking collectives  12.3 us (9%)
  other arithmetic  4.57 us (3%)
  local copies, waits for them, and re-layouts  2.61 us (2%)
    pallas_call x4, Pallas kernels, kernel_call(): pl.pallas_call(kernel, out_shape=tuple((jax.ShapeDtypeStruct(shape, jnp.f...  33.4 us
    ppermute x31, starting transfers between devices, swapped(): return lax.ppermute(values, axis, [(i, i ^ mask) for i in range(size)])  32.3 us
    ppermute x31, waiting for transfers between devices, swapped(): return lax.ppermute(values, axis, [(i, i ^ mask) for i in range(size)])  20.4 us
    dot_general x15, matrix products, mm(): jnp.dot(left, right, precision=HIGHEST, preferred_element_type=jnp.float32)  13.6 us
    all_to_all x1, blocking collectives, exchange(): return lax.all_to_all(values, POINT_AXES, 0, 0, tiled=True)  12.3 us
    ppermute x6, starting transfers between devices, shifted(): lax.ppermute(values, axis, [(i, (i + distance) % size) for i in range(siz...  10.3 us
    ppermute x6, waiting for transfers between devices, shifted(): lax.ppermute(values, axis, [(i, (i + distance) % size) for i in range(siz...  5.75 us
    ppermute x1, starting transfers between devices, local(): arrived = lax.ppermute(meta, ('blk', 'samp'), route)  3.08 us
  transfers between devices with their start and end apart: 38, of which 14 were waited for; matrix products, arithmetic and copies ran while one was open for 12% of the time, Pallas kernels for 21%

profile of v6, /device:TPU:0, one launch (start us, length us, event | category | flops | bytes accessed | tf_op | source)
XLA Modules:
  0.0 142.0 jit_solution(5930056743775574189)
XLA Ops:
  0.6 1.9 %prepare.1 = (f32[168,256]{1,0:T(8,128)}, f32[128,256]{1,0:T(8,128)}, f32[8,256]{1,0:T(8,128)}, f32[256,256]{1,0:T(8,128)}, f32[32,256]{1,0:T(8,128)}) custom-call(s32[1]{0:T(128)} %bitcast.core_ref, f32[3,256]{1,0:T(4,128)} %points_ref.1, s32[1,8]{1,0:T(1,128)} %neighbors_ref.1, f32[512,256]{1,0:T(8,128)} %omega_ref.1, f32[1,256]{1,0:T(1,128)} %bitcast.127, ...), custom_call_target="tpu_custom_call" | custom-call | flops 1000000 | bytes 524288 | tf_op jit(solution)/shard_map/prepare/pallas_call | solution.py:290
  2.5 3.1 %collective-permute-start.3 = (f32[8,256]{1,0:T(8,128)}, f32[8,256]{1,0:T(8,128)S(1)}, u32[]{:S(2)}, u32[]{:S(2)}) collective-permute-start(f32[8,256]{1,0:T(8,128)} %get-tuple-element.46.refs_1_), channel_id=1, source_target_pairs={{0,8},{1,25},{8,16},{9,1},{16,24},{17,9},{24,0},{25,17},{2,10},{3,... | collective-permute-start | bytes 24584 | tf_op jit(solution)/shard_map/ppermute | solution.py:442
  5.6 1.5 %collective-permute-start = (f32[168,256]{1,0:T(8,128)}, f32[168,256]{1,0:T(8,128)S(1)}, u32[]{:S(2)}, u32[]{:S(2)}) collective-permute-start(f32[168,256]{1,0:T(8,128)} %get-tuple-element.45), channel_id=1, source_target_pairs={{0,2},{2,0},{4,6},{6,4},{1,3},{3,1},{5,7},{7,5},{8,10},{10,8},{12,... | collective-permute-start | bytes 516104 | tf_op jit(solution)/shard_map/ppermute | solution.py:375
  7.1 1.5 %collective-permute-start.1 = (f32[168,256]{1,0:T(8,128)}, f32[168,256]{1,0:T(8,128)S(1)}, u32[]{:S(2)}, u32[]{:S(2)}) collective-permute-start(f32[168,256]{1,0:T(8,128)} %get-tuple-element.45), channel_id=1, source_target_pairs={{0,4},{2,6},{4,0},{6,2},{1,5},{3,7},{5,1},{7,3},{8,12},{10,14},{12... | collective-permute-start | bytes 516104 | tf_op jit(solution)/shard_map/ppermute | solution.py:375
  9.1 1.5 %collective-permute-start.7 = (f32[128,256]{1,0:T(8,128)}, f32[128,256]{1,0:T(8,128)S(1)}, u32[]{:S(2)}, u32[]{:S(2)}) collective-permute-start(f32[128,256]{1,0:T(8,128)} %get-tuple-element.54), channel_id=1, source_target_pairs={{0,2},{2,0},{4,6},{6,4},{1,3},{3,1},{5,7},{7,5},{8,10},{10,8},{12,... | collective-permute-start | bytes 393224 | tf_op jit(solution)/shard_map/ppermute | solution.py:375
  12.7 1.6 %collective-permute-start.8 = (f32[128,256]{1,0:T(8,128)}, f32[128,256]{1,0:T(8,128)S(1)}, u32[]{:S(2)}, u32[]{:S(2)}) collective-permute-start(f32[128,256]{1,0:T(8,128)} %get-tuple-element.54), channel_id=1, source_target_pairs={{0,4},{2,6},{4,0},{6,2},{1,5},{3,7},{5,1},{7,3},{8,12},{10,14},{12... | collective-permute-start | bytes 393224 | tf_op jit(solution)/shard_map/ppermute | solution.py:375
  16.2 1.2 collective-permute-done.1
  19.9 2.6 %collective-permute-start.6 = (f32[160,256]{1,0:T(8,128)S(1)}, f32[160,256]{1,0:T(8,128)S(1)}, u32[]{:S(2)}, u32[]{:S(2)}) collective-permute-start(f32[160,256]{1,0:T(8,128)S(1)} %fusion.25), channel_id=1, source_target_pairs={{0,24},{8,0},{16,8},{24,16},{1,25},{9,1},{17,9},{25,17},{2,26},{10... | collective-permute-start | bytes 491528 | tf_op jit(solution)/shard_map/ppermute | solution.py:370
  26.5 3.3 %collective-permute-start.11 = (f32[128,256]{1,0:T(8,128)S(1)}, f32[128,256]{1,0:T(8,128)S(1)}, u32[]{:S(2)}, u32[]{:S(2)}) collective-permute-start(f32[128,256]{1,0:T(8,128)S(1)} %fusion.56), channel_id=1, source_target_pairs={{0,24},{8,0},{16,8},{24,16},{1,25},{9,1},{17,9},{25,17},{2,26},{10... | collective-permute-start | bytes 393224 | tf_op jit(solution)/shard_map/ppermute | solution.py:370
  30.7 4.7 %collective-permute-done.10 = f32[128,256]{1,0:T(8,128)S(1)} collective-permute-done((f32[128,256]{1,0:T(8,128)S(1)}, f32[128,256]{1,0:T(8,128)S(1)}, u32[]{:S(2)}, u32[]{:S(2)}) %collective-permute-start.10) | collective-permute-done | bytes 131104 | tf_op jit(solution)/shard_map/ppermute | solution.py:370
  38.1 1.4 %collective-permute-done.12.other_ref = f32[256,256]{1,0:T(8,128)S(1)} collective-permute-done((f32[256,256]{1,0:T(8,128)S(1)}, f32[256,256]{1,0:T(8,128)S(1)}, u32[]{:S(2)}, u32[]{:S(2)}) %collective-permute-start.12) | collective-permute-done | bytes 262176 | tf_op jit(solution)/shard_map/ppermute | solution.py:375
  39.6 1.6 %payload.1 = (f32[512,256]{1,0:T(8,128)S(1)}, f32[192,128]{1,0:T(8,128)S(1)}, f32[192,128]{1,0:T(8,128)S(1)}, f32[192,128]{1,0:T(8,128)S(1)}, f32[192,128]{1,0:T(8,128)S(1)}) custom-call(s32[2]{0:T(128)S(1)} %pad_add_fusion.place_ref, f32[256,256]{1,0:T(8,128)S(1)} %copy-done.1, f32[256,256]{1,0:T(8,128)S(1)} %maximum_add_fusion.own_ref, ...), custom_call_target="tpu_custom_call" | custom-call | flops 1000000000 | bytes 1048576 | tf_op jit(solution)/shard_map/payload/pallas_call | solution.py:356
  43.3 1.4 %collective-permute-start.15 = (f32[192,128]{1,0:T(8,128)S(1)}, f32[192,128]{1,0:T(8,128)S(1)}, u32[]{:S(2)}, u32[]{:S(2)}) collective-permute-start(f32[192,128]{1,0:T(8,128)S(1)} %get-tuple-element.66), channel_id=1, source_target_pairs={{0,6},{2,4},{4,2},{6,0},{1,7},{3,5},{5,3},{7,1},{8,14},{10,12},{12... | collective-permute-start | bytes 294920 | tf_op jit(solution)/shard_map/ppermute | solution.py:375
  47.3 2.7 %collective-permute-done.15 = f32[192,128]{1,0:T(8,128)S(1)} collective-permute-done((f32[192,128]{1,0:T(8,128)S(1)}, f32[192,128]{1,0:T(8,128)S(1)}, u32[]{:S(2)}, u32[]{:S(2)}) %collective-permute-start.15) | collective-permute-done | bytes 98336 | tf_op jit(solution)/shard_map/ppermute | solution.py:375
  50.6 2.2 %collective-permute-start.17 = (f32[192,128]{1,0:T(8,128)S(1)}, f32[192,128]{1,0:T(8,128)S(1)}, u32[]{:S(2)}, u32[]{:S(2)}) collective-permute-start(f32[192,128]{1,0:T(8,128)S(1)} %add_add_fusion.2), channel_id=1, source_target_pairs={{0,16},{8,24},{16,0},{24,8},{1,17},{9,25},{17,1},{25,9},{2,18},{10... | collective-permute-start | bytes 294920 | tf_op jit(solution)/shard_map/ppermute | solution.py:375
  52.8 1.6 %collective-permute-start.18 = (f32[192,128]{1,0:T(8,128)S(1)}, f32[192,128]{1,0:T(8,128)S(1)}, u32[]{:S(2)}, u32[]{:S(2)}) collective-permute-start(f32[192,128]{1,0:T(8,128)S(1)} %add_add_fusion.2), channel_id=1, source_target_pairs={{0,24},{8,16},{16,8},{24,0},{1,25},{9,17},{17,9},{25,1},{2,26},{10... | collective-permute-start | bytes 294920 | tf_op jit(solution)/shard_map/ppermute | solution.py:375
  55.4 2.1 %collective-permute-start.24 = (f32[256,256]{1,0:T(8,128)S(1)}, f32[256,256]{1,0:T(8,128)S(1)}, u32[]{:S(2)}, u32[]{:S(2)}) collective-permute-start(f32[256,256]{1,0:T(8,128)S(1)} %maximum_add_fusion.own_ref), channel_id=1, source_target_pairs={{0,6},{2,4},{4,2},{6,0},{1,7},{3,5},{5,3},{7,1},{8,14},{10,12},{12... | collective-permute-start | bytes 786440 | tf_op jit(solution)/shard_map/ppermute | solution.py:375
  57.5 2.3 %collective-permute-done.17 = f32[192,128]{1,0:T(8,128)S(1)} collective-permute-done((f32[192,128]{1,0:T(8,128)S(1)}, f32[192,128]{1,0:T(8,128)S(1)}, u32[]{:S(2)}, u32[]{:S(2)}) %collective-permute-start.17) | collective-permute-done | bytes 98336 | tf_op jit(solution)/shard_map/ppermute | solution.py:375
  61.5 1.8 %collective-permute-start.21 = (f32[192,128]{1,0:T(8,128)S(1)}, f32[192,128]{1,0:T(8,128)S(1)}, u32[]{:S(2)}, u32[]{:S(2)}) collective-permute-start(f32[192,128]{1,0:T(8,128)S(1)} %add_add_fusion.1.refs_0_), channel_id=1, source_target_pairs={{0,6},{2,4},{4,2},{6,0},{1,7},{3,5},{5,3},{7,1},{8,14},{10,12},{12... | collective-permute-start | bytes 294920 | tf_op jit(solution)/shard_map/ppermute | solution.py:375
  63.4 5.9 %collective-permute-done.23 = f32[256,256]{1,0:T(8,128)S(1)} collective-permute-done((f32[256,256]{1,0:T(8,128)S(1)}, f32[256,256]{1,0:T(8,128)S(1)}, u32[]{:S(2)}, u32[]{:S(2)}) %collective-permute-start.23) | collective-permute-done | bytes 262176 | tf_op jit(solution)/shard_map/ppermute | solution.py:375
  73.9 3.5 %collective-permute-start.26 = (f32[256,256]{1,0:T(8,128)S(1)}, f32[256,256]{1,0:T(8,128)S(1)}, u32[]{:S(2)}, u32[]{:S(2)}) collective-permute-start(f32[256,256]{1,0:T(8,128)S(1)} %fusion.58), channel_id=1, source_target_pairs={{0,24},{8,0},{16,8},{24,16},{1,25},{9,1},{17,9},{25,17},{2,26},{10... | collective-permute-start | bytes 786440 | tf_op jit(solution)/shard_map/ppermute | solution.py:370
  77.4 29.8 %inverse_and_solve.1 = (f32[512,512]{1,0:T(8,128)S(1)}, f32[512,512]{1,0:T(8,128)S(1)}, f32[32,512]{1,0:T(8,128)S(1)}) custom-call(s32[2]{0:T(128)S(1)} %pad_add_fusion.place_ref, f32[192,128]{1,0:T(8,128)S(1)} %add_add_fusion.1.refs_0_, f32[192,128]{1,0:T(8,128)S(1)} %collective-permute-done.19.refs_1_, f32[192,128]{1,0:T(8,128)S(1)} %collective-permute-done.20.refs_2_, ...), custom_call_target="tpu_custom_call" | custom-call | flops 30000001024 | bytes 1048576 | tf_op jit(solution)/shard_map/inverse_and_solve/pallas_call | solution.py:356
  107.4 1.5 %collective-permute-done.31.other_ref = f32[256,256]{1,0:T(8,128)S(1)} collective-permute-done((f32[256,256]{1,0:T(8,128)S(1)}, f32[256,256]{1,0:T(8,128)S(1)}, u32[]{:S(2)}, u32[]{:S(2)}) %collective-permute-start.31) | collective-permute-done | bytes 262176 | tf_op jit(solution)/shard_map/ppermute | solution.py:375
  108.9 1.3 image.1
  111.2 2.5 %collective-permute-start.34 = (f32[200,128]{1,0:T(8,128)S(1)}, f32[200,128]{1,0:T(8,128)S(1)}, u32[]{:S(2)}, u32[]{:S(2)}) collective-permute-start(f32[200,128]{1,0:T(8,128)S(1)} %get-tuple-element.80), channel_id=1, source_target_pairs={{0,6},{2,4},{4,2},{6,0},{1,7},{3,5},{5,3},{7,1},{8,14},{10,12},{12... | collective-permute-start | bytes 307208 | tf_op jit(solution)/shard_map/ppermute | solution.py:375
  113.8 1.9 %fusion.60 = f32[512,512]{1,0:T(8,128)S(1)} fusion(f32[512,512]{1,0:T(8,128)S(1)} %get-tuple-element.83, f32[512,512]{1,0:T(8,128)S(1)} %get-tuple-element.84), kind=kOutput, calls=%fused_computation.136 | convolution fusion | flops 1610612736 | bytes 3145728 | tf_op jit(solution)/shard_map/dot_general | solution.py:20
  115.6 1.9 %convolution_subtract_fusion = bf16[512,512]{1,0:T(8,128)(2,1)S(1)} fusion(f32[512,512]{1,0:T(8,128)S(1)} %get-tuple-element.84, f32[512,512]{1,0:T(8,128)S(1)} %get-tuple-element.85, f32[512,512]{1,0:T(8,128)S(1)} %fusion.60), kind=kOutput, calls=%fused_computation.10 | convolution fusion | flops 1611137024 | bytes 3670016 | tf_op jit(solution)/shard_map/dot_general | solution.py:20
  119.0 1.2 collective-permute-start.35
  120.2 3.2 %collective-permute-start.37 = (f32[200,128]{1,0:T(8,128)S(1)}, f32[200,128]{1,0:T(8,128)S(1)}, u32[]{:S(2)}, u32[]{:S(2)}) collective-permute-start(f32[200,128]{1,0:T(8,128)S(1)} %get-tuple-element.101), channel_id=1, source_target_pairs={{0,24},{8,16},{16,8},{24,0},{1,25},{9,17},{17,9},{25,1},{2,26},{10... | collective-permute-start | bytes 307208 | tf_op jit(solution)/shard_map/ppermute | solution.py:375
  124.2 1.6 %collective-permute-done.35 = f32[200,128]{1,0:T(8,128)S(1)} collective-permute-done((f32[200,128]{1,0:T(8,128)S(1)}, f32[200,128]{1,0:T(8,128)S(1)}, u32[]{:S(2)}, u32[]{:S(2)}) %collective-permute-start.35) | collective-permute-done | bytes 102432 | tf_op jit(solution)/shard_map/ppermute | solution.py:375
  125.7 1.7 %collective-permute-done.37 = f32[200,128]{1,0:T(8,128)S(1)} collective-permute-done((f32[200,128]{1,0:T(8,128)S(1)}, f32[200,128]{1,0:T(8,128)S(1)}, u32[]{:S(2)}, u32[]{:S(2)}) %collective-permute-start.37) | collective-permute-done | bytes 102432 | tf_op jit(solution)/shard_map/ppermute | solution.py:375
  128.9 12.3 %all_to_all.6 = f32[16,8,128]{2,1,0:T(8,128)S(1)} all-to-all(f32[16,8,128]{2,1,0:T(8,128)S(1)} %broadcast_in_dim.5), channel_id=1, replica_groups=mesh['blk'=4,'leaf'=4,'samp'=2] {'blk','leaf'}, dimensions={0} | all-to-all | bytes 131072 | tf_op jit(solution)/shard_map/all_to_all | solution.py:387
  (137 shorter events, 32.4 us)
Async XLA Ops:
  2.5 8.1 %collective-permute-start.3 = (f32[8,256]{1,0:T(8,128)}, f32[8,256]{1,0:T(8,128)S(1)}, u32[]{:S(2)}, u32[]{:S(2)}) collective-permute-start(f32[8,256]{1,0:T(8,128)} %get-tuple-element.46.refs_1_), channel_id=1, source_target_pairs={{0,8},{1,25},{8,16},{9,1},{16,24},{17,9},{24,0},{25,17},{2,10},{3,... | collective-permute-start | bytes 24584 | tf_op jit(solution)/shard_map/ppermute | solution.py:442
  5.6 10.1 %collective-permute-start = (f32[168,256]{1,0:T(8,128)}, f32[168,256]{1,0:T(8,128)S(1)}, u32[]{:S(2)}, u32[]{:S(2)}) collective-permute-start(f32[168,256]{1,0:T(8,128)} %get-tuple-element.45), channel_id=1, source_target_pairs={{0,2},{2,0},{4,6},{6,4},{1,3},{3,1},{5,7},{7,5},{8,10},{10,8},{12,... | collective-permute-start | bytes 516104 | tf_op jit(solution)/shard_map/ppermute | solution.py:375
  7.1 10.4 %collective-permute-start.1 = (f32[168,256]{1,0:T(8,128)}, f32[168,256]{1,0:T(8,128)S(1)}, u32[]{:S(2)}, u32[]{:S(2)}) collective-permute-start(f32[168,256]{1,0:T(8,128)} %get-tuple-element.45), channel_id=1, source_target_pairs={{0,4},{2,6},{4,0},{6,2},{1,5},{3,7},{5,1},{7,3},{8,12},{10,14},{12... | collective-permute-start | bytes 516104 | tf_op jit(solution)/shard_map/ppermute | solution.py:375
  8.6 8.9 %collective-permute-start.2 = (f32[168,256]{1,0:T(8,128)}, f32[168,256]{1,0:T(8,128)S(1)}, u32[]{:S(2)}, u32[]{:S(2)}) collective-permute-start(f32[168,256]{1,0:T(8,128)} %get-tuple-element.45), channel_id=1, source_target_pairs={{0,6},{2,4},{4,2},{6,0},{1,7},{3,5},{5,3},{7,1},{8,14},{10,12},{12... | collective-permute-start | bytes 516104 | tf_op jit(solution)/shard_map/ppermute | solution.py:375
  9.1 15.2 %collective-permute-start.7 = (f32[128,256]{1,0:T(8,128)}, f32[128,256]{1,0:T(8,128)S(1)}, u32[]{:S(2)}, u32[]{:S(2)}) collective-permute-start(f32[128,256]{1,0:T(8,128)} %get-tuple-element.54), channel_id=1, source_target_pairs={{0,2},{2,0},{4,6},{6,4},{1,3},{3,1},{5,7},{7,5},{8,10},{10,8},{12,... | collective-permute-start | bytes 393224 | tf_op jit(solution)/shard_map/ppermute | solution.py:375
  12.7 11.5 %collective-permute-start.8 = (f32[128,256]{1,0:T(8,128)}, f32[128,256]{1,0:T(8,128)S(1)}, u32[]{:S(2)}, u32[]{:S(2)}) collective-permute-start(f32[128,256]{1,0:T(8,128)} %get-tuple-element.54), channel_id=1, source_target_pairs={{0,4},{2,6},{4,0},{6,2},{1,5},{3,7},{5,1},{7,3},{8,12},{10,14},{12... | collective-permute-start | bytes 393224 | tf_op jit(solution)/shard_map/ppermute | solution.py:375
  15.7 8.6 %collective-permute-start.9 = (f32[128,256]{1,0:T(8,128)}, f32[128,256]{1,0:T(8,128)S(1)}, u32[]{:S(2)}, u32[]{:S(2)}) collective-permute-start(f32[128,256]{1,0:T(8,128)} %get-tuple-element.54), channel_id=1, source_target_pairs={{0,6},{2,4},{4,2},{6,0},{1,7},{3,5},{5,3},{7,1},{8,14},{10,12},{12... | collective-permute-start | bytes 393224 | tf_op jit(solution)/shard_map/ppermute | solution.py:375
  19.9 17.2 %collective-permute-start.6 = (f32[160,256]{1,0:T(8,128)S(1)}, f32[160,256]{1,0:T(8,128)S(1)}, u32[]{:S(2)}, u32[]{:S(2)}) collective-permute-start(f32[160,256]{1,0:T(8,128)S(1)} %fusion.25), channel_id=1, source_target_pairs={{0,24},{8,0},{16,8},{24,16},{1,25},{9,1},{17,9},{25,17},{2,26},{10... | collective-permute-start | bytes 491528 | tf_op jit(solution)/shard_map/ppermute | solution.py:370
  24.2 12.9 %collective-permute-start.5 = (f32[160,256]{1,0:T(8,128)S(1)}, f32[160,256]{1,0:T(8,128)S(1)}, u32[]{:S(2)}, u32[]{:S(2)}) collective-permute-start(f32[160,256]{1,0:T(8,128)S(1)} %fusion.26), channel_id=1, source_target_pairs={{0,8},{8,16},{16,24},{24,0},{1,9},{9,17},{17,25},{25,1},{2,10},{10... | collective-permute-start | bytes 491528 | tf_op jit(solution)/shard_map/ppermute | solution.py:370
  25.7 9.7 %collective-permute-start.10 = (f32[128,256]{1,0:T(8,128)S(1)}, f32[128,256]{1,0:T(8,128)S(1)}, u32[]{:S(2)}, u32[]{:S(2)}) collective-permute-start(f32[128,256]{1,0:T(8,128)S(1)} %fusion.55), channel_id=1, source_target_pairs={{0,8},{8,16},{16,24},{24,0},{1,9},{9,17},{17,25},{25,1},{2,10},{10... | collective-permute-start | bytes 393224 | tf_op jit(solution)/shard_map/ppermute | solution.py:370
  26.5 10.0 %collective-permute-start.11 = (f32[128,256]{1,0:T(8,128)S(1)}, f32[128,256]{1,0:T(8,128)S(1)}, u32[]{:S(2)}, u32[]{:S(2)}) collective-permute-start(f32[128,256]{1,0:T(8,128)S(1)} %fusion.56), channel_id=1, source_target_pairs={{0,24},{8,0},{16,8},{24,16},{1,25},{9,1},{17,9},{25,17},{2,26},{10... | collective-permute-start | bytes 393224 | tf_op jit(solution)/shard_map/ppermute | solution.py:370
  41.2 5.2 %collective-permute-start.13 = (f32[192,128]{1,0:T(8,128)S(1)}, f32[192,128]{1,0:T(8,128)S(1)}, u32[]{:S(2)}, u32[]{:S(2)}) collective-permute-start(f32[192,128]{1,0:T(8,128)S(1)} %get-tuple-element.64), channel_id=1, source_target_pairs={{0,2},{2,0},{4,6},{6,4},{1,3},{3,1},{5,7},{7,5},{8,10},{10,8},{12,... | collective-permute-start | bytes 294920 | tf_op jit(solution)/shard_map/ppermute | solution.py:375
  42.2 5.1 %collective-permute-start.14 = (f32[192,128]{1,0:T(8,128)S(1)}, f32[192,128]{1,0:T(8,128)S(1)}, u32[]{:S(2)}, u32[]{:S(2)}) collective-permute-start(f32[192,128]{1,0:T(8,128)S(1)} %get-tuple-element.65), channel_id=1, source_target_pairs={{0,4},{2,6},{4,0},{6,2},{1,5},{3,7},{5,1},{7,3},{8,12},{10,14},{12... | collective-permute-start | bytes 294920 | tf_op jit(solution)/shard_map/ppermute | solution.py:375
  43.3 6.6 %collective-permute-start.15 = (f32[192,128]{1,0:T(8,128)S(1)}, f32[192,128]{1,0:T(8,128)S(1)}, u32[]{:S(2)}, u32[]{:S(2)}) collective-permute-start(f32[192,128]{1,0:T(8,128)S(1)} %get-tuple-element.66), channel_id=1, source_target_pairs={{0,6},{2,4},{4,2},{6,0},{1,7},{3,5},{5,3},{7,1},{8,14},{10,12},{12... | collective-permute-start | bytes 294920 | tf_op jit(solution)/shard_map/ppermute | solution.py:375
  44.8 16.7 %collective-permute-start.22 = (f32[256,256]{1,0:T(8,128)S(1)}, f32[256,256]{1,0:T(8,128)S(1)}, u32[]{:S(2)}, u32[]{:S(2)}) collective-permute-start(f32[256,256]{1,0:T(8,128)S(1)} %maximum_add_fusion.own_ref), channel_id=1, source_target_pairs={{0,2},{2,0},{4,6},{6,4},{1,3},{3,1},{5,7},{7,5},{8,10},{10,8},{12,... | collective-permute-start | bytes 786440 | tf_op jit(solution)/shard_map/ppermute | solution.py:375
  50.0 5.4 %collective-permute-start.16 = (f32[192,128]{1,0:T(8,128)S(1)}, f32[192,128]{1,0:T(8,128)S(1)}, u32[]{:S(2)}, u32[]{:S(2)}) collective-permute-start(f32[192,128]{1,0:T(8,128)S(1)} %add_add_fusion.2), channel_id=1, source_target_pairs={{0,8},{8,0},{16,24},{24,16},{1,9},{9,1},{17,25},{25,17},{2,10},{10... | collective-permute-start | bytes 294920 | tf_op jit(solution)/shard_map/ppermute | solution.py:375
  50.6 9.1 %collective-permute-start.17 = (f32[192,128]{1,0:T(8,128)S(1)}, f32[192,128]{1,0:T(8,128)S(1)}, u32[]{:S(2)}, u32[]{:S(2)}) collective-permute-start(f32[192,128]{1,0:T(8,128)S(1)} %add_add_fusion.2), channel_id=1, source_target_pairs={{0,16},{8,24},{16,0},{24,8},{1,17},{9,25},{17,1},{25,9},{2,18},{10... | collective-permute-start | bytes 294920 | tf_op jit(solution)/shard_map/ppermute | solution.py:375
  52.8 6.9 %collective-permute-start.18 = (f32[192,128]{1,0:T(8,128)S(1)}, f32[192,128]{1,0:T(8,128)S(1)}, u32[]{:S(2)}, u32[]{:S(2)}) collective-permute-start(f32[192,128]{1,0:T(8,128)S(1)} %add_add_fusion.2), channel_id=1, source_target_pairs={{0,24},{8,16},{16,8},{24,0},{1,25},{9,17},{17,9},{25,1},{2,26},{10... | collective-permute-start | bytes 294920 | tf_op jit(solution)/shard_map/ppermute | solution.py:375
  54.5 14.8 %collective-permute-start.23 = (f32[256,256]{1,0:T(8,128)S(1)}, f32[256,256]{1,0:T(8,128)S(1)}, u32[]{:S(2)}, u32[]{:S(2)}) collective-permute-start(f32[256,256]{1,0:T(8,128)S(1)} %maximum_add_fusion.own_ref), channel_id=1, source_target_pairs={{0,4},{2,6},{4,0},{6,2},{1,5},{3,7},{5,1},{7,3},{8,12},{10,14},{12... | collective-permute-start | bytes 786440 | tf_op jit(solution)/shard_map/ppermute | solution.py:375
  55.4 13.8 %collective-permute-start.24 = (f32[256,256]{1,0:T(8,128)S(1)}, f32[256,256]{1,0:T(8,128)S(1)}, u32[]{:S(2)}, u32[]{:S(2)}) collective-permute-start(f32[256,256]{1,0:T(8,128)S(1)} %maximum_add_fusion.own_ref), channel_id=1, source_target_pairs={{0,6},{2,4},{4,2},{6,0},{1,7},{3,5},{5,3},{7,1},{8,14},{10,12},{12... | collective-permute-start | bytes 786440 | tf_op jit(solution)/shard_map/ppermute | solution.py:375
  59.8 12.7 %collective-permute-start.19 = (f32[192,128]{1,0:T(8,128)S(1)}, f32[192,128]{1,0:T(8,128)S(1)}, u32[]{:S(2)}, u32[]{:S(2)}) collective-permute-start(f32[192,128]{1,0:T(8,128)S(1)} %add_add_fusion.1.refs_0_), channel_id=1, source_target_pairs={{0,2},{2,0},{4,6},{6,4},{1,3},{3,1},{5,7},{7,5},{8,10},{10,8},{12,... | collective-permute-start | bytes 294920 | tf_op jit(solution)/shard_map/ppermute | solution.py:375
  60.8 11.7 %collective-permute-start.20 = (f32[192,128]{1,0:T(8,128)S(1)}, f32[192,128]{1,0:T(8,128)S(1)}, u32[]{:S(2)}, u32[]{:S(2)}) collective-permute-start(f32[192,128]{1,0:T(8,128)S(1)} %add_add_fusion.1.refs_0_), channel_id=1, source_target_pairs={{0,4},{2,6},{4,0},{6,2},{1,5},{3,7},{5,1},{7,3},{8,12},{10,14},{12... | collective-permute-start | bytes 294920 | tf_op jit(solution)/shard_map/ppermute | solution.py:375
  61.5 11.0 %collective-permute-start.21 = (f32[192,128]{1,0:T(8,128)S(1)}, f32[192,128]{1,0:T(8,128)S(1)}, u32[]{:S(2)}, u32[]{:S(2)}) collective-permute-start(f32[192,128]{1,0:T(8,128)S(1)} %add_add_fusion.1.refs_0_), channel_id=1, source_target_pairs={{0,6},{2,4},{4,2},{6,0},{1,7},{3,5},{5,3},{7,1},{8,14},{10,12},{12... | collective-permute-start | bytes 294920 | tf_op jit(solution)/shard_map/ppermute | solution.py:375
  72.6 4.8 %collective-permute-start.28 = (f32[192,128]{1,0:T(8,128)S(1)}, f32[192,128]{1,0:T(8,128)S(1)}, u32[]{:S(2)}, u32[]{:S(2)}) collective-permute-start(f32[192,128]{1,0:T(8,128)S(1)} %collective-permute-done.19.refs_1_), channel_id=1, source_target_pairs={{0,1},{1,0},{2,3},{3,2},{4,5},{5,4},{6,7},{7,6},{8,9},{9,8},{10,11... | collective-permute-start | bytes 294920 | tf_op jit(solution)/shard_map/ppermute | solution.py:375
  73.6 33.6 %collective-permute-start.25 = (f32[256,256]{1,0:T(8,128)S(1)}, f32[256,256]{1,0:T(8,128)S(1)}, u32[]{:S(2)}, u32[]{:S(2)}) collective-permute-start(f32[256,256]{1,0:T(8,128)S(1)} %fusion.57), channel_id=1, source_target_pairs={{0,8},{8,16},{16,24},{24,0},{1,9},{9,17},{17,25},{25,1},{2,10},{10... | collective-permute-start | bytes 786440 | tf_op jit(solution)/shard_map/ppermute | solution.py:370
  73.9 33.4 %collective-permute-start.26 = (f32[256,256]{1,0:T(8,128)S(1)}, f32[256,256]{1,0:T(8,128)S(1)}, u32[]{:S(2)}, u32[]{:S(2)}) collective-permute-start(f32[256,256]{1,0:T(8,128)S(1)} %fusion.58), channel_id=1, source_target_pairs={{0,24},{8,0},{16,8},{24,16},{1,25},{9,1},{17,9},{25,17},{2,26},{10... | collective-permute-start | bytes 786440 | tf_op jit(solution)/shard_map/ppermute | solution.py:370
  110.2 7.3 %collective-permute-start.32 = (f32[200,128]{1,0:T(8,128)S(1)}, f32[200,128]{1,0:T(8,128)S(1)}, u32[]{:S(2)}, u32[]{:S(2)}) collective-permute-start(f32[200,128]{1,0:T(8,128)S(1)} %get-tuple-element.80), channel_id=1, source_target_pairs={{0,2},{2,0},{4,6},{6,4},{1,3},{3,1},{5,7},{7,5},{8,10},{10,8},{12,... | collective-permute-start | bytes 307208 | tf_op jit(solution)/shard_map/ppermute | solution.py:375
  110.5 7.0 %collective-permute-start.33 = (f32[200,128]{1,0:T(8,128)S(1)}, f32[200,128]{1,0:T(8,128)S(1)}, u32[]{:S(2)}, u32[]{:S(2)}) collective-permute-start(f32[200,128]{1,0:T(8,128)S(1)} %get-tuple-element.80), channel_id=1, source_target_pairs={{0,4},{2,6},{4,0},{6,2},{1,5},{3,7},{5,1},{7,3},{8,12},{10,14},{12... | collective-permute-start | bytes 307208 | tf_op jit(solution)/shard_map/ppermute | solution.py:375
  111.2 6.4 %collective-permute-start.34 = (f32[200,128]{1,0:T(8,128)S(1)}, f32[200,128]{1,0:T(8,128)S(1)}, u32[]{:S(2)}, u32[]{:S(2)}) collective-permute-start(f32[200,128]{1,0:T(8,128)S(1)} %get-tuple-element.80), channel_id=1, source_target_pairs={{0,6},{2,4},{4,2},{6,0},{1,7},{3,5},{5,3},{7,1},{8,14},{10,12},{12... | collective-permute-start | bytes 307208 | tf_op jit(solution)/shard_map/ppermute | solution.py:375
  118.3 5.9 %collective-permute-start.36 = (f32[136,128]{1,0:T(8,128)S(1)}, f32[136,128]{1,0:T(8,128)S(1)}, u32[]{:S(2)}, u32[]{:S(2)}) collective-permute-start(f32[136,128]{1,0:T(8,128)S(1)} %fusion.30), channel_id=1, source_target_pairs={{0,16},{8,24},{16,0},{24,8},{1,17},{9,25},{17,1},{25,9},{2,18},{10... | collective-permute-start | bytes 208904 | tf_op jit(solution)/shard_map/ppermute | solution.py:375
  119.0 6.7 %collective-permute-start.35 = (f32[200,128]{1,0:T(8,128)S(1)}, f32[200,128]{1,0:T(8,128)S(1)}, u32[]{:S(2)}, u32[]{:S(2)}) collective-permute-start(f32[200,128]{1,0:T(8,128)S(1)} %get-tuple-element.100), channel_id=1, source_target_pairs={{0,8},{8,0},{16,24},{24,16},{1,9},{9,1},{17,25},{25,17},{2,10},{10... | collective-permute-start | bytes 307208 | tf_op jit(solution)/shard_map/ppermute | solution.py:375
  120.2 7.2 %collective-permute-start.37 = (f32[200,128]{1,0:T(8,128)S(1)}, f32[200,128]{1,0:T(8,128)S(1)}, u32[]{:S(2)}, u32[]{:S(2)}) collective-permute-start(f32[200,128]{1,0:T(8,128)S(1)} %get-tuple-element.101), channel_id=1, source_target_pairs={{0,24},{8,16},{16,8},{24,0},{1,25},{9,17},{17,9},{25,1},{2,26},{10... | collective-permute-start | bytes 307208 | tf_op jit(solution)/shard_map/ppermute | solution.py:375
  (16 other events, 190.2 us)
